TPU v7x, 32 devices: a whole 2x2x4 slice. The times are simulated.
32 devices in a mesh: fsdp: 4 (over x, core), context: 2 (over y), tensor: 4 (over z).
Axes of the slice: x: 2, y: 2, z: 4, core: 2. Of those that a mesh axis runs over, the one named last changes fastest.
Arguments:
- block_in: bfloat16 [2048, 2048], P(('fsdp', 'context')), may hold values from -6 to 6
- seq_lengths: int32 [4, 6], P('fsdp'), may hold values from 0 to 512, as said below
- attn_gain: float32 [2048], replicated, may hold values from 0.25 to 1.75
- attn_bias: float32 [2048], replicated, may hold values from -1.75 to 1.75
- qkv_weight: bfloat16 [3, 2048, 2048], P(None, ('fsdp', 'context'), 'tensor'), may hold values from -0.125 to 0.125
- qkv_bias: float32 [3, 2048], P(None, 'tensor'), may hold values from -3 to 3
- out_weight: bfloat16 [2048, 2048], P('tensor', ('fsdp', 'context')), may hold values from -0.5 to 0.5
- ffn_gain: float32 [2048], replicated, may hold values from 0.25 to 1.75
- ffn_bias: float32 [2048], replicated, may hold values from -1.75 to 1.75
- gate_up_weight: bfloat16 [2, 2048, 5632], P(None, ('fsdp', 'context'), 'tensor'), may hold values from -0.125 to 0.125
- down_weight: bfloat16 [5632, 2048], P('tensor', ('fsdp', 'context')), may hold values from -0.15625 to 0.15625
- out_cotangent: bfloat16 [2048, 2048], P(('fsdp', 'context')), may hold values from -6 to 6
Outputs:
- block_out: bfloat16 [2048, 2048], P(('fsdp', 'context'))
- input_grad: bfloat16 [2048, 2048], P(('fsdp', 'context'))
- attn_gain_grad: float32 [2048], replicated
- attn_bias_grad: float32 [2048], replicated
- qkv_weight_grad: float32 [3, 2048, 2048], P(None, ('fsdp', 'context'), 'tensor')
- qkv_bias_grad: float32 [3, 2048], P(None, 'tensor')
- out_weight_grad: float32 [2048, 2048], P('tensor', ('fsdp', 'context'))
- ffn_gain_grad: float32 [2048], replicated
- ffn_bias_grad: float32 [2048], replicated
- gate_up_grad: float32 [2, 2048, 5632], P(None, ('fsdp', 'context'), 'tensor')
- down_grad: float32 [5632, 2048], P('tensor', ('fsdp', 'context'))
Inputs may be any that keep to these rules, and one draw needn't show every extreme that they name: `seq_lengths`: each row sums to 512; in each row one sequence starts before place 256 and ends after it.
All inputs are finite; a program needn't handle non-finite values.
Results may differ from a plain program's by a relative error of at most 0.015.
Values may be sent and summed in bfloat16 or wider, within the bound.
No kernel may reach another device: no remote copies, remote signals or barrier semaphores. Data moves between devices by JAX's collectives and lax.ppermute only.
A program may use at most 256 MiB of HBM per device.

v0:
```python
import math

import jax
import jax.numpy as jnp
from jax import lax
from jax.sharding import PartitionSpec as P

HD = 64
ROT = 16


EPS = 1e-05
NEG = -1e30


def shifted(array, axis, by):
    peers = lax.axis_size(axis)
    pairs = [(i, i + by) for i in range(peers) if 0 <= i + by < peers]
    return lax.ppermute(array, axis, pairs)


def norm_parts(values):
    center = values - jnp.mean(values, axis=-1, keepdims=True)
    inv_std = lax.rsqrt(jnp.mean(center * center, axis=-1, keepdims=True) + EPS)
    return (center * inv_std, inv_std)


def norm_back(normal, inv_std, grad_out, gain_vec):
    scaled = grad_out * gain_vec
    grad_in = inv_std * (
        scaled
        - jnp.mean(scaled, axis=-1, keepdims=True)
        - normal * jnp.mean(scaled * normal, axis=-1, keepdims=True)
    )
    return (grad_in, jnp.sum(grad_out * normal, axis=0), jnp.sum(grad_out, axis=0))


def rotation_tables(places):
    half_rot = ROT // 2
    frequency = jnp.exp(jnp.arange(half_rot).astype(jnp.float32) * (-2.0 * math.log(10000.0) / ROT))
    angles = places.astype(jnp.float32)[:, None] * frequency[None, :]
    return (jnp.cos(angles), jnp.sin(angles))


def rotate(values, cosine_table, sine_table):
    half_rot = ROT // 2
    cos_part = cosine_table[:, None, :]
    sin_part = sine_table[:, None, :]
    first_half = values[..., :half_rot]
    second_half = values[..., half_rot:ROT]
    return jnp.concatenate(
        [
            first_half * cos_part - second_half * sin_part,
            second_half * cos_part + first_half * sin_part,
            values[..., ROT:],
        ],
        axis=-1,
    )


def branch_total(partial_value):
    return lax.psum(partial_value, "tensor")


def grad_total(partial_value):
    return lax.psum(partial_value, "tensor")


def on_device(
    block_in,
    seq_lengths,
    attn_gain,
    attn_bias,
    qkv_weight,
    qkv_bias,
    out_weight,
    ffn_gain,
    ffn_bias,
    gate_up_weight,
    down_weight,
    out_cotangent,
):
    tok_rows = block_in.shape[0]
    heads_here = qkv_weight.shape[2] // HD
    feat_here = heads_here * HD
    score_scale = HD ** (-0.5)
    f32 = jnp.float32
    bf16 = jnp.bfloat16
    full_qkv, full_out, full_gate_up, full_down = (
        lax.all_gather(qkv_weight, ("fsdp", "context"), axis=1, tiled=True),
        lax.all_gather(out_weight, ("fsdp", "context"), axis=1, tiled=True),
        lax.all_gather(gate_up_weight, ("fsdp", "context"), axis=1, tiled=True),
        lax.all_gather(down_weight, ("fsdp", "context"), axis=1, tiled=True),
    )
    offset = lax.axis_index("context") * tok_rows
    places = offset + jnp.arange(tok_rows, dtype=jnp.int32)
    lengths_row = seq_lengths[0]
    seq_ends = jnp.cumsum(lengths_row)
    starts = jnp.sum(
        jnp.where(seq_ends[None, :] <= places[:, None], lengths_row[None, :], 0), axis=1
    )
    cosine_table, sine_table = rotation_tables(places - starts)
    key_places = offset - tok_rows + jnp.arange(2 * tok_rows, dtype=jnp.int32)
    input_f = block_in.astype(f32)
    normal_one, inv_one = norm_parts(input_f)
    normed_one = (normal_one * attn_gain + attn_bias).astype(bf16)
    projected = (
        jnp.einsum("td,kde->kte", normed_one, full_qkv, preferred_element_type=f32)
        + qkv_bias[:, None, :]
    )
    queries = rotate(
        projected[0].reshape(tok_rows, heads_here, HD), cosine_table, sine_table
    ).astype(bf16)
    keys_here = rotate(
        projected[1].reshape(tok_rows, heads_here, HD), cosine_table, sine_table
    ).astype(bf16)
    values_here = projected[2].astype(bf16)
    local_pair = jnp.stack([keys_here.reshape(tok_rows, feat_here), values_here])
    earlier_pair = shifted(local_pair, "context", 1)
    both_pairs = jnp.concatenate([earlier_pair, local_pair], axis=1).reshape(
        2, 2 * tok_rows, heads_here, HD
    )
    keys_all = both_pairs[0]
    values_all = both_pairs[1]
    block_rows = min(512, tok_rows)
    block_count = tok_rows // block_rows

    def masked_scores(query_blk):
        raw_scores = (
            jnp.einsum("qhd,khd->hqk", query_blk, keys_all, preferred_element_type=f32)
            * score_scale
        )
        visible = (key_places[None, :] <= places[:, None]) & (
            key_places[None, :] >= starts[:, None]
        )
        return jnp.where(visible[None], raw_scores, NEG)

    def attend(block_id):
        scores = masked_scores(queries)
        row_top = jnp.max(scores, axis=-1, keepdims=True)
        exp_scores = jnp.exp(scores - row_top)
        row_total = jnp.sum(exp_scores, axis=-1, keepdims=True)
        weights_blk = (exp_scores / row_total).astype(bf16)
        mixed_blk = jnp.einsum("hqk,khd->qhd", weights_blk, values_all, preferred_element_type=f32)
        return (mixed_blk.astype(bf16), (row_top + jnp.log(row_total))[..., 0])

    mixed_blocks, log_totals = lax.map(attend, jnp.arange(block_count, dtype=jnp.int32))
    attended = mixed_blocks.reshape(tok_rows, feat_here)
    residual_mid = input_f + branch_total(jnp.dot(attended, full_out, preferred_element_type=f32))
    normal_two, inv_two = norm_parts(residual_mid)
    normed_two = (normal_two * ffn_gain + ffn_bias).astype(bf16)
    gate_up = jnp.einsum("td,kdf->ktf", normed_two, full_gate_up, preferred_element_type=f32)
    gate_pre = gate_up[0]
    up_pre = gate_up[1]
    gate_sigmoid = jax.nn.sigmoid(gate_pre)
    silu_gate = gate_pre * gate_sigmoid
    hidden = (silu_gate * up_pre).astype(bf16)
    block_out = residual_mid + branch_total(jnp.dot(hidden, full_down, preferred_element_type=f32))
    back_qkv, back_out, back_gate_up, back_down = (
        lax.all_gather(qkv_weight, ("fsdp", "context"), axis=1, tiled=True),
        lax.all_gather(out_weight, ("fsdp", "context"), axis=1, tiled=True),
        lax.all_gather(gate_up_weight, ("fsdp", "context"), axis=1, tiled=True),
        lax.all_gather(down_weight, ("fsdp", "context"), axis=1, tiled=True),
    )
    cotangent = out_cotangent.astype(f32)
    down_grad = jnp.einsum("tf,td->fd", hidden, out_cotangent, preferred_element_type=f32)
    hidden_grad = jnp.einsum("td,fd->tf", out_cotangent, back_down, preferred_element_type=f32)
    gate_grad = hidden_grad * up_pre * gate_sigmoid * (1.0 + gate_pre * (1.0 - gate_sigmoid))
    up_grad = hidden_grad * silu_gate
    gate_up_back = jnp.stack([gate_grad, up_grad]).astype(bf16)
    gate_up_grad = jnp.einsum("td,ktf->kdf", normed_two, gate_up_back, preferred_element_type=f32)
    ffn_sent = (gate_up_grad, down_grad)
    two_grad = grad_total(
        jnp.einsum("ktf,kdf->td", gate_up_back, back_gate_up, preferred_element_type=f32)
    )
    mid_part, ffn_gain_grad, ffn_bias_grad = norm_back(normal_two, inv_two, two_grad, ffn_gain)
    mid_grad = cotangent + mid_part
    mid_low = mid_grad.astype(bf16)
    out_weight_grad = jnp.einsum("te,td->ed", attended, mid_low, preferred_element_type=f32)
    attended_grad = (
        jnp.einsum("td,ed->te", mid_low, back_out, preferred_element_type=f32)
        .astype(bf16)
        .reshape(tok_rows, heads_here, HD)
    )
    zero_grads = jnp.zeros((2 * tok_rows, heads_here, HD), f32)

    def attend_back(carry, block_id):
        keys_grad, values_grad = carry
        scores = masked_scores(queries)
        probs_blk = jnp.exp(scores - log_totals[block_id][..., None])
        weight_grad = jnp.einsum(
            "qhd,khd->hqk", attended_grad, values_all, preferred_element_type=f32
        )
        row_inner = jnp.sum(probs_blk * weight_grad, axis=-1, keepdims=True)
        score_grad = (probs_blk * (weight_grad - row_inner)).astype(bf16)
        query_grad = (
            jnp.einsum("hqk,khd->qhd", score_grad, keys_all, preferred_element_type=f32)
            * score_scale
        )
        keys_grad = (
            keys_grad
            + jnp.einsum("hqk,qhd->khd", score_grad, queries, preferred_element_type=f32)
            * score_scale
        )
        values_grad = values_grad + jnp.einsum(
            "hqk,qhd->khd", probs_blk.astype(bf16), attended_grad, preferred_element_type=f32
        )
        return ((keys_grad, values_grad), query_grad)

    (keys_grad, values_grad), query_grads = lax.scan(
        attend_back, (zero_grads, zero_grads), jnp.arange(block_count, dtype=jnp.int32)
    )
    sent_back = jnp.stack([keys_grad[:tok_rows], values_grad[:tok_rows]])
    returned = shifted(sent_back, "context", -1)
    keys_total = keys_grad[tok_rows:] + returned[0]
    values_total = values_grad[tok_rows:] + returned[1]
    query_total = query_grads.reshape(tok_rows, heads_here, HD)
    qkv_back = jnp.stack(
        [
            rotate(query_total, cosine_table, -sine_table).reshape(tok_rows, feat_here),
            rotate(keys_total, cosine_table, -sine_table).reshape(tok_rows, feat_here),
            values_total.reshape(tok_rows, feat_here),
        ]
    ).astype(bf16)
    qkv_weight_grad = jnp.einsum("td,kte->kde", normed_one, qkv_back, preferred_element_type=f32)
    qkv_bias_grad = jnp.sum(qkv_back, axis=1, dtype=f32)
    one_grad = grad_total(jnp.einsum("kte,kde->td", qkv_back, back_qkv, preferred_element_type=f32))
    in_part, attn_gain_grad, attn_bias_grad = norm_back(normal_one, inv_one, one_grad, attn_gain)
    input_grad = (mid_grad + in_part).astype(bf16)
    attn_gain_grad, attn_bias_grad, qkv_bias_grad, ffn_gain_grad, ffn_bias_grad = lax.psum(
        (attn_gain_grad, attn_bias_grad, qkv_bias_grad, ffn_gain_grad, ffn_bias_grad),
        ("fsdp", "context"),
    )
    qkv_weight_grad, out_weight_grad, gate_up_grad, down_grad = (
        lax.psum_scatter(qkv_weight_grad, ("fsdp", "context"), scatter_dimension=1, tiled=True),
        lax.psum_scatter(out_weight_grad, ("fsdp", "context"), scatter_dimension=1, tiled=True),
        lax.psum_scatter(ffn_sent[0], ("fsdp", "context"), scatter_dimension=1, tiled=True),
        lax.psum_scatter(ffn_sent[1], ("fsdp", "context"), scatter_dimension=1, tiled=True),
    )
    return (
        block_out.astype(bf16),
        input_grad,
        attn_gain_grad,
        attn_bias_grad,
        qkv_weight_grad,
        qkv_bias_grad,
        out_weight_grad,
        ffn_gain_grad,
        ffn_bias_grad,
        gate_up_grad,
        down_grad,
    )


def solution(mesh):
    in_specs = (
        P(("fsdp", "context"), None),
        P("fsdp", None),
        P(),
        P(),
        P(None, ("fsdp", "context"), "tensor"),
        P(None, "tensor"),
        P("tensor", ("fsdp", "context")),
        P(),
        P(),
        P(None, ("fsdp", "context"), "tensor"),
        P("tensor", ("fsdp", "context")),
        P(("fsdp", "context"), None),
    )
    out_specs = (
        P(("fsdp", "context"), None),
        P(("fsdp", "context"), None),
        P(),
        P(),
        P(None, ("fsdp", "context"), "tensor"),
        P(None, "tensor"),
        P("tensor", ("fsdp", "context")),
        P(),
        P(),
        P(None, ("fsdp", "context"), "tensor"),
        P("tensor", ("fsdp", "context")),
    )
    return jax.shard_map(
        on_device, mesh=mesh, in_specs=in_specs, out_specs=out_specs, check_vma=False
    )
```

profile of v0, /device:TPU:0, one launch (start us, length us, event | category | flops | bytes accessed | tf_op | source)
XLA Modules:
  0.0 1005.2 jit_solution(916874820785395383)
XLA Ops:
  10.4 1.4 convert_reduce_fusion
  13.0 45.2 %all-gather.5.cloned.1.call-done = bf16[3,2048,512]{2,1,0:T(8,128)(2,1)} async-done(((bf16[3,256,512]{2,1,0:T(8,128)(2,1)}), bf16[3,2048,512]{2,1,0:T(8,128)(2,1)}) %all-gather.5.cloned.1.call-update) | async-done | bytes 6291472 | tf_op jit(solution)/shard_map/all_gather | solution.py:90
  58.2 4.6 add_bitcast_fusion
  63.7 3.2 collective-permute-start
  67.1 14.1 %collective-permute-done = bf16[2,256,512]{2,1,0:T(8,128)(2,1)S(1)} collective-permute-done((bf16[2,256,512]{2,1,0:T(8,128)(2,1)S(1)}, bf16[2,256,512]{2,1,0:T(8,128)(2,1)S(1)}, u32[]{:S(2)}, u32[]{:S(2)}) %collective-permute-start) | collective-permute-done | bytes 524320 | tf_op jit(solution)/shard_map/ppermute | solution.py:19
  82.8 1.2 fusion
  84.9 1.4 fusion.27
  86.3 4.8 all-gather.7.cloned.1.call-done
  91.1 3.6 fusion.51
  96.2 85.3 %all-reduce.6.cloned.1.call-done = f32[256,2048]{1,0:T(8,128)} async-done(((f32[256,2048]{1,0:T(8,128)}), f32[256,2048]{1,0:T(8,128)}) %all-reduce.6.cloned.1.call-update) | async-done | bytes 2097168 | tf_op jit(solution)/shard_map/psum | solution.py:62
  181.5 1.9 fusion.47
  183.8 66.3 %all-gather.9.cloned.1.call-done = bf16[2,2048,1408]{2,1,0:T(8,128)(2,1)} async-done(((bf16[2,256,1408]{2,1,0:T(8,128)(2,1)}), bf16[2,2048,1408]{2,1,0:T(8,128)(2,1)}) %all-gather.9.cloned.1.call-update) | async-done | bytes 11534352 | tf_op jit(solution)/shard_map/all_gather | solution.py:92
  250.1 9.1 convolution_bitcast_fusion.2
  259.2 37.2 %all-gather.11.cloned.1.call-done = bf16[1408,2048]{1,0:T(8,128)(2,1)} async-done(((bf16[1408,256]{1,0:T(8,128)(2,1)}), bf16[1408,2048]{1,0:T(8,128)(2,1)}) %all-gather.11.cloned.1.call-update) | async-done | bytes 5767184 | tf_op jit(solution)/shard_map/all_gather | solution.py:93
  296.3 7.0 fusion.31
  304.5 4.5 convolution_bitcast_fusion.4
  309.7 86.0 %all-reduce.8.cloned.1.call-done = f32[256,2048]{1,0:T(8,128)} async-done(((f32[256,2048]{1,0:T(8,128)}), f32[256,2048]{1,0:T(8,128)}) %all-reduce.8.cloned.1.call-update) | async-done | bytes 2097168 | tf_op jit(solution)/shard_map/psum | solution.py:66
  395.7 3.3 multiply_reduce_fusion.1
  399.9 1.3 copy-done.3
  401.2 1.4 convolution_convert_fusion
  402.6 1.1 copy.61
  403.7 3.2 fusion.22
  407.3 1.4 multiply_reduce_fusion
  410.5 1.4 collective-permute-start.1
  411.9 3.1 fusion.52
  416.5 20.8 %collective-permute-done.1 = f32[2,256,8,64]{1,3,2,0:T(8,128)S(1)} collective-permute-done((f32[2,256,8,64]{1,3,2,0:T(8,128)S(1)}, f32[2,256,8,64]{1,3,2,0:T(8,128)S(1)}, u32[]{:S(2)}, u32[]{:S(2)}) %collective-permute-start.1) | collective-permute-done | bytes 1048608 | tf_op jit(solution)/shard_map/ppermute | solution.py:19
  439.0 1.1 copy.64
  440.1 1.7 pad_maximum_fusion.8
  441.7 1.8 copy.62
  443.5 1.6 pad_maximum_fusion.9
  445.2 1.8 copy.63
  447.0 6.1 convolution_bitcast_fusion.3
  453.8 7.6 convolution_bitcast_fusion.1
  462.2 11.0 %convolution_bitcast_fusion = f32[2,2048,1408]{1,2,0:T(8,128)} fusion(bf16[1,256,1408]{2,1,0:T(8,128)(2,1)} %copy-done.18, bf16[1,256,1408]{2,1,0:T(8,128)(2,1)} %copy-done.17, f32[256,2048]{1,0:T(8,128)S(1)} %get-tuple-element.123, f32[2048]{0:T(1024)S(1)} %copy-done.38, f32[2048]{0:T(1024)S(1)} %copy-done.21, f32[256]{0:T(256)S(1)} %copy-done.34, ...), kind=kOutput, calls=%fused_computation | convolution fusion | flops 2956132352 | bytes 26626048 | tf_op jit(solution)/shard_map/td,ktf->kdf/dot_general | solution.py:171
  473.2 4.3 fusion.35
  477.6 7.4 fusion.53
  485.1 1.2 convert_reduce_fusion.1
  486.3 120.6 %all-reduce.10.cloned.1.call-done = (f32[256,2048]{1,0:T(8,128)}, f32[256,2048]{1,0:T(8,128)}) async-done(((f32[256,2048]{1,0:T(8,128)}, f32[256,2048]{1,0:T(8,128)}), (f32[256,2048]{1,0:T(8,128)}, f32[256,2048]{1,0:T(8,128)})) %all-reduce.10.cloned.1.call-update) | async-done | bytes 4194320 | tf_op jit(solution)/shard_map/psum | solution.py:62
  606.9 2.6 fusion.15
  609.5 25.4 %all-reduce = (f32[2048]{0:T(1024)}, f32[2048]{0:T(1024)}, f32[3,512]{1,0:T(4,128)}, f32[2048]{0:T(1024)}, f32[2048]{0:T(1024)}) all-reduce(f32[2048]{0:T(1024)S(1)} %get-tuple-element.109, f32[2048]{0:T(1024)S(1)} %get-tuple-element.114, ...), channel_id=1, replica_groups=mesh['fsdp'=4,'context'=2,'tensor'=4] {'fsdp','context'}, use_global_device_ids=true, to_apply=%region_18.19 | all-reduce | flops 9728 | bytes 77824 | tf_op jit(solution)/shard_map/psum | solution.py:230
  634.9 3.0 add_convert_fusion
  637.9 1.8 fusion.14
  639.7 62.5 %reduce-scatter.5.cloned.1.call-done = f32[3,256,512]{1,2,0:T(8,128)} async-done(((f32[3,2048,512]{1,2,0:T(8,128)}), f32[3,256,512]{1,2,0:T(8,128)}) %reduce-scatter.5.cloned.1.call-update) | async-done | bytes 1572880 | tf_op jit(solution)/shard_map/reduce_scatter | solution.py:235
  702.2 3.0 copy.67
  705.3 147.0 %reduce-scatter.9.cloned.1.call-done = f32[2,256,1408]{1,2,0:T(8,128)} async-done(((f32[2,2048,1408]{1,2,0:T(8,128)}), f32[2,256,1408]{1,2,0:T(8,128)}) %reduce-scatter.9.cloned.1.call-update) | async-done | bytes 2883600 | tf_op jit(solution)/shard_map/reduce_scatter | solution.py:237
  852.2 3.4 copy.68
  855.6 52.1 %reduce-scatter.7.cloned.1.call-done = f32[512,256]{1,0:T(8,128)} async-done(((f32[512,2048]{1,0:T(8,128)}), f32[512,256]{1,0:T(8,128)}) %reduce-scatter.7.cloned.1.call-update) | async-done | bytes 524304 | tf_op jit(solution)/shard_map/reduce_scatter | solution.py:236
  907.7 90.9 %reduce-scatter.11.cloned.1.call-done = f32[1408,256]{1,0:T(8,128)} async-done(((f32[1408,2048]{1,0:T(8,128)}), f32[1408,256]{1,0:T(8,128)}) %reduce-scatter.11.cloned.1.call-update) | async-done | bytes 1441808 | tf_op jit(solution)/shard_map/reduce_scatter | solution.py:238
  (152 shorter events, 18.8 us)
Async XLA Ops:
  7.2 4.6 copy-start.2
  7.2 51.0 %copy-start.19 = (f32[2048]{0:T(1024)S(1)}, f32[2048]{0:T(1024)}, u32[]{:S(2)}) copy-start(f32[2048]{0:T(1024)} %param.14) | copy-start | bytes 24580
  7.2 51.0 %copy-start.35 = (f32[2048]{0:T(1024)S(1)}, f32[2048]{0:T(1024)}, u32[]{:S(2)}) copy-start(f32[2048]{0:T(1024)} %param.15) | copy-start | bytes 24580
  7.2 51.0 %copy-start.40 = (f32[3,512]{1,0:T(4,128)S(1)}, f32[3,512]{1,0:T(4,128)}, u32[]{:S(2)}) copy-start(f32[3,512]{1,0:T(4,128)} %param.17) | copy-start | bytes 18436
  7.2 51.0 %all-gather.5.cloned.1.call-start = ((), (), s32[]{:S(2)}) async-start(), calls=%async_computation.4 | async-start | bytes 7077888 | tf_op jit(solution)/shard_map/all_gather | solution.py:90
  8.0 83.2 %all-gather.7.cloned.1.call-start = ((), (), s32[]{:S(2)}) async-start(), calls=%async_computation.5 | async-start | bytes 2359296 | tf_op jit(solution)/shard_map/all_gather | solution.py:91
  8.7 172.8 %all-reduce.6.cloned.1.call-start = ((), (), s32[]{:S(2)}) async-start(), calls=%async_computation.6 | async-start | bytes 4194304 | tf_op jit(solution)/shard_map/psum | solution.py:62
  11.8 51.0 %copy-start.27 = (f32[256]{0:T(256)}, f32[256]{0:T(256)S(1)}, u32[]{:S(2)}) copy-start(f32[256]{0:T(256)S(1)} %broadcast_multiply_fusion.5) | copy-start | bytes 3076
  13.0 49.9 %copy-start.31 = (f32[256]{0:T(256)}, f32[256]{0:T(256)S(1)}, u32[]{:S(2)}) copy-start(f32[256]{0:T(256)S(1)} %add_rsqrt_fusion.1) | copy-start | bytes 3076
  63.7 17.5 %collective-permute-start = (bf16[2,256,512]{2,1,0:T(8,128)(2,1)S(1)}, bf16[2,256,512]{2,1,0:T(8,128)(2,1)S(1)}, u32[]{:S(2)}, u32[]{:S(2)}) collective-permute-start(bf16[2,256,512]{2,1,0:T(8,128)(2,1)S(1)} %pad_maximum_fusion.5), channel_id=1, source_target_pairs={{0,4},{1,5},{2,6},{3,7},{8,12},{9,13},{10,14},{11,15},{16,20},{17,... | collective-permute-start | bytes 1572872 | tf_op jit(solution)/shard_map/ppermute | solution.py:19
  67.1 14.7 %copy-start.15 = (bf16[256,8,48]{0,2,1:T(8,128)(2,1)}, bf16[256,8,48]{0,2,1:T(8,128)(2,1)S(1)}, u32[]{:S(2)}) copy-start(bf16[256,8,48]{0,2,1:T(8,128)(2,1)S(1)} %slice.186) | copy-start | bytes 589828
  81.6 1.2 copy-start.11
  81.8 2.2 copy-start.9
  82.8 2.1 copy-start
  82.8 2.1 copy-start.24
  86.3 8.5 copy-start.13
  94.8 155.3 %all-gather.9.cloned.1.call-start = ((), (), s32[]{:S(2)}) async-start(), calls=%async_computation.7 | async-start | bytes 12976128 | tf_op jit(solution)/shard_map/all_gather | solution.py:92
  95.4 200.9 %all-gather.11.cloned.1.call-start = ((), (), s32[]{:S(2)}) async-start(), calls=%async_computation.8 | async-start | bytes 6488064 | tf_op jit(solution)/shard_map/all_gather | solution.py:93
  96.0 299.7 %all-reduce.8.cloned.1.call-start = ((), (), s32[]{:S(2)}) async-start(), calls=%async_computation.9 | async-start | bytes 4194304 | tf_op jit(solution)/shard_map/psum | solution.py:66
  183.3 66.7 %copy-start.20 = (f32[2048]{0:T(1024)S(1)}, f32[2048]{0:T(1024)}, u32[]{:S(2)}) copy-start(f32[2048]{0:T(1024)} %param.19) | copy-start | bytes 24580
  183.4 66.7 %copy-start.37 = (f32[2048]{0:T(1024)S(1)}, f32[2048]{0:T(1024)}, u32[]{:S(2)}) copy-start(f32[2048]{0:T(1024)} %param.20) | copy-start | bytes 24580
  183.4 215.5 %copy-start.29 = (f32[256]{0:T(256)}, f32[256]{0:T(256)S(1)}, u32[]{:S(2)}) copy-start(f32[256]{0:T(256)S(1)} %broadcast_multiply_fusion.4) | copy-start | bytes 3076
  183.8 215.2 %copy-start.33 = (f32[256]{0:T(256)}, f32[256]{0:T(256)S(1)}, u32[]{:S(2)}) copy-start(f32[256]{0:T(256)S(1)} %add_rsqrt_fusion) | copy-start | bytes 3076
  296.3 8.1 copy-start.39
  303.4 0.9 copy-start.17
  303.4 1.1 copy-start.18
  309.0 297.9 %all-reduce.10.cloned.1.call-start = ((), (), s32[]{:S(2)}) async-start(), calls=%async_computation.14 | async-start | bytes 8388608 | tf_op jit(solution)/shard_map/psum | solution.py:62
  395.7 3.3 copy-start.7
  395.7 3.3 copy-start.8
  399.0 2.2 copy-start.5
  399.9 1.3 copy-start.3
  403.7 3.5 copy-start.1
  403.7 3.6 copy-start.10
  408.7 3.2 slice-start
  408.8 1.1 copy-start.16
  408.8 3.1 slice-start.1
  410.3 1.6 copy-start.14
  410.5 26.9 %collective-permute-start.1 = (f32[2,256,8,64]{1,3,2,0:T(8,128)S(1)}, f32[2,256,8,64]{1,3,2,0:T(8,128)S(1)}, u32[]{:S(2)}, u32[]{:S(2)}) collective-permute-start(f32[2,256,8,64]{1,3,2,0:T(8,128)S(1)} %pad_maximum_fusion.1), channel_id=1, source_target_pairs={{4,0},{5,1},{6,2},{7,3},{12,8},{13,9},{14,10},{15,11},{20,16},{21,... | collective-permute-start | bytes 3145736 | tf_op jit(solution)/shard_map/ppermute | solution.py:19
  411.9 3.1 copy-start.12
  415.8 23.1 %copy-start.26 = (f32[256,8]{0,1:T(8,128)S(1)}, f32[256,8]{0,1:T(8,128)}, u32[]{:S(2)}) copy-start(f32[256,8]{0,1:T(8,128)} %get-tuple-element.145) | copy-start | bytes 24580
  453.2 249.1 %reduce-scatter.5.cloned.1.call-start = ((), (), s32[]{:S(2)}) async-start(), calls=%async_computation.10 | async-start | bytes 14155776 | tf_op jit(solution)/shard_map/reduce_scatter | solution.py:235
  461.5 390.8 %reduce-scatter.9.cloned.1.call-start = ((), (), s32[]{:S(2)}) async-start(), calls=%async_computation.12 | async-start | bytes 25952256 | tf_op jit(solution)/shard_map/reduce_scatter | solution.py:237
  473.1 434.6 %reduce-scatter.7.cloned.1.call-start = ((), (), s32[]{:S(2)}) async-start(), calls=%async_computation.11 | async-start | bytes 4718592 | tf_op jit(solution)/shard_map/reduce_scatter | solution.py:236
  477.6 521.1 %reduce-scatter.11.cloned.1.call-start = ((), (), s32[]{:S(2)}) async-start(), calls=%async_computation.13 | async-start | bytes 12976128 | tf_op jit(solution)/shard_map/reduce_scatter | solution.py:238
  485.1 124.4 %copy-start.22 = (f32[2048]{0:T(1024)S(1)}, f32[2048]{0:T(1024)}, u32[]{:S(2)}) copy-start(f32[2048]{0:T(1024)} %get-tuple-element.107) | copy-start | bytes 24580
  485.1 124.4 %copy-start.23 = (f32[2048]{0:T(1024)S(1)}, f32[2048]{0:T(1024)}, u32[]{:S(2)}) copy-start(f32[2048]{0:T(1024)} %get-tuple-element.113) | copy-start | bytes 24580
  634.9 3.0 copy-start.4
  634.9 3.0 copy-start.6
  (8 other events, 5.6 us)
Sparse Core Ops, SparseCore 0:
  10.0 48.2 all-gather.4
  60.1 31.0 all-gather.6
  94.9 86.4 all-reduce.5
  183.4 66.6 all-gather.8
  251.9 44.3 all-gather.10
  309.1 86.5 all-reduce.7
  453.3 153.5 all-reduce.9
  610.8 91.3 reduce-scatter.4
  706.3 145.9 reduce-scatter.8
  856.4 51.2 reduce-scatter.6
  911.8 86.7 reduce-scatter.10
where the time goes:
time: 1010 us
  waiting for transfers between devices  835 us (83%)
  matrix products  78.1 us (8%)
  other arithmetic  25.9 us (3%)
  blocking collectives  25.4 us (3%)
  local copies, waits for them, and re-layouts  20.1 us (2%)
  between operations  14.5 us (1%)
    psum x2, waiting for transfers between devices, branch_total(): return lax.psum(partial_value, 'tensor')  206 us
    reduce_scatter x1, waiting for transfers between devices, on_device(): lax.psum_scatter(ffn_sent[0], ('fsdp', 'context'), scatter_dimension=1, t...  147 us
    reduce_scatter x1, waiting for transfers between devices, on_device(): lax.psum_scatter(ffn_sent[1], ('fsdp', 'context'), scatter_dimension=1, t...  90.9 us
    psum x1, waiting for transfers between devices, grad_total(): return lax.psum(partial_value, 'tensor')  86 us
    all_gather x1, waiting for transfers between devices, on_device(): lax.all_gather(gate_up_weight, ('fsdp', 'context'), axis=1, tiled=True)  66.3 us
    reduce_scatter x1, waiting for transfers between devices, on_device(): lax.psum_scatter(qkv_weight_grad, ('fsdp', 'context'), scatter_dimension=...  62.5 us
    reduce_scatter x1, waiting for transfers between devices, on_device(): lax.psum_scatter(out_weight_grad, ('fsdp', 'context'), scatter_dimension=...  52.1 us
    all_gather x1, waiting for transfers between devices, on_device(): lax.all_gather(qkv_weight, ('fsdp', 'context'), axis=1, tiled=True)  45.2 us
  transfers between devices with their start and end apart: 13, of which 13 were waited for; matrix products, arithmetic and copies ran while one was open for 7% of the time, Pallas kernels for 0%

commit v1 on v0

v1 whole, which is shorter than its diff:
```python
import functools
import math

import jax
import jax.numpy as jnp
from jax import lax
from jax.experimental import pallas as pl
from jax.experimental.pallas import tpu as pltpu
from jax.sharding import PartitionSpec as P

HD = 64
ROT = 16
EPS = 1e-05
NEG = -1e30
f32 = jnp.float32
bf16 = jnp.bfloat16
VM = pl.BlockSpec(memory_space=pltpu.VMEM)
SM = pl.BlockSpec(memory_space=pltpu.SMEM)
PLANE = ("fsdp", "context")


def shape(dims, dtype):
    return jax.ShapeDtypeStruct(tuple(dims), dtype)


def call(kernel, name, outs, args, specs, scratch=(), flops=0, moved=0):
    return pl.pallas_call(
        kernel,
        name=name,
        out_shape=outs,
        in_specs=specs,
        out_specs=jax.tree.map(lambda _: VM, outs),
        scratch_shapes=list(scratch),
        compiler_params=pltpu.CompilerParams(vmem_limit_bytes=56 * 2**20),
        cost_estimate=pl.CostEstimate(flops=flops, bytes_accessed=moved, transcendentals=0),
    )(*args)


def dot(a, b, dims=((1,), (0,))):
    return lax.dot_general(a, b, (dims, ((), ())), preferred_element_type=f32)


NT = ((1,), (1,))
TN = ((0,), (0,))


class Plane:
    def __init__(self):
        self.fsdp = lax.axis_size("fsdp")
        self.context = lax.axis_size("context")
        self.count = self.fsdp * self.context
        self.me = lax.axis_index("fsdp") * self.context + lax.axis_index("context")
        core = self.context
        rest = [1 << i for i in range(int(math.log2(self.count))) if (1 << i) != core]
        self.core = core
        self.orders = (rest[::-1], rest)

    def swap(self, value, bit):
        if bit < self.context:
            pairs = [(i, i ^ bit) for i in range(self.context)]
            return lax.ppermute(value, "context", pairs)
        step = bit // self.context
        pairs = [(i, i ^ step) for i in range(self.fsdp)]
        return lax.ppermute(value, "fsdp", pairs)

    def gather(self, halves):
        slots = [{0: halves[0]}, {0: halves[1]}]
        for step in range(len(self.orders[0]) + 1):
            for h in (0, 1):
                order = self.orders[h] + [self.core]
                bit = order[step]
                for k in list(slots[h]):
                    slots[h][k ^ bit] = self.swap(slots[h][k], bit)
        return slots

    def scatter(self, slots):
        slots = [dict(slots[0]), dict(slots[1])]
        for step in range(len(self.orders[0]) + 1):
            last = step == len(self.orders[0])
            for h in (0, 1):
                order = [self.core] + self.orders[h]
                bit = order[step]
                sent = {k: self.swap(v, bit) for k, v in slots[h].items() if k & bit}
                kept = {}
                for k, v in slots[h].items():
                    if not k & bit:
                        total = v.astype(f32) + sent[k ^ bit].astype(f32)
                        kept[k] = total if last else total.astype(bf16)
                slots[h] = kept
        return slots[0][0], slots[1][0]

    def total(self, value, over_tensor):
        value = value + 0.0
        bit = 1
        while bit < self.count:
            value = value + self.swap(value, bit)
            bit *= 2
        if over_tensor:
            value = value + sum(tensor_swap(value, j) for j in range(1, lax.axis_size("tensor")))
        return value


def tensor_swap(value, j):
    peers = lax.axis_size("tensor")
    return lax.ppermute(value, "tensor", [(i, i ^ j) for i in range(peers)])


def tensor_exchange(parts):
    return [tensor_swap(part, j) for j, part in enumerate(parts) if j]


def tensor_gather(part):
    return [part] + [tensor_swap(part, j) for j in range(1, lax.axis_size("tensor"))]


def row_stats(x3):
    size = x3.shape[0] * x3.shape[2]
    mean = jnp.sum(jnp.sum(x3, axis=0), axis=-1, keepdims=True) / size
    center = x3 - mean[None]
    var = jnp.sum(jnp.sum(center * center, axis=0), axis=-1, keepdims=True) / size
    inv = lax.rsqrt(var + EPS)
    return center * inv[None], inv


def row_mean(x3):
    return jnp.sum(jnp.sum(x3, axis=0), axis=-1, keepdims=True) / (x3.shape[0] * x3.shape[2])


def split(x, count):
    width = x.shape[1] // count
    return jnp.stack([x[:, i * width : (i + 1) * width] for i in range(count)])


def norm_kernel(x_ref, gain_ref, bias_ref, out_ref):
    normal, _ = row_stats(split(x_ref[...].astype(f32), out_ref.shape[0]))
    out_ref[...] = (normal * gain_ref[...] + bias_ref[...]).astype(bf16)


def reorder_kernel(at_ref, x_ref, out_ref):
    rows = x_ref.shape[0] // at_ref.shape[0]
    for j in range(at_ref.shape[0]):
        block = x_ref[pl.ds(pl.multiple_of(at_ref[j] * rows, rows), rows), :]
        out_ref[:, j * rows : (j + 1) * rows, :] = split(block, out_ref.shape[0])


def spin(x, tables, sign):
    parts = []
    for i in range(x.shape[1] // 128):
        v = x[:, i * 128 : (i + 1) * 128]
        turned = pltpu.roll(v, 128 - ROT // 2, 1) * tables[1] + pltpu.roll(v, ROT // 2, 1) * tables[2]
        parts.append(v * tables[0] + (turned if sign > 0 else -turned))
    return jnp.concatenate(parts, axis=1)


def qkv_kernel(count, order_ref, normed_ref, bias_ref, table_ref, *refs):
    weights = refs[: 2 * count]
    q_ref, kv_ref = refs[2 * count :]
    width = q_ref.shape[1] // 2
    for h in range(2):
        cols = slice(h * width, (h + 1) * width)
        for j in range(3):
            total = bias_ref[j, :, cols]
            for k in range(count):
                total = total + dot(normed_ref[order_ref[k]], weights[h * count + k][j])
            if j < 2:
                total = spin(total, table_ref[...], 1)
            if j == 0:
                q_ref[:, cols] = total.astype(bf16)
            else:
                kv_ref[j - 1, :, cols] = total.astype(bf16)


def head_mask(rows, h):
    lane = lax.broadcasted_iota(jnp.int32, (rows, 2 * HD), 1)
    return (lane // HD) == h


def attend_kernel(count, order_ref, at_ref, hide_ref, q_ref, here_ref, early_ref, *refs):
    weights = refs[: 2 * count]
    att_ref, log_ref, own_ref = refs[2 * count : 2 * count + 3]
    sends = refs[2 * count + 3 : -1]
    part_ref = refs[-1]
    rows, feat = q_ref.shape
    scale = HD**-0.5
    for pair in range(feat // (2 * HD)):
        cols = slice(pair * 2 * HD, (pair + 1) * 2 * HD)
        q = q_ref[:, cols]
        k = jnp.concatenate([early_ref[0, :, cols], here_ref[0, :, cols]], axis=0)
        v = jnp.concatenate([early_ref[1, :, cols], here_ref[1, :, cols]], axis=0)
        out = []
        for h in range(2):
            mask = head_mask(rows, h)
            scores = dot(jnp.where(mask, q, 0), k, NT) * scale + hide_ref[...]
            top = jnp.max(scores, axis=-1, keepdims=True)
            exps = jnp.exp(scores - top)
            total = jnp.sum(exps, axis=-1, keepdims=True)
            log_ref[2 * pair + h] = top + jnp.log(total)
            out.append(dot((exps / total).astype(bf16), v))
        att_ref[:, cols] = jnp.where(head_mask(rows, 0), out[0], out[1]).astype(bf16)
    half = feat // 2
    for k in range(count):
        part_ref[order_ref[k]] = dot(att_ref[:, :half], weights[k][...]) + dot(
            att_ref[:, half:], weights[count + k][...]
        )
    hand_out(at_ref, part_ref, own_ref, sends)


def hand_out(at_ref, part_ref, own_ref, sends):
    rows = own_ref.shape[1]
    for j in range(at_ref.shape[0]):
        block = part_ref[:, pl.ds(pl.multiple_of(at_ref[j] * rows, rows), rows), :]
        if j == 0:
            own_ref[...] = block
        else:
            sends[j - 1][...] = block.astype(bf16)


def mid_kernel(at_ref, x_ref, gain_ref, bias_ref, own_ref, *refs):
    mid_ref, normed_ref = refs[-2:]
    rows = own_ref.shape[1]
    total = own_ref[...]
    for ref in refs[:-2]:
        total = total + ref[...].astype(f32)
    block = x_ref[pl.ds(pl.multiple_of(at_ref[0] * rows, rows), rows), :].astype(f32)
    mid = split(block, own_ref.shape[0]) + total
    mid_ref[...] = mid
    normal, _ = row_stats(mid)
    normed_ref[...] = (normal * gain_ref[...] + bias_ref[...]).astype(bf16)


def stacked(refs):
    return jnp.concatenate([ref[0] for ref in refs], axis=0)


def ffn_kernel(peers, *refs):
    blocks = refs[:peers]
    cot_ref, w_ref, hidden_ref, gate_grad_ref, up_grad_ref, gate, up, back = refs[peers:]
    step = pl.program_id(0)
    width = cot_ref.shape[2]
    x = stacked(blocks)

    @pl.when(step == 0)
    def _():
        gate[...] = jnp.zeros_like(gate)
        up[...] = jnp.zeros_like(up)
        back[...] = jnp.zeros_like(back)

    gate[...] += dot(x, w_ref[0, :width])
    up[...] += dot(x, w_ref[0, width : 2 * width])
    back[...] += dot(cot_ref[0], w_ref[0, 2 * width :])

    @pl.when(step == pl.num_programs(0) - 1)
    def _():
        gate_pre, up_pre, hidden_grad = gate[...], up[...], back[...]
        sigma = 1.0 / (1.0 + jnp.exp(-gate_pre))
        silu = gate_pre * sigma
        hidden_ref[...] = (silu * up_pre).astype(bf16)
        gate_grad_ref[...] = (
            hidden_grad * up_pre * sigma * (1.0 + gate_pre * (1.0 - sigma))
        ).astype(bf16)
        up_grad_ref[...] = (hidden_grad * silu).astype(bf16)


def cut(total, own_ref, sends):
    rows = own_ref.shape[1]
    own_ref[0] = total[:rows]
    for j, ref in enumerate(sends):
        ref[0] = total[(j + 1) * rows : (j + 2) * rows].astype(bf16)


def two_grad_kernel(gate_grad_ref, up_grad_ref, w_ref, own_ref, *sends):
    width = own_ref.shape[2]
    total = dot(gate_grad_ref[...], w_ref[0, :width], NT) + dot(
        up_grad_ref[...], w_ref[0, width : 2 * width], NT
    )
    cut(total, own_ref, sends)


def down_kernel(hidden_ref, w_ref, own_ref, *sends):
    cut(dot(hidden_ref[...], w_ref[0], NT), own_ref, sends)


def ffn_weights_kernel(peers, *refs):
    blocks = refs[:peers]
    cot_ref, hidden_ref, gate_grad_ref, up_grad_ref, out_ref = refs[peers:]
    width = cot_ref.shape[2]
    x = stacked(blocks)
    out_ref[0, :width] = dot(x, gate_grad_ref[...], TN).astype(bf16)
    out_ref[0, width : 2 * width] = dot(x, up_grad_ref[...], TN).astype(bf16)
    out_ref[0, 2 * width :] = dot(cot_ref[0], hidden_ref[...], TN).astype(bf16)


def norm_back(normal, inv, grad, gain):
    scaled = grad * gain
    inner = row_mean(scaled * normal)
    return inv[None] * (scaled - row_mean(scaled)[None] - normal * inner[None])


def token_sum(x3):
    return jnp.sum(x3, axis=1, keepdims=True)


def mid_back_kernel(mid_ref, cot_ref, gain_ref, own_ref, *refs):
    grad_ref, low_ref, gain_grad_ref, bias_grad_ref = refs[-4:]
    total = own_ref[...]
    for ref in refs[:-4]:
        total = total + ref[...].astype(f32)
    normal, inv = row_stats(mid_ref[...])
    gain_grad_ref[...] = token_sum(total * normal)
    bias_grad_ref[...] = token_sum(total)
    grad = cot_ref[...].astype(f32) + norm_back(normal, inv, total, gain_ref[...])
    grad_ref[...] = grad
    low_ref[...] = grad.astype(bf16)


def block_out_kernel(mid_ref, own_ref, *refs):
    total = mid_ref[...] + own_ref[...]
    for ref in refs[:-1]:
        total = total + ref[...].astype(f32)
    refs[-1][...] = total.astype(bf16)


def attend_back_kernel(
    count, peers, order_ref, at_ref, hide_ref, table_ref, q_ref, here_ref, early_ref, log_ref, *refs
):
    lows = refs[:peers]
    weights = refs[peers : peers + 2 * count]
    low_ref, dq_ref, dhere_ref, dearly_ref, datt = refs[peers + 2 * count :]
    rows, feat = q_ref.shape
    part = rows // peers
    scale = HD**-0.5
    for j in range(peers):
        low_ref[:, pl.ds(pl.multiple_of(at_ref[j] * part, part), part), :] = lows[j][...]
    half = feat // 2
    for h in range(2):
        total = dot(low_ref[order_ref[0]], weights[h * count][...], NT)
        for k in range(1, count):
            total = total + dot(low_ref[order_ref[k]], weights[h * count + k][...], NT)
        datt[:, h * half : (h + 1) * half] = total.astype(bf16)
    for pair in range(feat // (2 * HD)):
        cols = slice(pair * 2 * HD, (pair + 1) * 2 * HD)
        q = q_ref[:, cols]
        k = jnp.concatenate([early_ref[0, :, cols], here_ref[0, :, cols]], axis=0)
        v = jnp.concatenate([early_ref[1, :, cols], here_ref[1, :, cols]], axis=0)
        da = datt[:, cols]
        grads = []
        for h in range(2):
            mask = head_mask(rows, h)
            scores = dot(jnp.where(mask, q, 0), k, NT) * scale + hide_ref[...]
            probs = jnp.exp(scores - log_ref[2 * pair + h])
            weight_grad = dot(jnp.where(mask, da, 0), v, NT)
            inner = jnp.sum(probs * weight_grad, axis=-1, keepdims=True)
            score_grad = (probs * (weight_grad - inner)).astype(bf16)
            grads.append(
                (
                    dot(score_grad, k) * scale,
                    dot(score_grad, q, TN) * scale,
                    dot(probs.astype(bf16), da, TN),
                )
            )
        dq = jnp.where(head_mask(rows, 0), grads[0][0], grads[1][0])
        dq_ref[:, cols] = spin(dq, table_ref[...], -1).astype(bf16)
        for i in (1, 2):
            both = jnp.where(head_mask(2 * rows, 0), grads[0][i], grads[1][i])
            dearly_ref[i - 1, :, cols] = both[:rows].astype(bf16)
            dhere_ref[i - 1, :, cols] = both[rows:]


def out_weights_kernel(count, order_ref, att_ref, low_ref, *outs):
    half = att_ref.shape[1] // 2
    for h in range(2):
        for k in range(count):
            outs[h * count + k][...] = dot(
                att_ref[:, h * half : (h + 1) * half], low_ref[order_ref[k]], TN
            ).astype(bf16)


def one_grad_kernel(
    count, order_ref, at_ref, x_ref, table_ref, dq_ref, dhere_ref, dback_ref, *refs
):
    weights = refs[: 2 * count]
    back_ref, bias_ref, gain_grad_ref, norm_bias_ref, own_ref = refs[2 * count : 2 * count + 5]
    sends = refs[2 * count + 5 : -1]
    part_ref = refs[-1]
    back_ref[0] = dq_ref[...]
    dk = dhere_ref[0] + dback_ref[0].astype(f32)
    back_ref[1] = spin(dk, table_ref[...], -1).astype(bf16)
    back_ref[2] = (dhere_ref[1] + dback_ref[1].astype(f32)).astype(bf16)
    bias_ref[...] = jnp.sum(back_ref[...].astype(f32), axis=1, keepdims=True)
    half = dq_ref.shape[1] // 2
    for k in range(count):
        total = None
        for h in range(2):
            for j in range(3):
                term = dot(
                    back_ref[j, :, h * half : (h + 1) * half], weights[h * count + k][j], NT
                )
                total = term if total is None else total + term
        part_ref[order_ref[k]] = total
    normal, _ = row_stats(split(x_ref[...].astype(f32), count))
    gain_grad_ref[...] = token_sum(part_ref[...] * normal)
    norm_bias_ref[...] = token_sum(part_ref[...])
    hand_out(at_ref, part_ref, own_ref, sends)


def qkv_weights_kernel(count, order_ref, normed_ref, back_ref, *outs):
    half = back_ref.shape[2] // 2
    for h in range(2):
        for k in range(count):
            for j in range(3):
                outs[h * count + k][j] = dot(
                    normed_ref[order_ref[k]], back_ref[j, :, h * half : (h + 1) * half], TN
                ).astype(bf16)


def input_grad_kernel(at_ref, x_ref, gain_ref, mid_grad_ref, own_ref, *refs):
    rows = own_ref.shape[1]
    total = own_ref[...]
    for ref in refs[:-1]:
        total = total + ref[...].astype(f32)
    block = x_ref[pl.ds(pl.multiple_of(at_ref[0] * rows, rows), rows), :].astype(f32)
    normal, inv = row_stats(split(block, own_ref.shape[0]))
    refs[-1][...] = (mid_grad_ref[...] + norm_back(normal, inv, total, gain_ref[...])).astype(bf16)


def join_kernel(at_ref, *refs):
    out_ref = refs[-1]
    slices, rows, width = refs[0].shape
    for j, ref in enumerate(refs[:-1]):
        at = pl.ds(pl.multiple_of(at_ref[j] * rows, rows), rows)
        for n in range(slices):
            out_ref[at, n * width : (n + 1) * width] = ref[n]


def on_device(
    block_in,
    seq_lengths,
    attn_gain,
    attn_bias,
    qkv_weight,
    qkv_bias,
    out_weight,
    ffn_gain,
    ffn_bias,
    gate_up_weight,
    down_weight,
    out_cotangent,
):
    tok, model = block_in.shape
    feat = qkv_weight.shape[2]
    hid = down_weight.shape[0]
    plane = Plane()
    count = plane.count
    width = model // count
    peers = lax.axis_size("tensor")
    chunk = tok // peers
    heads = feat // HD
    order = plane.me ^ jnp.arange(count, dtype=jnp.int32)
    at = lax.axis_index("tensor") ^ jnp.arange(peers, dtype=jnp.int32)

    half = feat // 2
    qkv_slots = plane.gather((qkv_weight[:, :, :half], qkv_weight[:, :, half:]))
    out_slots = plane.gather((out_weight[:half], out_weight[half:]))
    qkv_list = [qkv_slots[h][k] for h in range(2) for k in range(count)]
    out_list = [out_slots[h][k] for h in range(2) for k in range(count)]
    ffn_shard = jnp.concatenate([gate_up_weight[0], gate_up_weight[1], down_weight.T], axis=0)
    ffn_all = lax.all_gather(ffn_shard, PLANE, axis=0, tiled=False)

    offset = lax.axis_index("context") * tok
    places = offset + jnp.arange(tok, dtype=jnp.int32)
    lengths = seq_lengths[0]
    ends = jnp.cumsum(lengths)
    starts = jnp.sum(jnp.where(ends[None, :] <= places[:, None], lengths[None, :], 0), axis=1)
    turn = ROT // 2
    frequency = jnp.exp(jnp.arange(turn).astype(f32) * (-2.0 * math.log(10000.0) / ROT))
    angles = (places - starts).astype(f32)[:, None] * frequency[None, :]
    cosine = jnp.tile(jnp.cos(angles), (1, 128 // turn))
    sine = jnp.tile(jnp.sin(angles), (1, 128 // turn))
    lane = jnp.arange(128)[None, :] % HD
    tables = jnp.stack(
        [
            jnp.where(lane < ROT, cosine, 1.0),
            jnp.where(lane < turn, -sine, 0.0),
            jnp.where((lane >= turn) & (lane < ROT), sine, 0.0),
        ]
    )
    key_places = offset - tok + jnp.arange(2 * tok, dtype=jnp.int32)
    visible = (key_places[None, :] <= places[:, None]) & (key_places[None, :] >= starts[:, None])
    hide = jnp.where(visible, 0.0, NEG).astype(f32)

    by_slice = lambda vec: vec.reshape(count, 1, width)
    normed_one = call(
        norm_kernel, "norm_one", shape((count, tok, width), bf16),
        (block_in, by_slice(attn_gain), by_slice(attn_bias)), [VM] * 3,
    )
    cot = call(
        reorder_kernel, "cotangent_rows", shape((count, tok, width), bf16),
        (at, out_cotangent), [SM, VM],
    )

    queries, here = call(
        functools.partial(qkv_kernel, count), "qkv",
        (shape((tok, feat), bf16), shape((2, tok, feat), bf16)),
        (order, normed_one, qkv_bias.reshape(3, 1, feat), tables, *qkv_list),
        [SM] + [VM] * (3 + 2 * count), flops=6 * tok * model * feat, moved=6 * model * feat,
    )
    early = lax.ppermute(here, "context", [(i, i + 1) for i in range(plane.context - 1)])
    sends = [shape((count, chunk, width), bf16)] * (peers - 1)
    own_shape = shape((count, chunk, width), f32)
    attended, logs, own, *parts = call(
        functools.partial(attend_kernel, count), "attend",
        (shape((tok, feat), bf16), shape((heads, tok, 1), f32), own_shape, *sends),
        (order, at, hide, queries, here, early, *out_list),
        [SM, SM] + [VM] * (4 + 2 * count),
        scratch=[pltpu.VMEM((count, tok, width), f32)],
        flops=8 * tok * tok * feat + 2 * tok * model * feat, moved=2 * model * feat,
    )
    got = tensor_exchange([None] + parts)
    mid, normed_chunk = call(
        mid_kernel, "mid", (own_shape, sends[0]),
        (at, block_in, by_slice(ffn_gain), by_slice(ffn_bias), own, *got),
        [SM] + [VM] * (4 + len(got)),
    )
    normed_two = tensor_gather(normed_chunk)

    big = pltpu.CompilerParams(vmem_limit_bytes=56 * 2**20, dimension_semantics=("arbitrary",))
    by_n = lambda *dims: pl.BlockSpec((1,) + dims, lambda n: (n,) + (0,) * len(dims))
    whole = lambda *dims: pl.BlockSpec(dims, lambda n: (0,) * len(dims))
    hid_shape = shape((tok, hid), bf16)
    hidden, gate_grad, up_grad = pl.pallas_call(
        functools.partial(ffn_kernel, peers),
        name="ffn",
        grid=(count,),
        out_shape=(hid_shape,) * 3,
        in_specs=[by_n(chunk, width)] * peers + [by_n(tok, width), by_n(3 * width, hid)],
        out_specs=[whole(tok, hid)] * 3,
        scratch_shapes=[pltpu.VMEM((tok, hid), f32)] * 3,
        compiler_params=big,
        cost_estimate=pl.CostEstimate(
            flops=6 * tok * model * hid, bytes_accessed=6 * model * hid, transcendentals=0
        ),
    )(*normed_two, cot, ffn_all)
    grad_own, *grad_parts = pl.pallas_call(
        two_grad_kernel,
        name="two_grad",
        grid=(count,),
        out_shape=(own_shape, *sends),
        in_specs=[whole(tok, hid)] * 2 + [by_n(2 * width, hid)],
        out_specs=[by_n(chunk, width)] * peers,
        compiler_params=big,
        cost_estimate=pl.CostEstimate(
            flops=4 * tok * model * hid, bytes_accessed=4 * model * hid, transcendentals=0
        ),
    )(gate_grad, up_grad, ffn_all)
    got = tensor_exchange([None] + grad_parts)
    ffn_grads = pl.pallas_call(
        functools.partial(ffn_weights_kernel, peers),
        name="ffn_weights",
        grid=(count,),
        out_shape=shape((count, 3 * width, hid), bf16),
        in_specs=[by_n(chunk, width)] * peers + [by_n(tok, width)] + [whole(tok, hid)] * 3,
        out_specs=by_n(3 * width, hid),
        compiler_params=big,
        cost_estimate=pl.CostEstimate(
            flops=6 * tok * model * hid, bytes_accessed=6 * model * hid, transcendentals=0
        ),
    )(*normed_two, cot, hidden, gate_grad, up_grad)
    ffn_total = lax.psum_scatter(ffn_grads, PLANE, scatter_dimension=0, tiled=False)
    down_own, *down_parts = pl.pallas_call(
        down_kernel,
        name="down",
        grid=(count,),
        out_shape=(own_shape, *sends),
        in_specs=[whole(tok, hid), pl.BlockSpec((1, width, hid), lambda n: (n, 2, 0))],
        out_specs=[by_n(chunk, width)] * peers,
        compiler_params=big,
        cost_estimate=pl.CostEstimate(
            flops=2 * tok * model * hid, bytes_accessed=2 * model * hid, transcendentals=0
        ),
    )(hidden, ffn_all)
    vec = shape((count, 1, width), f32)
    mid_grad, low_chunk, ffn_gain_grad, ffn_bias_grad = call(
        mid_back_kernel, "mid_back", (own_shape, sends[0], vec, vec),
        (mid, cot[:, :chunk], by_slice(ffn_gain), grad_own, *got),
        [VM] * (4 + len(got)),
    )
    low_blocks = tensor_gather(low_chunk)
    down_got = tensor_exchange([None] + down_parts)
    out_chunk = call(
        block_out_kernel, "block_out", sends[0], (mid, down_own, *down_got),
        [VM] * (2 + len(down_got)),
    )
    block_out = call(
        join_kernel, "block_out_rows", shape((tok, model), bf16),
        (at, *tensor_gather(out_chunk)), [SM] + [VM] * peers,
    )

    low, dq, dhere, dearly = call(
        functools.partial(attend_back_kernel, count, peers), "attend_back",
        (
            shape((count, tok, width), bf16), shape((tok, feat), bf16),
            shape((2, tok, feat), f32), shape((2, tok, feat), bf16),
        ),
        (order, at, hide, tables, queries, here, early, logs, *low_blocks, *out_list),
        [SM, SM] + [VM] * (6 + peers + 2 * count),
        scratch=[pltpu.VMEM((tok, feat), bf16)],
        flops=20 * tok * tok * feat + 2 * tok * model * feat, moved=2 * model * feat,
    )
    dback = lax.ppermute(dearly, "context", [(i + 1, i) for i in range(plane.context - 1)])
    out_grads = call(
        functools.partial(out_weights_kernel, count), "out_weights",
        (shape((half, width), bf16),) * (2 * count),
        (order, attended, low), [SM, VM, VM],
        flops=2 * tok * model * feat, moved=2 * model * feat,
    )
    out_a, out_b = plane.scatter(
        [{k: out_grads[h * count + k] for k in range(count)} for h in range(2)]
    )
    back, bias_grad, attn_gain_grad, attn_bias_grad, own, *parts = call(
        functools.partial(one_grad_kernel, count), "one_grad",
        (
            shape((3, tok, feat), bf16), shape((3, 1, feat), f32), vec, vec, own_shape, *sends,
        ),
        (order, at, block_in, tables, dq, dhere, dback, *qkv_list),
        [SM, SM] + [VM] * (5 + 2 * count),
        scratch=[pltpu.VMEM((count, tok, width), f32)],
        flops=6 * tok * model * feat, moved=6 * model * feat,
    )
    got = tensor_exchange([None] + parts)
    qkv_grads = call(
        functools.partial(qkv_weights_kernel, count), "qkv_weights",
        (shape((3, width, half), bf16),) * (2 * count),
        (order, normed_one, back), [SM, VM, VM],
        flops=6 * tok * model * feat, moved=6 * model * feat,
    )
    qkv_a, qkv_b = plane.scatter(
        [{k: qkv_grads[h * count + k] for k in range(count)} for h in range(2)]
    )
    grad_chunk = call(
        input_grad_kernel, "input_grad", sends[0],
        (at, block_in, by_slice(attn_gain), mid_grad, own, *got),
        [SM] + [VM] * (4 + len(got)),
    )
    input_grad = call(
        join_kernel, "input_grad_rows", shape((tok, model), bf16),
        (at, *tensor_gather(grad_chunk)), [SM] + [VM] * peers,
    )

    vectors = jnp.stack(
        [v.reshape(model) for v in (attn_gain_grad, attn_bias_grad, ffn_gain_grad, ffn_bias_grad)]
    )
    vectors = plane.total(vectors, True)
    qkv_bias_grad = plane.total(bias_grad.reshape(3, feat), False)

    return (
        block_out,
        input_grad,
        vectors[0],
        vectors[1],
        jnp.concatenate([qkv_a, qkv_b], axis=2),
        qkv_bias_grad,
        jnp.concatenate([out_a, out_b], axis=0),
        vectors[2],
        vectors[3],
        ffn_total[: 2 * width].reshape(2, width, hid).astype(f32),
        ffn_total[2 * width :].T.astype(f32),
    )


def solution(mesh):
    in_specs = (
        P(("fsdp", "context"), None),
        P("fsdp", None),
        P(),
        P(),
        P(None, ("fsdp", "context"), "tensor"),
        P(None, "tensor"),
        P("tensor", ("fsdp", "context")),
        P(),
        P(),
        P(None, ("fsdp", "context"), "tensor"),
        P("tensor", ("fsdp", "context")),
        P(("fsdp", "context"), None),
    )
    out_specs = (
        P(("fsdp", "context"), None),
        P(("fsdp", "context"), None),
        P(),
        P(),
        P(None, ("fsdp", "context"), "tensor"),
        P(None, "tensor"),
        P("tensor", ("fsdp", "context")),
        P(),
        P(),
        P(None, ("fsdp", "context"), "tensor"),
        P("tensor", ("fsdp", "context")),
    )
    return jax.shard_map(
        on_device, mesh=mesh, in_specs=in_specs, out_specs=out_specs, check_vma=False
    )
```

time: 1010 us -> 470 us (0.47)
  waiting for transfers between devices: 835 us -> 152 us
  starting transfers between devices: 5.7 us -> 136 us
  Pallas kernels: 0 us -> 104 us
  matrix products: 78.1 us -> 0 us
  blocking collectives: 25.4 us -> 0 us
  local copies, waits for them, and re-layouts: 20.1 us -> 43.6 us
    reduce_scatter x4 -> x1, waiting for transfers between devices: 353 us -> 0.01 us  [on_device(): lax.psum_scatter(ffn_grads, PLANE, scatter_dimension=0, tiled=False)]
    psum x3 -> x0, waiting for transfers between devices: 292 us -> none  [the longest x2 206 us: branch_total(): return lax.psum(partial_value, 'tensor')]
    all_gather x4 -> x1, waiting for transfers between devices: 153 us -> 0.01 us  [on_device(): ffn_all = lax.all_gather(ffn_shard, PLANE, axis=0, tiled=False)]
    ppermute x2 -> x91, starting transfers between devices: 4.59 us -> 136 us  [the longest x27 83.8 us: tensor_swap(): return lax.ppermute(value, 'tensor', [(i, i ^ j) for i in range(peers)])]
    ppermute x2 -> x91, waiting for transfers between devices: 35 us -> 152 us  [the longest x27 61.3 us: tensor_swap(): return lax.ppermute(value, 'tensor', [(i, i ^ j) for i in range(peers)])]
    pallas_call x0 -> x18, Pallas kernels: none -> 104 us  [the longest x14 60 us: call(): pl.pallas_call(kernel, name=name, out_shape=outs, in_specs=specs, out_spe...]
    dot_general x18 -> x0, matrix products: 78.1 us -> none  [the longest x1 11 us: on_device(): jnp.einsum('td,ktf->kdf', normed_two, gate_up_back, preferred_element_typ...]
    psum x1 -> x0, blocking collectives: 25.4 us -> none  [on_device(): lax.psum((attn_gain_grad, attn_bias_grad, qkv_bias_grad, ffn_gain_grad, f...]
  transfers between devices with their start and end apart: 13 -> 93, of which waited for: 13 -> 23; matrix products, arithmetic and copies ran while one was open for 7% -> 9% of each run, Pallas kernels for 0% -> 17%
where the time goes in v1:
time: 470 us; the launch traced here: 468 us
  waiting for transfers between devices  152 us (32%)
  starting transfers between devices  136 us (29%)
  Pallas kernels  104 us (22%)
  local copies, waits for them, and re-layouts  43.6 us (9%)
  other arithmetic  17.5 us (4%)
  between operations  15.1 us (3%)
    ppermute x27, starting transfers between devices, tensor_swap(): return lax.ppermute(value, 'tensor', [(i, i ^ j) for i in range(peers)])  83.8 us
    ppermute x27, waiting for transfers between devices, tensor_swap(): return lax.ppermute(value, 'tensor', [(i, i ^ j) for i in range(peers)])  61.3 us
    pallas_call x14, Pallas kernels, call(): pl.pallas_call(kernel, name=name, out_shape=outs, in_specs=specs, out_spe...  60 us
    ppermute x48, waiting for transfers between devices, swap(): return lax.ppermute(value, 'fsdp', pairs)  54.1 us
    ppermute x14, waiting for transfers between devices, swap(): return lax.ppermute(value, 'context', pairs)  36.3 us
    ppermute x48, starting transfers between devices, swap(): return lax.ppermute(value, 'fsdp', pairs)  26.7 us
    all_gather x1, local copies, waits for them, and re-layouts, on_device(): ffn_all = lax.all_gather(ffn_shard, PLANE, axis=0, tiled=False)  21.1 us
    ppermute x14, starting transfers between devices, swap(): return lax.ppermute(value, 'context', pairs)  20.4 us
  transfers between devices with their start and end apart: 93, of which 23 were waited for; matrix products, arithmetic and copies ran while one was open for 9% of the time, Pallas kernels for 17%

profile of v1, /device:TPU:0, one launch (start us, length us, event | category | flops | bytes accessed | tf_op | source)
XLA Modules:
  0.0 468.0 jit_solution(3705149141438879449)
XLA Ops:
  12.5 3.0 collective-permute-start.10
  20.8 10.8 %collective-permute-done.25.refs_12_.refs_16_ = bf16[256,256]{1,0:T(8,128)(2,1)} collective-permute-done((bf16[256,256]{1,0:T(8,128)(2,1)S(1)}, bf16[256,256]{1,0:T(8,128)(2,1)}, u32[]{:S(2)}, u32[]{:S(2)}) %collective-permute-start.25) | collective-permute-done | bytes 131104 | tf_op jit(solution)/shard_map/ppermute | solution.py:64
  33.4 2.4 collective-permute-start.11
  35.8 12.7 %collective-permute-done.3.refs_4_ = bf16[3,256,256]{2,1,0:T(8,128)(2,1)S(1)} collective-permute-done((bf16[3,256,256]{2,1,0:T(8,128)(2,1)S(1)}, bf16[3,256,256]{2,1,0:T(8,128)(2,1)S(1)}, u32[]{:S(2)}, u32[]{:S(2)}) %collective-permute-start.3) | collective-permute-done | bytes 393248 | tf_op jit(solution)/shard_map/ppermute | solution.py:64
  54.8 9.4 %collective-permute-done.11.refs_13_ = bf16[3,256,256]{2,1,0:T(8,128)(2,1)} collective-permute-done((bf16[3,256,256]{2,1,0:T(8,128)(2,1)S(1)}, bf16[3,256,256]{2,1,0:T(8,128)(2,1)}, u32[]{:S(2)}, u32[]{:S(2)}) %collective-permute-start.11) | collective-permute-done | bytes 393248 | tf_op jit(solution)/shard_map/ppermute | solution.py:64
  64.2 2.9 collective-permute-done.4.refs_5_
  70.0 3.0 norm_one.1.normed_ref
  77.5 6.0 %qkv.1 = (bf16[256,512]{1,0:T(8,128)(2,1)}, bf16[2,256,512]{2,1,0:T(8,128)(2,1)}) custom-call(s32[8]{0:T(128)} %iota_xor_fusion.order_ref, bf16[8,256,256]{2,1,0:T(8,128)(2,1)} %norm_one.1.normed_ref, f32[3,1,512]{2,1,0:T(1,128)} %reshape.288.bias_ref, f32[3,256,128]{2,1,0:T(8,128)} %pad_maximum_fusion.3.table_ref, bf16[3,256,256]{2,1,0:T(8,128)(2,1)} %copy-done.1, ...), custom_call_target="tpu_custom_call" | custom-call | flops 1610612736 | bytes 6291456 | tf_op jit(solution)/shard_map/qkv/pallas_call | solution.py:27
  83.5 3.2 collective-permute-start.14
  91.4 4.5 collective-permute-done.26.refs_13_.refs_17_
  96.4 19.7 %collective-permute-done.19.refs_5_.refs_9_ = bf16[256,256]{1,0:T(8,128)(2,1)S(1)} collective-permute-done((bf16[256,256]{1,0:T(8,128)(2,1)}, bf16[256,256]{1,0:T(8,128)(2,1)S(1)}, u32[]{:S(2)}, u32[]{:S(2)}) %collective-permute-start.19) | collective-permute-done | bytes 131104 | tf_op jit(solution)/shard_map/ppermute | solution.py:61
  118.5 7.4 %attend.1 = (bf16[256,512]{1,0:T(8,128)(2,1)}, f32[8,256,1]{2,1,0:T(8,128)}, f32[8,64,256]{2,1,0:T(8,128)}, bf16[8,64,256]{2,1,0:T(8,128)(2,1)}, bf16[8,64,256]{...) custom-call(s32[8]{0:T(128)} %iota_xor_fusion.order_ref, s32[4]{0:T(128)} %iota_xor_fusion.1.at_ref, ...), custom_call_target="tpu_custom_call" | custom-call | flops 805306368 | bytes 2097152 | tf_op jit(solution)/shard_map/attend/pallas_call | solution.py:27
  127.6 2.6 collective-permute-start.30
  130.4 9.9 %collective-permute-done.29.refs_0_ = bf16[8,64,256]{2,1,0:T(8,128)(2,1)S(1)} collective-permute-done((bf16[8,64,256]{2,1,0:T(8,128)(2,1)}, bf16[8,64,256]{2,1,0:T(8,128)(2,1)S(1)}, u32[]{:S(2)}, u32[]{:S(2)}) %collective-permute-start.29) | collective-permute-done | bytes 262176 | tf_op jit(solution)/shard_map/ppermute | solution.py:105
  140.3 8.8 %collective-permute-done.30.refs_1_ = bf16[8,64,256]{2,1,0:T(8,128)(2,1)S(1)} collective-permute-done((bf16[8,64,256]{2,1,0:T(8,128)(2,1)}, bf16[8,64,256]{2,1,0:T(8,128)(2,1)S(1)}, u32[]{:S(2)}, u32[]{:S(2)}) %collective-permute-start.30) | collective-permute-done | bytes 262176 | tf_op jit(solution)/shard_map/ppermute | solution.py:105
  149.9 2.7 mid.1
  152.6 2.5 collective-permute-start.34
  155.1 4.4 collective-permute-start.33
  161.9 21.1 %copy.39 = bf16[6144,1408]{1,0:T(8,128)(2,1)} copy(bf16[6144,1408]{0,1:T(8,128)(2,1)} %all-gather.3.cloned.1.call-done) | data formatting | bytes 34603008 | tf_op jit(solution)/shard_map/all_gather | solution.py:467
  183.9 14.0 %ffn.1 = (bf16[256,1408]{1,0:T(8,128)(2,1)}, bf16[256,1408]{1,0:T(8,128)(2,1)}, bf16[256,1408]{1,0:T(8,128)(2,1)}) custom-call(bf16[8,64,256]{2,1,0:T(8,128)(2,1)} %get-tuple-element.87.refs_0_, bf16[8,64,256]{2,1,0:T(8,128)(2,1)} %copy-done.15, bf16[8,64,256]{2,1,0:T(8,128)(2,1)} %copy-done.14, bf16[8,64,256]{2,1,0:T(8,128)(2,1)} %copy-done.13, ...), custom_call_target="tpu_custom_call" | custom-call | flops 4429185024 | bytes 17301504 | tf_op jit(solution)/shard_map/ffn/pallas_call | solution.py:530
  197.9 11.8 %ffn_weights.1 = bf16[8,768,1408]{2,1,0:T(8,128)(2,1)} custom-call(bf16[8,64,256]{2,1,0:T(8,128)(2,1)} %get-tuple-element.87.refs_0_, bf16[8,64,256]{2,1,0:T(8,128)(2,1)} %copy-done.15, bf16[8,64,256]{2,1,0:T(8,128)(2,1)} %copy-done.14, bf16[8,64,256]{2,1,0:T(8,128)(2,1)} %copy-done.13, bf16[8,256,256]{2,1,0:T(8,128)(2,1)} %cotangent_rows.1.refs_4_, ...), custom_call_target="tpu_custom_call" | custom-call | flops 4429185024 | bytes 17301504 | tf_op jit(solution)/shard_map/ffn_weights/pallas_call | solution.py:556
  209.7 9.9 %two_grad.1 = (f32[8,64,256]{2,1,0:T(8,128)}, bf16[8,64,256]{2,1,0:T(8,128)(2,1)}, bf16[8,64,256]{2,1,0:T(8,128)(2,1)}, bf16[8,64,256]{2,1,0:T(8,128)(2,1)}) custom-call(bf16[256,1408]{1,0:T(8,128)(2,1)} %get-tuple-element.93.gate_grad_ref.refs_6_, bf16[256,1408]{1,0:T(8,128)(2,1)} %get-tuple-element.94.up_grad_ref.refs_7_, bf16[8,768,1408]{2,1,0:T(8,128)(2,1)} %bitcast.38), custom_call_target="tpu_custom_call" | custom-call | flops 2952790016 | bytes 11534336 | tf_op jit(solution)/shard_map/two_grad/pallas_call | solution.py:543
  224.2 8.4 %down.1 = (f32[8,64,256]{2,1,0:T(8,128)}, bf16[8,64,256]{2,1,0:T(8,128)(2,1)}, bf16[8,64,256]{2,1,0:T(8,128)(2,1)}, bf16[8,64,256]{2,1,0:T(8,128)(2,1)}) custom-call(bf16[256,1408]{1,0:T(8,128)(2,1)} %get-tuple-element.88.hidden_ref.refs_5_, bf16[8,768,1408]{2,1,0:T(8,128)(2,1)} %bitcast.39), custom_call_target="tpu_custom_call" | custom-call | flops 1476395008 | bytes 5767168 | tf_op jit(solution)/shard_map/down/pallas_call | solution.py:569
  235.2 2.3 collective-permute-start.36
  238.7 4.6 collective-permute-done.42.refs_1_
  244.1 3.0 mid_back.1
  247.1 2.5 collective-permute-start.46
  249.6 24.9 %collective-permute-start.45 = (bf16[8,64,256]{2,1,0:T(8,128)(2,1)}, bf16[8,64,256]{2,1,0:T(8,128)(2,1)S(1)}, u32[]{:S(2)}, u32[]{:S(2)}) collective-permute-start(bf16[8,64,256]{2,1,0:T(8,128)(2,1)} %get-tuple-element.101.refs_0_), channel_id=1, source_target_pairs={{0,2},{1,3},{2,0},{3,1},{4,6},{5,7},{6,4},{7,5},{8,10},{9,11},{10,... | collective-permute-start | bytes 786440 | tf_op jit(solution)/shard_map/ppermute | solution.py:105
  277.7 2.4 collective-permute-start.40
  280.1 12.2 %collective-permute-start.39 = (bf16[8,64,256]{2,1,0:T(8,128)(2,1)}, bf16[8,64,256]{2,1,0:T(8,128)(2,1)S(1)}, u32[]{:S(2)}, u32[]{:S(2)}) collective-permute-start(bf16[8,64,256]{2,1,0:T(8,128)(2,1)} %block_out.1.refs_0_), channel_id=1, source_target_pairs={{0,2},{1,3},{2,0},{3,1},{4,6},{5,7},{6,4},{7,5},{8,10},{9,11},{10,... | collective-permute-start | bytes 786440 | tf_op jit(solution)/shard_map/ppermute | solution.py:105
  292.3 4.9 %collective-permute-start.38 = (bf16[8,64,256]{2,1,0:T(8,128)(2,1)}, bf16[8,64,256]{2,1,0:T(8,128)(2,1)S(1)}, u32[]{:S(2)}, u32[]{:S(2)}) collective-permute-start(bf16[8,64,256]{2,1,0:T(8,128)(2,1)} %block_out.1.refs_0_), channel_id=1, source_target_pairs={{0,1},{1,0},{2,3},{3,2},{4,5},{5,4},{6,7},{7,6},{8,9},{9,8},{10,11... | collective-permute-start | bytes 786440 | tf_op jit(solution)/shard_map/ppermute | solution.py:105
  297.3 7.8 %collective-permute-done.45.refs_2_ = bf16[8,64,256]{2,1,0:T(8,128)(2,1)S(1)} collective-permute-done((bf16[8,64,256]{2,1,0:T(8,128)(2,1)}, bf16[8,64,256]{2,1,0:T(8,128)(2,1)S(1)}, u32[]{:S(2)}, u32[]{:S(2)}) %collective-permute-start.45) | collective-permute-done | bytes 262176 | tf_op jit(solution)/shard_map/ppermute | solution.py:105
  305.9 9.7 %attend_back.1 = (bf16[8,256,256]{2,1,0:T(8,128)(2,1)}, bf16[256,512]{1,0:T(8,128)(2,1)}, f32[2,256,512]{2,1,0:T(8,128)}, bf16[2,256,512]{2,1,0:T(8,128)(2,1)}) custom-call(s32[8]{0:T(128)} %iota_xor_fusion.order_ref, s32[4]{0:T(128)} %iota_xor_fusion.1.at_ref, f32[256,512]{1,0:T(8,128)} %and_select_fusion.hide_ref, ...), custom_call_target="tpu_custom_call" | custom-call | flops 1207959552 | bytes 2097152 | tf_op jit(solution)/shard_map/attend_back/pallas_call | solution.py:27
  315.6 3.1 out_weights.1
  328.6 4.2 collective-permute-done.82
  332.8 3.0 collective-permute-start.89
  337.3 4.8 %collective-permute-done.89 = bf16[256,256]{1,0:T(8,128)(2,1)S(1)} collective-permute-done((bf16[256,256]{1,0:T(8,128)(2,1)S(1)}, bf16[256,256]{1,0:T(8,128)(2,1)S(1)}, u32[]{:S(2)}, u32[]{:S(2)}) %collective-permute-start.89) | collective-permute-done | bytes 131104 | tf_op jit(solution)/shard_map/ppermute | solution.py:61
  345.7 2.7 collective-permute-done.83
  349.3 7.6 %one_grad.1 = (bf16[3,256,512]{2,1,0:T(8,128)(2,1)}, f32[3,1,512]{2,1,0:T(1,128)}, f32[8,1,256]{2,1,0:T(1,128)}, f32[8,1,256]{2,1,0:T(1,128)}, f32[8,64,256]{2,1...) custom-call(s32[8]{0:T(128)} %iota_xor_fusion.order_ref, ...), custom_call_target="tpu_custom_call" | custom-call | flops 1610612736 | bytes 6291456 | tf_op jit(solution)/shard_map/one_grad/pallas_call | solution.py:27
  369.0 2.9 collective-permute-start.59
  373.4 5.5 %qkv_weights.1 = (bf16[3,256,256]{2,1,0:T(8,128)(2,1)}, bf16[3,256,256]{2,1,0:T(8,128)(2,1)}, bf16[3,256,256]{2,1,0:T(8,128)(2,1)}, bf16[3,256,256]{2,1,0:T(8,12...) custom-call(s32[8]{0:T(128)} %iota_xor_fusion.order_ref, ...), custom_call_target="tpu_custom_call" | custom-call | flops 1610612736 | bytes 6291456 | tf_op jit(solution)/shard_map/qkv_weights/pallas_call | solution.py:27
  383.2 14.6 %collective-permute-done.49.refs_1_ = bf16[8,64,256]{2,1,0:T(8,128)(2,1)S(1)} collective-permute-done((bf16[8,64,256]{2,1,0:T(8,128)(2,1)S(1)}, bf16[8,64,256]{2,1,0:T(8,128)(2,1)S(1)}, u32[]{:S(2)}, u32[]{:S(2)}) %collective-permute-start.49) | collective-permute-done | bytes 262176 | tf_op jit(solution)/shard_map/ppermute | solution.py:105
  398.7 3.0 input_grad.1.refs_0_
  407.0 7.9 %collective-permute-done.65 = bf16[3,256,256]{2,1,0:T(8,128)(2,1)S(1)} collective-permute-done((bf16[3,256,256]{2,1,0:T(8,128)(2,1)S(1)}, bf16[3,256,256]{2,1,0:T(8,128)(2,1)S(1)}, u32[]{:S(2)}, u32[]{:S(2)}) %collective-permute-start.65) | collective-permute-done | bytes 393248 | tf_op jit(solution)/shard_map/ppermute | solution.py:64
  415.0 2.5 collective-permute-start.53
  417.7 4.7 %collective-permute-start.52 = (bf16[8,64,256]{2,1,0:T(8,128)(2,1)S(1)}, bf16[8,64,256]{2,1,0:T(8,128)(2,1)S(1)}, u32[]{:S(2)}, u32[]{:S(2)}) collective-permute-start(bf16[8,64,256]{2,1,0:T(8,128)(2,1)S(1)} %copy-done.16), channel_id=1, source_target_pairs={{0,2},{1,3},{2,0},{3,1},{4,6},{5,7},{6,4},{7,5},{8,10},{9,11},{10,... | collective-permute-start | bytes 786440 | tf_op jit(solution)/shard_map/ppermute | solution.py:105
  426.3 15.1 %collective-permute-done.52.refs_2_ = bf16[8,64,256]{2,1,0:T(8,128)(2,1)S(1)} collective-permute-done((bf16[8,64,256]{2,1,0:T(8,128)(2,1)S(1)}, bf16[8,64,256]{2,1,0:T(8,128)(2,1)S(1)}, u32[]{:S(2)}, u32[]{:S(2)}) %collective-permute-start.52) | collective-permute-done | bytes 262176 | tf_op jit(solution)/shard_map/ppermute | solution.py:105
  447.4 5.0 %collective-permute-done.66 = bf16[3,256,256]{2,1,0:T(8,128)(2,1)S(1)} collective-permute-done((bf16[3,256,256]{2,1,0:T(8,128)(2,1)S(1)}, bf16[3,256,256]{2,1,0:T(8,128)(2,1)S(1)}, u32[]{:S(2)}, u32[]{:S(2)}) %collective-permute-start.66) | collective-permute-done | bytes 393248 | tf_op jit(solution)/shard_map/ppermute | solution.py:61
  (392 shorter events, 110.5 us)
Async XLA Ops:
  7.2 154.7 %all-gather.3.cloned.1.call-start = ((), (), s32[]{:S(2)}) async-start(), calls=%async_computation.2 | async-start | bytes 19464192 | tf_op jit(solution)/shard_map/all_gather | solution.py:467
  11.3 444.0 %reduce-scatter.2.cloned.1.call-start = ((), (), s32[]{:S(2)}) async-start(), calls=%async_computation.1 | async-start | bytes 19464192 | tf_op jit(solution)/shard_map/reduce_scatter | solution.py:568
  12.5 19.2 %collective-permute-start.10 = (bf16[3,256,256]{2,1,0:T(8,128)(2,1)S(1)}, bf16[3,256,256]{2,1,0:T(8,128)(2,1)S(1)}, u32[]{:S(2)}, u32[]{:S(2)}) collective-permute-start(bf16[3,256,256]{2,1,0:T(8,128)(2,1)S(1)} %get-tuple-element.184.refs_8_), channel_id=1, source_target_pairs={{0,16},{8,24},{16,0},{24,8},{1,17},{9,25},{17,1},{25,9},{2,18},{10... | collective-permute-start | bytes 1179656 | tf_op jit(solution)/shard_map/ppermute | solution.py:64
  15.5 17.8 %collective-permute-start.8 = (bf16[3,256,256]{2,1,0:T(8,128)(2,1)S(1)}, bf16[3,256,256]{2,1,0:T(8,128)(2,1)S(1)}, u32[]{:S(2)}, u32[]{:S(2)}) collective-permute-start(bf16[3,256,256]{2,1,0:T(8,128)(2,1)S(1)} %get-tuple-element.184.refs_8_), channel_id=1, source_target_pairs={{0,8},{8,0},{16,24},{24,16},{1,9},{9,1},{17,25},{25,17},{2,10},{10... | collective-permute-start | bytes 1179656 | tf_op jit(solution)/shard_map/ppermute | solution.py:64
  15.5 17.9 %collective-permute-start.7 = (bf16[3,256,256]{2,1,0:T(8,128)(2,1)S(1)}, bf16[3,256,256]{2,1,0:T(8,128)(2,1)S(1)}, u32[]{:S(2)}, u32[]{:S(2)}) collective-permute-start(bf16[3,256,256]{2,1,0:T(8,128)(2,1)S(1)} %get-tuple-element.184.refs_8_), channel_id=1, source_target_pairs={{0,4},{4,0},{1,5},{5,1},{2,6},{6,2},{3,7},{7,3},{8,12},{12,8},{9,1... | collective-permute-start | bytes 1179656 | tf_op jit(solution)/shard_map/ppermute | solution.py:61
  18.2 30.3 %collective-permute-start.3 = (bf16[3,256,256]{2,1,0:T(8,128)(2,1)S(1)}, bf16[3,256,256]{2,1,0:T(8,128)(2,1)S(1)}, u32[]{:S(2)}, u32[]{:S(2)}) collective-permute-start(bf16[3,256,256]{2,1,0:T(8,128)(2,1)S(1)} %get-tuple-element.185.refs_0_), channel_id=1, source_target_pairs={{0,16},{8,24},{16,0},{24,8},{1,17},{9,25},{17,1},{25,9},{2,18},{10... | collective-permute-start | bytes 1179656 | tf_op jit(solution)/shard_map/ppermute | solution.py:64
  31.7 22.5 %collective-permute-start.1 = (bf16[3,256,256]{2,1,0:T(8,128)(2,1)S(1)}, bf16[3,256,256]{2,1,0:T(8,128)(2,1)S(1)}, u32[]{:S(2)}, u32[]{:S(2)}) collective-permute-start(bf16[3,256,256]{2,1,0:T(8,128)(2,1)S(1)} %get-tuple-element.185.refs_0_), channel_id=1, source_target_pairs={{0,8},{8,0},{16,24},{24,16},{1,9},{9,1},{17,25},{25,17},{2,10},{10... | collective-permute-start | bytes 1179656 | tf_op jit(solution)/shard_map/ppermute | solution.py:64
  31.7 22.5 %collective-permute-start = (bf16[3,256,256]{2,1,0:T(8,128)(2,1)S(1)}, bf16[3,256,256]{2,1,0:T(8,128)(2,1)S(1)}, u32[]{:S(2)}, u32[]{:S(2)}) collective-permute-start(bf16[3,256,256]{2,1,0:T(8,128)(2,1)S(1)} %get-tuple-element.185.refs_0_), channel_id=1, source_target_pairs={{0,4},{4,0},{1,5},{5,1},{2,6},{6,2},{3,7},{7,3},{8,12},{12,8},{9,1... | collective-permute-start | bytes 1179656 | tf_op jit(solution)/shard_map/ppermute | solution.py:61
  33.2 21.5 %collective-permute-start.12 = (bf16[3,256,256]{2,1,0:T(8,128)(2,1)S(1)}, bf16[3,256,256]{2,1,0:T(8,128)(2,1)S(1)}, u32[]{:S(2)}, u32[]{:S(2)}) collective-permute-start(bf16[3,256,256]{2,1,0:T(8,128)(2,1)S(1)} %collective-permute-done.10.refs_12_), channel_id=1, source_target_pairs={{0,8},{8,0},{16,24},{24,16},{1,9},{9,1},{17,25},{25,17},{2,10},{10... | collective-permute-start | bytes 1179656 | tf_op jit(solution)/shard_map/ppermute | solution.py:64
  33.4 30.8 %collective-permute-start.11 = (bf16[3,256,256]{2,1,0:T(8,128)(2,1)S(1)}, bf16[3,256,256]{2,1,0:T(8,128)(2,1)}, u32[]{:S(2)}, u32[]{:S(2)}) collective-permute-start(bf16[3,256,256]{2,1,0:T(8,128)(2,1)S(1)} %collective-permute-done.7.refs_9_), channel_id=1, source_target_pairs={{0,16},{8,24},{16,0},{24,8},{1,17},{9,25},{17,1},{25,9},{2,18},{10... | collective-permute-start | bytes 1179656 | tf_op jit(solution)/shard_map/ppermute | solution.py:64
  48.5 18.6 %collective-permute-start.4 = (bf16[3,256,256]{2,1,0:T(8,128)(2,1)S(1)}, bf16[3,256,256]{2,1,0:T(8,128)(2,1)}, u32[]{:S(2)}, u32[]{:S(2)}) collective-permute-start(bf16[3,256,256]{2,1,0:T(8,128)(2,1)S(1)} %collective-permute-done.3.refs_4_), channel_id=1, source_target_pairs={{0,4},{4,0},{1,5},{5,1},{2,6},{6,2},{3,7},{7,3},{8,12},{12,8},{9,1... | collective-permute-start | bytes 1179656 | tf_op jit(solution)/shard_map/ppermute | solution.py:61
  54.2 19.6 %collective-permute-start.9 = (bf16[3,256,256]{2,1,0:T(8,128)(2,1)S(1)}, bf16[3,256,256]{2,1,0:T(8,128)(2,1)}, u32[]{:S(2)}, u32[]{:S(2)}) collective-permute-start(bf16[3,256,256]{2,1,0:T(8,128)(2,1)S(1)} %collective-permute-done.7.refs_9_), channel_id=1, source_target_pairs={{0,8},{8,0},{16,24},{24,16},{1,9},{9,1},{17,25},{25,17},{2,10},{10... | collective-permute-start | bytes 1179656 | tf_op jit(solution)/shard_map/ppermute | solution.py:64
  54.2 20.2 %collective-permute-start.5 = (bf16[3,256,256]{2,1,0:T(8,128)(2,1)S(1)}, bf16[3,256,256]{2,1,0:T(8,128)(2,1)}, u32[]{:S(2)}, u32[]{:S(2)}) collective-permute-start(bf16[3,256,256]{2,1,0:T(8,128)(2,1)S(1)} %collective-permute-done.3.refs_4_), channel_id=1, source_target_pairs={{0,8},{8,0},{16,24},{24,16},{1,9},{9,1},{17,25},{25,17},{2,10},{10... | collective-permute-start | bytes 1179656 | tf_op jit(solution)/shard_map/ppermute | solution.py:64
  54.7 21.2 %collective-permute-start.2 = (bf16[3,256,256]{2,1,0:T(8,128)(2,1)S(1)}, bf16[3,256,256]{2,1,0:T(8,128)(2,1)}, u32[]{:S(2)}, u32[]{:S(2)}) collective-permute-start(bf16[3,256,256]{2,1,0:T(8,128)(2,1)S(1)} %collective-permute-done.refs_1_), channel_id=1, source_target_pairs={{0,8},{8,0},{16,24},{24,16},{1,9},{9,1},{17,25},{25,17},{2,10},{10... | collective-permute-start | bytes 1179656 | tf_op jit(solution)/shard_map/ppermute | solution.py:64
  83.5 34.1 %collective-permute-start.14 = (bf16[2,256,512]{2,1,0:T(8,128)(2,1)}, bf16[2,256,512]{2,1,0:T(8,128)(2,1)S(1)}, u32[]{:S(2)}, u32[]{:S(2)}) collective-permute-start(bf16[2,256,512]{2,1,0:T(8,128)(2,1)} %get-tuple-element.81.here_ref), channel_id=1, source_target_pairs={{0,4},{1,5},{2,6},{3,7},{8,12},{9,13},{10,14},{11,15},{16,20},{17,... | collective-permute-start | bytes 1572872 | tf_op jit(solution)/shard_map/ppermute | solution.py:507
  89.7 26.4 %collective-permute-start.19 = (bf16[256,256]{1,0:T(8,128)(2,1)}, bf16[256,256]{1,0:T(8,128)(2,1)S(1)}, u32[]{:S(2)}, u32[]{:S(2)}) collective-permute-start(bf16[256,256]{1,0:T(8,128)(2,1)} %collective-permute-done.18.refs_4_.refs_8_), channel_id=1, source_target_pairs={{0,4},{4,0},{1,5},{5,1},{2,6},{6,2},{3,7},{7,3},{8,12},{12,8},{9,1... | collective-permute-start | bytes 393224 | tf_op jit(solution)/shard_map/ppermute | solution.py:61
  91.3 26.3 %collective-permute-start.20 = (bf16[256,256]{1,0:T(8,128)(2,1)}, bf16[256,256]{1,0:T(8,128)(2,1)S(1)}, u32[]{:S(2)}, u32[]{:S(2)}) collective-permute-start(bf16[256,256]{1,0:T(8,128)(2,1)} %collective-permute-done.18.refs_4_.refs_8_), channel_id=1, source_target_pairs={{0,8},{8,0},{16,24},{24,16},{1,9},{9,1},{17,25},{25,17},{2,10},{10... | collective-permute-start | bytes 393224 | tf_op jit(solution)/shard_map/ppermute | solution.py:64
  95.9 21.7 %collective-permute-start.17 = (bf16[256,256]{1,0:T(8,128)(2,1)}, bf16[256,256]{1,0:T(8,128)(2,1)S(1)}, u32[]{:S(2)}, u32[]{:S(2)}) collective-permute-start(bf16[256,256]{1,0:T(8,128)(2,1)} %copy-done.23), channel_id=1, source_target_pairs={{0,8},{8,0},{16,24},{24,16},{1,9},{9,1},{17,25},{25,17},{2,10},{10... | collective-permute-start | bytes 393224 | tf_op jit(solution)/shard_map/ppermute | solution.py:64
  95.9 21.7 %collective-permute-start.28 = (bf16[256,256]{1,0:T(8,128)(2,1)S(1)}, bf16[256,256]{1,0:T(8,128)(2,1)S(1)}, u32[]{:S(2)}, u32[]{:S(2)}) collective-permute-start(bf16[256,256]{1,0:T(8,128)(2,1)S(1)} %collective-permute-done.26.refs_13_.refs_17_), channel_id=1, source_target_pairs={{0,8},{8,0},{16,24},{24,16},{1,9},{9,1},{17,25},{25,17},{2,10},{10... | collective-permute-start | bytes 393224 | tf_op jit(solution)/shard_map/ppermute | solution.py:64
  127.6 21.5 %collective-permute-start.30 = (bf16[8,64,256]{2,1,0:T(8,128)(2,1)}, bf16[8,64,256]{2,1,0:T(8,128)(2,1)S(1)}, u32[]{:S(2)}, u32[]{:S(2)}) collective-permute-start(bf16[8,64,256]{2,1,0:T(8,128)(2,1)} %get-tuple-element.84), channel_id=1, source_target_pairs={{0,2},{1,3},{2,0},{3,1},{4,6},{5,7},{6,4},{7,5},{8,10},{9,11},{10,... | collective-permute-start | bytes 786440 | tf_op jit(solution)/shard_map/ppermute | solution.py:105
  130.2 18.9 %collective-permute-start.31 = (bf16[8,64,256]{2,1,0:T(8,128)(2,1)}, bf16[8,64,256]{2,1,0:T(8,128)(2,1)S(1)}, u32[]{:S(2)}, u32[]{:S(2)}) collective-permute-start(bf16[8,64,256]{2,1,0:T(8,128)(2,1)} %get-tuple-element.85), channel_id=1, source_target_pairs={{0,3},{1,2},{2,1},{3,0},{4,7},{5,6},{6,5},{7,4},{8,11},{9,10},{10,... | collective-permute-start | bytes 786440 | tf_op jit(solution)/shard_map/ppermute | solution.py:105
  152.6 30.4 %collective-permute-start.34 = (bf16[8,64,256]{2,1,0:T(8,128)(2,1)}, bf16[8,64,256]{2,1,0:T(8,128)(2,1)S(1)}, u32[]{:S(2)}, u32[]{:S(2)}) collective-permute-start(bf16[8,64,256]{2,1,0:T(8,128)(2,1)} %get-tuple-element.87.refs_0_), channel_id=1, source_target_pairs={{0,3},{1,2},{2,1},{3,0},{4,7},{5,6},{6,5},{7,4},{8,11},{9,10},{10,... | collective-permute-start | bytes 786440 | tf_op jit(solution)/shard_map/ppermute | solution.py:105
  155.1 27.9 %collective-permute-start.33 = (bf16[8,64,256]{2,1,0:T(8,128)(2,1)}, bf16[8,64,256]{2,1,0:T(8,128)(2,1)S(1)}, u32[]{:S(2)}, u32[]{:S(2)}) collective-permute-start(bf16[8,64,256]{2,1,0:T(8,128)(2,1)} %get-tuple-element.87.refs_0_), channel_id=1, source_target_pairs={{0,2},{1,3},{2,0},{3,1},{4,6},{5,7},{6,4},{7,5},{8,10},{9,11},{10,... | collective-permute-start | bytes 786440 | tf_op jit(solution)/shard_map/ppermute | solution.py:105
  159.5 23.5 %collective-permute-start.32 = (bf16[8,64,256]{2,1,0:T(8,128)(2,1)}, bf16[8,64,256]{2,1,0:T(8,128)(2,1)S(1)}, u32[]{:S(2)}, u32[]{:S(2)}) collective-permute-start(bf16[8,64,256]{2,1,0:T(8,128)(2,1)} %get-tuple-element.87.refs_0_), channel_id=1, source_target_pairs={{0,1},{1,0},{2,3},{3,2},{4,5},{5,4},{6,7},{7,6},{8,9},{9,8},{10,11... | collective-permute-start | bytes 786440 | tf_op jit(solution)/shard_map/ppermute | solution.py:105
  219.7 17.9 %collective-permute-start.41 = (bf16[8,64,256]{2,1,0:T(8,128)(2,1)}, bf16[8,64,256]{2,1,0:T(8,128)(2,1)S(1)}, u32[]{:S(2)}, u32[]{:S(2)}) collective-permute-start(bf16[8,64,256]{2,1,0:T(8,128)(2,1)} %get-tuple-element.96), channel_id=1, source_target_pairs={{0,1},{1,0},{2,3},{3,2},{4,5},{5,4},{6,7},{7,6},{8,9},{9,8},{10,11... | collective-permute-start | bytes 786440 | tf_op jit(solution)/shard_map/ppermute | solution.py:105
  221.6 21.6 %collective-permute-start.42 = (bf16[8,64,256]{2,1,0:T(8,128)(2,1)}, bf16[8,64,256]{2,1,0:T(8,128)(2,1)S(1)}, u32[]{:S(2)}, u32[]{:S(2)}) collective-permute-start(bf16[8,64,256]{2,1,0:T(8,128)(2,1)} %get-tuple-element.97), channel_id=1, source_target_pairs={{0,2},{1,3},{2,0},{3,1},{4,6},{5,7},{6,4},{7,5},{8,10},{9,11},{10,... | collective-permute-start | bytes 786440 | tf_op jit(solution)/shard_map/ppermute | solution.py:105
  223.1 20.2 %collective-permute-start.43 = (bf16[8,64,256]{2,1,0:T(8,128)(2,1)}, bf16[8,64,256]{2,1,0:T(8,128)(2,1)S(1)}, u32[]{:S(2)}, u32[]{:S(2)}) collective-permute-start(bf16[8,64,256]{2,1,0:T(8,128)(2,1)} %get-tuple-element.98), channel_id=1, source_target_pairs={{0,3},{1,2},{2,1},{3,0},{4,7},{5,6},{6,5},{7,4},{8,11},{9,10},{10,... | collective-permute-start | bytes 786440 | tf_op jit(solution)/shard_map/ppermute | solution.py:105
  232.6 41.9 %collective-permute-start.35 = (bf16[8,64,256]{2,1,0:T(8,128)(2,1)}, bf16[8,64,256]{2,1,0:T(8,128)(2,1)S(1)}, u32[]{:S(2)}, u32[]{:S(2)}) collective-permute-start(bf16[8,64,256]{2,1,0:T(8,128)(2,1)} %get-tuple-element.90), channel_id=1, source_target_pairs={{0,1},{1,0},{2,3},{3,2},{4,5},{5,4},{6,7},{7,6},{8,9},{9,8},{10,11... | collective-permute-start | bytes 786440 | tf_op jit(solution)/shard_map/ppermute | solution.py:105
  235.2 39.4 %collective-permute-start.36 = (bf16[8,64,256]{2,1,0:T(8,128)(2,1)}, bf16[8,64,256]{2,1,0:T(8,128)(2,1)S(1)}, u32[]{:S(2)}, u32[]{:S(2)}) collective-permute-start(bf16[8,64,256]{2,1,0:T(8,128)(2,1)} %get-tuple-element.91), channel_id=1, source_target_pairs={{0,2},{1,3},{2,0},{3,1},{4,6},{5,7},{6,4},{7,5},{8,10},{9,11},{10,... | collective-permute-start | bytes 786440 | tf_op jit(solution)/shard_map/ppermute | solution.py:105
  237.6 37.1 %collective-permute-start.37 = (bf16[8,64,256]{2,1,0:T(8,128)(2,1)}, bf16[8,64,256]{2,1,0:T(8,128)(2,1)S(1)}, u32[]{:S(2)}, u32[]{:S(2)}) collective-permute-start(bf16[8,64,256]{2,1,0:T(8,128)(2,1)} %get-tuple-element.92), channel_id=1, source_target_pairs={{0,3},{1,2},{2,1},{3,0},{4,7},{5,6},{6,5},{7,4},{8,11},{9,10},{10,... | collective-permute-start | bytes 786440 | tf_op jit(solution)/shard_map/ppermute | solution.py:105
  247.1 45.2 %collective-permute-start.46 = (bf16[8,64,256]{2,1,0:T(8,128)(2,1)}, bf16[8,64,256]{2,1,0:T(8,128)(2,1)S(1)}, u32[]{:S(2)}, u32[]{:S(2)}) collective-permute-start(bf16[8,64,256]{2,1,0:T(8,128)(2,1)} %get-tuple-element.101.refs_0_), channel_id=1, source_target_pairs={{0,3},{1,2},{2,1},{3,0},{4,7},{5,6},{6,5},{7,4},{8,11},{9,10},{10,... | collective-permute-start | bytes 786440 | tf_op jit(solution)/shard_map/ppermute | solution.py:105
  249.6 55.5 %collective-permute-start.45 = (bf16[8,64,256]{2,1,0:T(8,128)(2,1)}, bf16[8,64,256]{2,1,0:T(8,128)(2,1)S(1)}, u32[]{:S(2)}, u32[]{:S(2)}) collective-permute-start(bf16[8,64,256]{2,1,0:T(8,128)(2,1)} %get-tuple-element.101.refs_0_), channel_id=1, source_target_pairs={{0,2},{1,3},{2,0},{3,1},{4,6},{5,7},{6,4},{7,5},{8,10},{9,11},{10,... | collective-permute-start | bytes 786440 | tf_op jit(solution)/shard_map/ppermute | solution.py:105
  274.5 30.6 %collective-permute-start.44 = (bf16[8,64,256]{2,1,0:T(8,128)(2,1)}, bf16[8,64,256]{2,1,0:T(8,128)(2,1)S(1)}, u32[]{:S(2)}, u32[]{:S(2)}) collective-permute-start(bf16[8,64,256]{2,1,0:T(8,128)(2,1)} %get-tuple-element.101.refs_0_), channel_id=1, source_target_pairs={{0,1},{1,0},{2,3},{3,2},{4,5},{5,4},{6,7},{7,6},{8,9},{9,8},{10,11... | collective-permute-start | bytes 786440 | tf_op jit(solution)/shard_map/ppermute | solution.py:105
  277.7 42.8 %collective-permute-start.40 = (bf16[8,64,256]{2,1,0:T(8,128)(2,1)}, bf16[8,64,256]{2,1,0:T(8,128)(2,1)S(1)}, u32[]{:S(2)}, u32[]{:S(2)}) collective-permute-start(bf16[8,64,256]{2,1,0:T(8,128)(2,1)} %block_out.1.refs_0_), channel_id=1, source_target_pairs={{0,3},{1,2},{2,1},{3,0},{4,7},{5,6},{6,5},{7,4},{8,11},{9,10},{10,... | collective-permute-start | bytes 786440 | tf_op jit(solution)/shard_map/ppermute | solution.py:105
  280.1 40.8 %collective-permute-start.39 = (bf16[8,64,256]{2,1,0:T(8,128)(2,1)}, bf16[8,64,256]{2,1,0:T(8,128)(2,1)S(1)}, u32[]{:S(2)}, u32[]{:S(2)}) collective-permute-start(bf16[8,64,256]{2,1,0:T(8,128)(2,1)} %block_out.1.refs_0_), channel_id=1, source_target_pairs={{0,2},{1,3},{2,0},{3,1},{4,6},{5,7},{6,4},{7,5},{8,10},{9,11},{10,... | collective-permute-start | bytes 786440 | tf_op jit(solution)/shard_map/ppermute | solution.py:105
  292.3 28.7 %collective-permute-start.38 = (bf16[8,64,256]{2,1,0:T(8,128)(2,1)}, bf16[8,64,256]{2,1,0:T(8,128)(2,1)S(1)}, u32[]{:S(2)}, u32[]{:S(2)}) collective-permute-start(bf16[8,64,256]{2,1,0:T(8,128)(2,1)} %block_out.1.refs_0_), channel_id=1, source_target_pairs={{0,1},{1,0},{2,3},{3,2},{4,5},{5,4},{6,7},{7,6},{8,9},{9,8},{10,11... | collective-permute-start | bytes 786440 | tf_op jit(solution)/shard_map/ppermute | solution.py:105
  318.8 29.7 %collective-permute-start.47 = (bf16[2,256,512]{2,1,0:T(8,128)(2,1)}, bf16[2,256,512]{2,1,0:T(8,128)(2,1)S(1)}, u32[]{:S(2)}, u32[]{:S(2)}) collective-permute-start(bf16[2,256,512]{2,1,0:T(8,128)(2,1)} %get-tuple-element.104), channel_id=1, source_target_pairs={{4,0},{5,1},{6,2},{7,3},{12,8},{13,9},{14,10},{15,11},{20,16},{21,... | collective-permute-start | bytes 1572872 | tf_op jit(solution)/shard_map/ppermute | solution.py:609
  320.5 21.7 %collective-permute-start.77 = (bf16[256,256]{1,0:T(8,128)(2,1)}, bf16[256,256]{1,0:T(8,128)(2,1)S(1)}, u32[]{:S(2)}, u32[]{:S(2)}) collective-permute-start(bf16[256,256]{1,0:T(8,128)(2,1)} %get-tuple-element.134), channel_id=1, source_target_pairs={{0,8},{8,0},{16,24},{24,16},{1,9},{9,1},{17,25},{25,17},{2,10},{10... | collective-permute-start | bytes 393224 | tf_op jit(solution)/shard_map/ppermute | solution.py:64
  324.0 33.8 %collective-permute-start.84 = (bf16[256,256]{1,0:T(8,128)(2,1)}, bf16[256,256]{1,0:T(8,128)(2,1)S(1)}, u32[]{:S(2)}, u32[]{:S(2)}) collective-permute-start(bf16[256,256]{1,0:T(8,128)(2,1)} %get-tuple-element.142), channel_id=1, source_target_pairs={{0,8},{8,0},{16,24},{24,16},{1,9},{9,1},{17,25},{25,17},{2,10},{10... | collective-permute-start | bytes 393224 | tf_op jit(solution)/shard_map/ppermute | solution.py:64
  379.0 18.9 %collective-permute-start.49 = (bf16[8,64,256]{2,1,0:T(8,128)(2,1)S(1)}, bf16[8,64,256]{2,1,0:T(8,128)(2,1)S(1)}, u32[]{:S(2)}, u32[]{:S(2)}) collective-permute-start(bf16[8,64,256]{2,1,0:T(8,128)(2,1)S(1)} %copy-done.82), channel_id=1, source_target_pairs={{0,2},{1,3},{2,0},{3,1},{4,6},{5,7},{6,4},{7,5},{8,10},{9,11},{10,... | collective-permute-start | bytes 786440 | tf_op jit(solution)/shard_map/ppermute | solution.py:105
  382.5 19.2 %collective-permute-start.61 = (bf16[3,256,256]{2,1,0:T(8,128)(2,1)}, bf16[3,256,256]{2,1,0:T(8,128)(2,1)S(1)}, u32[]{:S(2)}, u32[]{:S(2)}) collective-permute-start(bf16[3,256,256]{2,1,0:T(8,128)(2,1)} %get-tuple-element.117), channel_id=1, source_target_pairs={{0,8},{8,0},{16,24},{24,16},{1,9},{9,1},{17,25},{25,17},{2,10},{10... | collective-permute-start | bytes 1179656 | tf_op jit(solution)/shard_map/ppermute | solution.py:64
  382.5 19.8 %collective-permute-start.64 = (bf16[3,256,256]{2,1,0:T(8,128)(2,1)}, bf16[3,256,256]{2,1,0:T(8,128)(2,1)S(1)}, u32[]{:S(2)}, u32[]{:S(2)}) collective-permute-start(bf16[3,256,256]{2,1,0:T(8,128)(2,1)} %get-tuple-element.121), channel_id=1, source_target_pairs={{0,8},{8,0},{16,24},{24,16},{1,9},{9,1},{17,25},{25,17},{2,10},{10... | collective-permute-start | bytes 1179656 | tf_op jit(solution)/shard_map/ppermute | solution.py:64
  383.1 39.7 %collective-permute-start.60 = (bf16[3,256,256]{2,1,0:T(8,128)(2,1)}, bf16[3,256,256]{2,1,0:T(8,128)(2,1)S(1)}, u32[]{:S(2)}, u32[]{:S(2)}) collective-permute-start(bf16[3,256,256]{2,1,0:T(8,128)(2,1)} %get-tuple-element.115), channel_id=1, source_target_pairs={{0,8},{8,0},{16,24},{24,16},{1,9},{9,1},{17,25},{25,17},{2,10},{10... | collective-permute-start | bytes 1179656 | tf_op jit(solution)/shard_map/ppermute | solution.py:64
  406.9 45.7 %collective-permute-start.67 = (bf16[3,256,256]{2,1,0:T(8,128)(2,1)S(1)}, bf16[3,256,256]{2,1,0:T(8,128)(2,1)S(1)}, u32[]{:S(2)}, u32[]{:S(2)}) collective-permute-start(bf16[3,256,256]{2,1,0:T(8,128)(2,1)S(1)} %copy-done.78), channel_id=1, source_target_pairs={{0,8},{8,0},{16,24},{24,16},{1,9},{9,1},{17,25},{25,17},{2,10},{10... | collective-permute-start | bytes 1179656 | tf_op jit(solution)/shard_map/ppermute | solution.py:64
  417.7 23.7 %collective-permute-start.52 = (bf16[8,64,256]{2,1,0:T(8,128)(2,1)S(1)}, bf16[8,64,256]{2,1,0:T(8,128)(2,1)S(1)}, u32[]{:S(2)}, u32[]{:S(2)}) collective-permute-start(bf16[8,64,256]{2,1,0:T(8,128)(2,1)S(1)} %copy-done.16), channel_id=1, source_target_pairs={{0,2},{1,3},{2,0},{3,1},{4,6},{5,7},{6,4},{7,5},{8,10},{9,11},{10,... | collective-permute-start | bytes 786440 | tf_op jit(solution)/shard_map/ppermute | solution.py:105
  422.4 20.6 %collective-permute-start.51 = (bf16[8,64,256]{2,1,0:T(8,128)(2,1)S(1)}, bf16[8,64,256]{2,1,0:T(8,128)(2,1)S(1)}, u32[]{:S(2)}, u32[]{:S(2)}) collective-permute-start(bf16[8,64,256]{2,1,0:T(8,128)(2,1)S(1)} %copy-done.16), channel_id=1, source_target_pairs={{0,1},{1,0},{2,3},{3,2},{4,5},{5,4},{6,7},{7,6},{8,9},{9,8},{10,11... | collective-permute-start | bytes 786440 | tf_op jit(solution)/shard_map/ppermute | solution.py:105
  422.8 24.6 %collective-permute-start.62 = (bf16[3,256,256]{2,1,0:T(8,128)(2,1)S(1)}, bf16[3,256,256]{2,1,0:T(8,128)(2,1)S(1)}, u32[]{:S(2)}, u32[]{:S(2)}) collective-permute-start(bf16[3,256,256]{2,1,0:T(8,128)(2,1)S(1)} %add_convert_fusion.10), channel_id=1, source_target_pairs={{0,16},{8,24},{16,0},{24,8},{1,17},{9,25},{17,1},{25,9},{2,18},{10... | collective-permute-start | bytes 1179656 | tf_op jit(solution)/shard_map/ppermute | solution.py:64
  424.7 27.9 %collective-permute-start.69 = (bf16[3,256,256]{2,1,0:T(8,128)(2,1)S(1)}, bf16[3,256,256]{2,1,0:T(8,128)(2,1)S(1)}, u32[]{:S(2)}, u32[]{:S(2)}) collective-permute-start(bf16[3,256,256]{2,1,0:T(8,128)(2,1)S(1)} %add_convert_fusion.4), channel_id=1, source_target_pairs={{0,4},{4,0},{1,5},{5,1},{2,6},{6,2},{3,7},{7,3},{8,12},{12,8},{9,1... | collective-permute-start | bytes 1179656 | tf_op jit(solution)/shard_map/ppermute | solution.py:61
  (133 other events, 1413.2 us)
Sparse Core Ops, SparseCore 0:
  11.4 129.1 all-gather.2
  209.9 123.2 reduce-scatter.1

commit v2 on v1

v2 whole, which is shorter than its diff:
```python
import functools
import math

import jax
import jax.numpy as jnp
from jax import lax
from jax.experimental import pallas as pl
from jax.experimental.pallas import tpu as pltpu
from jax.sharding import PartitionSpec as P

HD = 64
ROT = 16
EPS = 1e-05
NEG = -1e30
f32 = jnp.float32
bf16 = jnp.bfloat16
VM = pl.BlockSpec(memory_space=pltpu.VMEM)
SM = pl.BlockSpec(memory_space=pltpu.SMEM)
HB = pl.BlockSpec(memory_space=pl.ANY)
PLANE = ("fsdp", "context")


def shape(dims, dtype):
    return jax.ShapeDtypeStruct(tuple(dims), dtype)


WEIGHT = dict(qkv=10, mid=20, mid_back=60, attend_back=200, input_grad=20, input_grad_rows=20)


def params(name):
    return dict(
        name=name,
        compiler_params=pltpu.CompilerParams(vmem_limit_bytes=56 * 2**20),
        cost_estimate=pl.CostEstimate(
            flops=int(1.15e9 * WEIGHT.get(name, 0)), bytes_accessed=0, transcendentals=0
        ),
    )


def call(kernel, name, outs, args, specs, scratch=()):
    return pl.pallas_call(
        kernel,
        out_shape=outs,
        in_specs=specs,
        out_specs=jax.tree.map(lambda _: VM, outs),
        scratch_shapes=list(scratch),
        **params(name),
    )(*args)


def dot(a, b, dims=((1,), (0,))):
    return lax.dot_general(a, b, (dims, ((), ())), preferred_element_type=f32)


NT = ((1,), (1,))
TN = ((0,), (0,))


def tie(value, *others):
    return lax.optimization_barrier((value, others))[0]


class Plane:
    def __init__(self):
        self.fsdp = lax.axis_size("fsdp")
        self.context = lax.axis_size("context")
        self.count = self.fsdp * self.context
        self.me = lax.axis_index("fsdp") * self.context + lax.axis_index("context")
        self.core = self.context
        bits = [1 << i for i in range(int(math.log2(self.count))) if (1 << i) != self.core]
        self.up, self.down = bits, bits[::-1]
        self.kept = [k for k in range(self.count) if not k & self.core]
        self.sent = [k ^ self.core for k in self.kept]
        own = [[d for d in range(self.count) if d & self.core == c] for c in (0, self.core)]
        self.groups = own

    def rank(self, k):
        low = self.core - 1
        squeeze = lambda d: (d & low) | ((d >> 1) & ~low)
        return squeeze(self.me) ^ squeeze(k)

    def swap(self, value, bit):
        if bit < self.context:
            pairs = [(i, i ^ bit) for i in range(self.context)]
            return lax.ppermute(value, "context", pairs)
        step = bit // self.context
        pairs = [(i, i ^ step) for i in range(self.fsdp)]
        return lax.ppermute(value, "fsdp", pairs)

    def across(self, value):
        return jax.tree.map(lambda v: self.swap(v, self.core), value)

    def gather(self, shard, order, *after):
        slots = {0: shard}
        for bit in order + [self.core]:
            for k in list(slots):
                wait = after if k and bit != self.core else ()
                slots[k ^ bit] = self.swap(tie(slots[k], wait) if wait else slots[k], bit)
        return slots

    def gather_halves(self, shard, *prepared):
        if len(self.up) != 2:
            return {k: (v,) for k, v in self.gather(shard, self.up).items()}
        y, x = self.up
        half = shard.shape[-1] // 2
        over_x, over_y = self.swap(shard, x), self.swap(shard, y)
        first, second = tie((over_x[..., :half], over_y[..., half:]), prepared)
        both = (self.swap(first, y), self.swap(second, x))
        slots = {0: (shard,), x: (over_x,), y: (over_y,), x ^ y: both}
        return slots | {k ^ self.core: self.across(v) for k, v in slots.items()}

    def halves(self, order):
        slots = sorted(self.kept, key=lambda k: tuple(not k & bit for bit in order))
        return slots[: len(slots) // 2], slots[len(slots) // 2 :]

    def total(self, value):
        bit = 1
        while bit < self.count:
            value = value + self.swap(value, bit)
            bit *= 2
        return value


class Scatter:
    def __init__(self, plane, first, second, order):
        self.plane, self.order = plane, list(order)
        self.low, self.terms = first, [second]

    def step(self, *after):
        got = self.plane.swap(tie(self.low, after), self.order.pop(0))
        self.terms.append(got)
        if self.order:
            rest = got.shape[0] // 2
            self.low = sum(t[:rest].astype(f32) for t in self.terms).astype(bf16)
            self.terms = [t[rest:] for t in self.terms]
        return got

    def total(self, *after):
        while self.order:
            self.step(*after)
        return sum(t[0].astype(f32) for t in self.terms)


def tensor_swap(value, j):
    peers = lax.axis_size("tensor")
    return lax.ppermute(value, "tensor", [(i, i ^ j) for i in range(peers)])


def tensor_exchange(parts):
    return [tensor_swap(part, j) for j, part in enumerate(parts) if j]


def tensor_gather(part):
    return [part] + [tensor_swap(part, j) for j in range(1, lax.axis_size("tensor"))]


def row_stats(x3):
    size = x3.shape[0] * x3.shape[2]
    mean = jnp.sum(jnp.sum(x3, axis=0), axis=-1, keepdims=True) / size
    center = x3 - mean[None]
    var = jnp.sum(jnp.sum(center * center, axis=0), axis=-1, keepdims=True) / size
    inv = lax.rsqrt(var + EPS)
    return center * inv[None], inv


def row_mean(x3):
    return jnp.sum(jnp.sum(x3, axis=0), axis=-1, keepdims=True) / (x3.shape[0] * x3.shape[2])


def split(x, count):
    width = x.shape[1] // count
    return jnp.stack([x[:, i * width : (i + 1) * width] for i in range(count)])


def by_slot(slots, order_ref, from_ref, kept_ref, sent_ref):
    for ref, which in zip((kept_ref, sent_ref), slots):
        for i, k in enumerate(which):
            ref[i] = from_ref[order_ref[k]]


def norm_kernel(slots, order_ref, x_ref, gain_ref, bias_ref, kept_ref, sent_ref, normed):
    normal, _ = row_stats(split(x_ref[...].astype(f32), normed.shape[0]))
    normed[...] = (normal * gain_ref[...] + bias_ref[...]).astype(bf16)
    by_slot(slots, order_ref, normed, kept_ref, sent_ref)


def reorder_kernel(slots, order_ref, at_ref, x_ref, out_ref, kept_ref, sent_ref, slices):
    rows = x_ref.shape[0] // at_ref.shape[0]
    for j in range(at_ref.shape[0]):
        block = x_ref[pl.ds(pl.multiple_of(at_ref[j] * rows, rows), rows), :]
        out_ref[j * rows : (j + 1) * rows, :] = block
        slices[:, j * rows : (j + 1) * rows, :] = split(block, slices.shape[0])
    by_slot(slots, order_ref, slices, kept_ref, sent_ref)


def spin(x, tables, sign):
    parts = []
    for i in range(x.shape[1] // 128):
        v = x[:, i * 128 : (i + 1) * 128]
        turned = pltpu.roll(v, 128 - ROT // 2, 1) * tables[1] + pltpu.roll(v, ROT // 2, 1) * tables[2]
        parts.append(v * tables[0] + (turned if sign > 0 else -turned))
    return jnp.concatenate(parts, axis=1)


def take(refs, lengths):
    groups, at = [], 0
    for n in lengths:
        groups.append(refs[at : at + n])
        at += n
    return groups, refs[at:]


def qkv_kernel(slots, pieces, kept_ref, sent_ref, bias_ref, table_ref, *refs):
    weights, (q_ref, kv_ref) = take(refs, pieces)
    feat = q_ref.shape[1]
    x = {k: ref[i] for ref, which in zip((kept_ref, sent_ref), slots) for i, k in enumerate(which)}
    for cols in tiles(feat):
        for j in range(3):
            total = bias_ref[j, :, cols]
            for k, parts in enumerate(weights):
                part, at = parts[cols.start * len(parts) // feat], cols.start % (feat // len(parts))
                total = total + dot(x[k], part[j, :, at : at + cols.stop - cols.start])
            if j < 2:
                total = spin(total, table_ref[...], 1)
            if j == 0:
                q_ref[:, cols] = total.astype(bf16)
            else:
                kv_ref[j - 1, :, cols] = total.astype(bf16)


def head_mask(rows, h):
    lane = lax.broadcasted_iota(jnp.int32, (rows, 2 * HD), 1)
    return (lane // HD) == h


def attend_kernel(count, order_ref, at_ref, hide_ref, q_ref, here_ref, early_ref, *refs):
    weights = refs[:count]
    att_ref, log_ref, own_ref = refs[count : count + 3]
    sends = refs[count + 3 : -1]
    part_ref = refs[-1]
    rows, feat = q_ref.shape
    scale = HD**-0.5
    for pair in range(feat // (2 * HD)):
        cols = slice(pair * 2 * HD, (pair + 1) * 2 * HD)
        q = q_ref[:, cols]
        k = jnp.concatenate([early_ref[0, :, cols], here_ref[0, :, cols]], axis=0)
        v = jnp.concatenate([early_ref[1, :, cols], here_ref[1, :, cols]], axis=0)
        out = []
        for h in range(2):
            mask = head_mask(rows, h)
            scores = dot(jnp.where(mask, q, 0), k, NT) * scale + hide_ref[...]
            top = jnp.max(scores, axis=-1, keepdims=True)
            exps = jnp.exp(scores - top)
            total = jnp.sum(exps, axis=-1, keepdims=True)
            log_ref[2 * pair + h] = top + jnp.log(total)
            out.append(dot((exps / total).astype(bf16), v))
        att_ref[:, cols] = jnp.where(head_mask(rows, 0), out[0], out[1]).astype(bf16)
    for k in range(count):
        part_ref[order_ref[k]] = dot(att_ref[...], weights[k][...])
    hand_out(at_ref, part_ref, own_ref, sends)


def hand_out(at_ref, part_ref, own_ref, sends):
    rows = own_ref.shape[1]
    for j in range(at_ref.shape[0]):
        block = part_ref[:, pl.ds(pl.multiple_of(at_ref[j] * rows, rows), rows), :]
        if j == 0:
            own_ref[...] = block
        else:
            sends[j - 1][...] = block.astype(bf16)


def ffn_out_kernel(total_ref, gate_up_ref, down_ref):
    width = down_ref.shape[1]
    for i in range(2):
        gate_up_ref[i] = total_ref[i * width : (i + 1) * width].astype(f32)
    down_ref[...] = total_ref[2 * width :].astype(f32).T


def mid_kernel(at_ref, x_ref, gain_ref, bias_ref, own_ref, *refs):
    mid_ref, normed_ref = refs[-2:]
    rows = own_ref.shape[1]
    total = own_ref[...]
    for ref in refs[:-2]:
        total = total + ref[...].astype(f32)
    block = x_ref[pl.ds(pl.multiple_of(at_ref[0] * rows, rows), rows), :].astype(f32)
    mid = split(block, own_ref.shape[0]) + total
    mid_ref[...] = mid
    normal, _ = row_stats(mid)
    normed_ref[...] = (normal * gain_ref[...] + bias_ref[...]).astype(bf16)


def pack_kernel(gate_up_ref, down_ref, out_ref):
    width = down_ref.shape[1]
    out_ref[:width] = gate_up_ref[0]
    out_ref[width : 2 * width] = gate_up_ref[1]
    out_ref[2 * width :] = down_ref[...].T


def fetch(all_ref, which, to_ref, sem):
    count, rows, _ = all_ref.shape
    width = rows // 3
    copies = [
        pltpu.make_async_copy(
            all_ref.at[n, pl.ds(which * width, width)], to_ref.at[pl.ds(n * width, width)], sem.at[n]
        )
        for n in range(count)
    ]
    for copy in copies:
        copy.start()
    return copies


def tiles(size, step=256):
    return [slice(i, min(i + step, size)) for i in range(0, size, step)]


def ffn_kernel(slots, peers, order_ref, *refs):
    blocks = refs[:peers]
    cot_ref, all_ref, kept_ref, sent_ref, hidden_ref, gate_grad_ref, up_grad_ref, own_ref = refs[
        peers : peers + 8
    ]
    sends, (gate, up, down, sems, x_ref, pre_ref) = refs[peers + 8 : -6], refs[-6:]
    copies = [fetch(all_ref, i, ref, sems.at[i]) for i, ref in enumerate((gate, up, down))]
    rows, width = own_ref.shape[1:]
    for j, ref in enumerate(blocks):
        at = slice(j * rows, (j + 1) * rows)
        for n in range(own_ref.shape[0]):
            x_ref[at, n * width : (n + 1) * width] = ref[n]
        for to_ref, which in zip((kept_ref, sent_ref), slots):
            for i, k in enumerate(which):
                to_ref[i, at, :] = ref[order_ref[k]]
    x = x_ref[...]
    for copy in copies[0]:
        copy.wait()
    for cols in tiles(hidden_ref.shape[1]):
        pre_ref[:, cols] = dot(x, gate[:, cols])
    for copy in copies[1] + copies[2]:
        copy.wait()
    for cols in tiles(hidden_ref.shape[1]):
        gate_pre = pre_ref[:, cols]
        up_pre = dot(x, up[:, cols])
        hidden_grad = dot(cot_ref[...], down[:, cols])
        sigma = 1.0 / (1.0 + jnp.exp(-gate_pre))
        silu = gate_pre * sigma
        hidden_ref[:, cols] = (silu * up_pre).astype(bf16)
        gate_grad_ref[:, cols] = (
            hidden_grad * up_pre * sigma * (1.0 + gate_pre * (1.0 - sigma))
        ).astype(bf16)
        up_grad_ref[:, cols] = (hidden_grad * silu).astype(bf16)
    for n in range(own_ref.shape[0]):
        at = slice(n * width, (n + 1) * width)
        total = dot(gate_grad_ref[...], gate[at], NT) + dot(up_grad_ref[...], up[at], NT)
        cut(n, total, own_ref, sends)


def cut(n, total, own_ref, sends):
    rows = own_ref.shape[1]
    own_ref[n] = total[:rows]
    for j, ref in enumerate(sends):
        ref[n] = total[(j + 1) * rows : (j + 2) * rows].astype(bf16)


def down_kernel(at_ref, hidden_ref, all_ref, mid_ref, out_ref, down, sem):
    for copy in fetch(all_ref, 2, down, sem):
        copy.wait()
    count, rows, width = mid_ref.shape
    for n in range(count):
        at = slice(n * width, (n + 1) * width)
        total = dot(hidden_ref[...], down[at], NT)
        for j in range(at_ref.shape[0]):
            block = total[j * rows : (j + 1) * rows]
            block = block + mid_ref[n] if j == 0 else block
            out_ref[pl.ds(pl.multiple_of(at_ref[j] * rows, rows), rows), at] = block.astype(bf16)


def ffn_weights_kernel(place_ref, *refs):
    x, cot, grads, out_ref = refs[:2], refs[2:4], refs[4:10], refs[10]
    width = x[0].shape[2]
    for i, left in enumerate((x, x, cot)):
        total = dot(left[0][0], grads[2 * i][...], TN) + dot(left[1][0], grads[2 * i + 1][...], TN)
        out_ref[i * width : (i + 1) * width] = total.astype(bf16)


def norm_back(normal, inv, grad, gain):
    scaled = grad * gain
    inner = row_mean(scaled * normal)
    return inv[None] * (scaled - row_mean(scaled)[None] - normal * inner[None])


def token_sum(x3):
    return jnp.sum(x3, axis=1, keepdims=True)


def mid_back_kernel(mid_ref, cot_ref, gain_ref, own_ref, *refs):
    grad_ref, low_ref, gain_grad_ref, bias_grad_ref = refs[-4:]
    total = own_ref[...]
    for ref in refs[:-4]:
        total = total + ref[...].astype(f32)
    normal, inv = row_stats(mid_ref[...])
    gain_grad_ref[...] = token_sum(total * normal)
    bias_grad_ref[...] = token_sum(total)
    cot = split(cot_ref[: mid_ref.shape[1]].astype(f32), mid_ref.shape[0])
    grad = cot + norm_back(normal, inv, total, gain_ref[...])
    grad_ref[...] = grad
    low_ref[...] = grad.astype(bf16)


def attend_back_kernel(
    slots, peers, order_ref, at_ref, hide_ref, table_ref, q_ref, here_ref, early_ref, log_ref, *refs
):
    count = order_ref.shape[0]
    lows = refs[:peers]
    weights = refs[peers : peers + count]
    kept_ref, sent_ref, dq_ref, dhere_ref, dearly_ref, datt = refs[peers + count :]
    rows, feat = q_ref.shape
    part = rows // peers
    scale = HD**-0.5
    low = {}
    for ref, which in zip((kept_ref, sent_ref), slots):
        for i, k in enumerate(which):
            low[k] = ref.at[i]
            for j in range(peers):
                at = pl.ds(pl.multiple_of(at_ref[j] * part, part), part)
                ref[i, at, :] = lows[j][order_ref[k]]
    for cols in tiles(feat):
        total = dot(low[0][...], weights[0][cols], NT)
        for k in range(1, count):
            total = total + dot(low[k][...], weights[k][cols], NT)
        datt[:, cols] = total.astype(bf16)
    for pair in range(feat // (2 * HD)):
        cols = slice(pair * 2 * HD, (pair + 1) * 2 * HD)
        q = q_ref[:, cols]
        k = jnp.concatenate([early_ref[0, :, cols], here_ref[0, :, cols]], axis=0)
        v = jnp.concatenate([early_ref[1, :, cols], here_ref[1, :, cols]], axis=0)
        da = datt[:, cols]
        grads = []
        for h in range(2):
            mask = head_mask(rows, h)
            scores = dot(jnp.where(mask, q, 0), k, NT) * scale + hide_ref[...]
            probs = jnp.exp(scores - log_ref[2 * pair + h])
            weight_grad = dot(jnp.where(mask, da, 0), v, NT)
            inner = jnp.sum(probs * weight_grad, axis=-1, keepdims=True)
            score_grad = (probs * (weight_grad - inner)).astype(bf16)
            grads.append(
                (
                    dot(score_grad, k) * scale,
                    dot(score_grad, q, TN) * scale,
                    dot(probs.astype(bf16), da, TN),
                )
            )
        dq = jnp.where(head_mask(rows, 0), grads[0][0], grads[1][0])
        dq_ref[:, cols] = spin(dq, table_ref[...], -1).astype(bf16)
        for i in (1, 2):
            both = jnp.where(head_mask(2 * rows, 0), grads[0][i], grads[1][i])
            dearly_ref[i - 1, :, cols] = both[:rows].astype(bf16)
            dhere_ref[i - 1, :, cols] = both[rows:]


def out_weights_kernel(slots, halves, *refs):
    att, low, outs = refs[:2], refs[2:4], refs[4:]
    part = att[0].shape[1] // 2
    for h, both in enumerate(halves):
        cols = slice(h * part, (h + 1) * part)
        for ref, which in zip(outs[2 * h :], both):
            for i, k in enumerate(which):
                at = slots[0].index(k)
                total = dot(att[0][:, cols], low[0][at], TN) + dot(att[1][:, cols], low[1][at], TN)
                ref[i] = total.astype(bf16)


def one_grad_kernel(
    pieces, order_ref, at_ref, x_ref, table_ref, dq_ref, dhere_ref, dback_ref, *refs
):
    weights, refs = take(refs, pieces)
    *back_refs, bias_ref, gain_grad_ref, norm_bias_ref, own_ref = refs[:7]
    sends, part_ref = refs[7:-1], refs[-1]
    back_refs[0][...] = dq_ref[...]
    dk = dhere_ref[0] + dback_ref[0].astype(f32)
    back_refs[1][...] = spin(dk, table_ref[...], -1).astype(bf16)
    back_refs[2][...] = (dhere_ref[1] + dback_ref[1].astype(f32)).astype(bf16)
    for j, ref in enumerate(back_refs):
        bias_ref[j] = jnp.sum(ref[...].astype(f32), axis=0, keepdims=True)
    for k, parts in enumerate(weights):
        total, at = None, 0
        for part in parts:
            size = part.shape[2]
            for j, ref in enumerate(back_refs):
                term = dot(ref[:, at : at + size], part[j], NT)
                total = term if total is None else total + term
            at += size
        part_ref[order_ref[k]] = total
    normal, _ = row_stats(split(x_ref[...].astype(f32), len(weights)))
    gain_grad_ref[...] = token_sum(part_ref[...] * normal)
    norm_bias_ref[...] = token_sum(part_ref[...])
    hand_out(at_ref, part_ref, own_ref, sends)


def qkv_weights_kernel(slots, halves, *refs):
    x, grads, outs = refs[:2], refs[2:8], refs[8:]
    part = grads[0].shape[1] // 2
    for h, both in enumerate(halves):
        cols = slice(h * part, (h + 1) * part)
        for ref, which in zip(outs[2 * h :], both):
            for i, k in enumerate(which):
                at = slots[0].index(k)
                for j in range(3):
                    total = dot(x[0][at], grads[j][:, cols], TN)
                    total = total + dot(x[1][at], grads[3 + j][:, cols], TN)
                    ref[i, j] = total.astype(bf16)


def input_grad_kernel(at_ref, x_ref, gain_ref, mid_grad_ref, own_ref, *refs):
    rows = own_ref.shape[1]
    total = own_ref[...]
    for ref in refs[:-1]:
        total = total + ref[...].astype(f32)
    block = x_ref[pl.ds(pl.multiple_of(at_ref[0] * rows, rows), rows), :].astype(f32)
    normal, inv = row_stats(split(block, own_ref.shape[0]))
    refs[-1][...] = (mid_grad_ref[...] + norm_back(normal, inv, total, gain_ref[...])).astype(bf16)


def join_kernel(at_ref, *refs):
    out_ref = refs[-1]
    slices, rows, width = refs[0].shape
    for j, ref in enumerate(refs[:-1]):
        at = pl.ds(pl.multiple_of(at_ref[j] * rows, rows), rows)
        for n in range(slices):
            out_ref[at, n * width : (n + 1) * width] = ref[n]


def on_device(
    block_in,
    seq_lengths,
    attn_gain,
    attn_bias,
    qkv_weight,
    qkv_bias,
    out_weight,
    ffn_gain,
    ffn_bias,
    gate_up_weight,
    down_weight,
    out_cotangent,
):
    tok, model = block_in.shape
    feat = qkv_weight.shape[2]
    hid = down_weight.shape[0]
    plane = Plane()
    count = plane.count
    width = model // count
    peers = lax.axis_size("tensor")
    chunk = tok // peers
    heads = feat // HD
    order = plane.me ^ jnp.arange(count, dtype=jnp.int32)
    at = lax.axis_index("tensor") ^ jnp.arange(peers, dtype=jnp.int32)

    offset = lax.axis_index("context") * tok
    places = offset + jnp.arange(tok, dtype=jnp.int32)
    lengths = seq_lengths[0]
    ends = jnp.cumsum(lengths)
    starts = jnp.sum(jnp.where(ends[None, :] <= places[:, None], lengths[None, :], 0), axis=1)
    turn = ROT // 2
    frequency = jnp.exp(jnp.arange(turn).astype(f32) * (-2.0 * math.log(10000.0) / ROT))
    angles = (places - starts).astype(f32)[:, None] * frequency[None, :]
    cosine = jnp.tile(jnp.cos(angles), (1, 128 // turn))
    sine = jnp.tile(jnp.sin(angles), (1, 128 // turn))
    lane = jnp.arange(128)[None, :] % HD
    tables = jnp.stack(
        [
            jnp.where(lane < ROT, cosine, 1.0),
            jnp.where(lane < turn, -sine, 0.0),
            jnp.where((lane >= turn) & (lane < ROT), sine, 0.0),
        ]
    )
    key_places = offset - tok + jnp.arange(2 * tok, dtype=jnp.int32)
    visible = (key_places[None, :] <= places[:, None]) & (key_places[None, :] >= starts[:, None])
    hide = jnp.where(visible, 0.0, NEG).astype(f32)

    by_slice = lambda vec: vec.reshape(count, 1, width)
    slots = (plane.kept, plane.sent)
    slice_pair = (shape((count // 2, tok, width), bf16),) * 2
    slices = pltpu.VMEM((count, tok, width), bf16)
    one_kept, one_sent = call(
        functools.partial(norm_kernel, slots), "norm_one", slice_pair,
        (order, block_in, by_slice(attn_gain), by_slice(attn_bias)), [SM] + [VM] * 3,
        scratch=[slices],
    )
    cot, cot_kept, cot_sent = call(
        functools.partial(reorder_kernel, slots), "cotangent_rows",
        (shape((tok, model), bf16), *slice_pair), (order, at, out_cotangent), [SM, SM, VM],
        scratch=[slices],
    )

    qkv_slots = plane.gather_halves(qkv_weight, one_kept, one_sent, tables, hide, cot)
    pieces = [len(qkv_slots[k]) for k in range(count)]
    qkv_list = [piece for k in range(count) for piece in qkv_slots[k]]
    first = (qkv_slots[plane.up[0]], qkv_slots[plane.up[-1]])
    passed = qkv_slots[plane.up[0] ^ plane.up[-1]]
    ffn_shard = call(
        pack_kernel, "ffn_shard", shape((3 * width, hid), bf16), (gate_up_weight, down_weight),
        [VM, VM],
    )
    out_slots = plane.gather(tie(out_weight, ffn_shard), plane.up, passed)
    out_list = [out_slots[k] for k in range(count)]
    ffn_all = lax.all_gather(tie(ffn_shard, first), PLANE, axis=0, tiled=False)

    queries, here = call(
        functools.partial(qkv_kernel, slots, pieces), "qkv",
        (shape((tok, feat), bf16), shape((2, tok, feat), bf16)),
        (one_kept, one_sent, qkv_bias.reshape(3, 1, feat), tables, *qkv_list),
        [VM] * (4 + sum(pieces)),
    )
    early = lax.ppermute(here, "context", [(i, i + 1) for i in range(plane.context - 1)])
    sends = [shape((count, chunk, width), bf16)] * (peers - 1)
    own_shape = shape((count, chunk, width), f32)
    attended, logs, own, *parts = call(
        functools.partial(attend_kernel, count), "attend",
        (shape((tok, feat), bf16), shape((heads, tok, 1), f32), own_shape, *sends),
        (order, at, hide, queries, here, early, *out_list),
        [SM, SM] + [VM] * (4 + count),
        scratch=[pltpu.VMEM((count, tok, width), f32)],
    )
    got = tensor_exchange([None] + parts)
    mid, normed_chunk = call(
        mid_kernel, "mid", (own_shape, sends[0]),
        (at, block_in, by_slice(ffn_gain), by_slice(ffn_bias), own, *got),
        [SM] + [VM] * (4 + len(got)),
    )
    normed_two = tensor_gather(normed_chunk)

    hid_shape = shape((tok, hid), bf16)
    buffer = pltpu.VMEM((model, hid), bf16)
    two_kept, two_sent, hidden, gate_grad, up_grad, grad_own, *grad_parts = call(
        functools.partial(ffn_kernel, slots, peers), "ffn",
        (*slice_pair, hid_shape, hid_shape, hid_shape, own_shape, *sends),
        (order, *normed_two, cot, ffn_all), [SM] + [VM] * (peers + 1) + [HB],
        scratch=[buffer] * 3
        + [
            pltpu.SemaphoreType.DMA((3, count)), pltpu.VMEM((tok, model), bf16),
            pltpu.VMEM((tok, hid), f32),
        ],
    )
    got = tensor_exchange([None] + grad_parts)
    two_got, cot_got, hidden_got, gate_got, up_got = plane.across(
        (two_sent, cot_sent, hidden, gate_grad, up_grad)
    )
    place = jnp.stack([plane.rank(k) for k in plane.kept])
    of_slot = pl.BlockSpec((1, tok, width), lambda i, place: (i, 0, 0))
    whole = pl.BlockSpec((tok, hid), lambda i, place: (0, 0))
    ffn_grads = pl.pallas_call(
        ffn_weights_kernel,
        grid_spec=pltpu.PrefetchScalarGridSpec(
            num_scalar_prefetch=1,
            grid=(count // 2,),
            in_specs=[of_slot] * 4 + [whole] * 6,
            out_specs=pl.BlockSpec((3 * width, hid), lambda i, place: (place[i], 0)),
        ),
        out_shape=shape((count // 2 * 3 * width, hid), bf16),
        **params("ffn_weights"),
    )(
        place, two_kept, two_got, cot_kept, cot_got,
        gate_grad, gate_got, up_grad, up_got, hidden, hidden_got,
    )
    block_part = call(
        down_kernel, "down", shape((tok, model), bf16), (at, hidden, ffn_all, mid),
        [SM, VM, HB, VM], scratch=[buffer, pltpu.SemaphoreType.DMA((count,))],
    )
    block_out = lax.psum(block_part, "tensor")
    ffn_total = lax.psum_scatter(
        tie(ffn_grads, block_part),
        PLANE, scatter_dimension=0, axis_index_groups=plane.groups, tiled=True,
    )
    grad_own = tie(grad_own, ffn_grads, block_part)
    vec = shape((count, 1, width), f32)
    mid_grad, low_chunk, ffn_gain_grad, ffn_bias_grad = call(
        mid_back_kernel, "mid_back", (own_shape, sends[0], vec, vec),
        (mid, cot, by_slice(ffn_gain), grad_own, *got),
        [VM] * (4 + len(got)),
    )
    low_blocks = tensor_gather(low_chunk)

    low_kept, low_sent, dq, dhere, dearly = call(
        functools.partial(attend_back_kernel, slots, peers), "attend_back",
        (
            *slice_pair, shape((tok, feat), bf16),
            shape((2, tok, feat), f32), shape((2, tok, feat), bf16),
        ),
        (order, at, hide, tables, queries, here, early, logs, *low_blocks, *out_list),
        [SM, SM] + [VM] * (6 + peers + count),
        scratch=[pltpu.VMEM((tok, feat), bf16)],
    )
    dback = lax.ppermute(dearly, "context", [(i + 1, i) for i in range(plane.context - 1)])
    halves = (plane.halves(plane.down), plane.halves(plane.up))
    half = feat // 2
    stacks = lambda *dims: (shape((count // 4,) + dims, bf16),) * 4
    out_grads = call(
        functools.partial(out_weights_kernel, slots, halves), "out_weights", stacks(half, width),
        (attended, plane.across(attended), low_kept, plane.across(low_sent)), [VM] * 4,
    )
    out_a = Scatter(plane, *out_grads[:2], plane.down)
    out_b = Scatter(plane, *out_grads[2:], plane.up)
    out_total = [out_a.total(dback), out_b.total(dback)]
    results = call(
        functools.partial(one_grad_kernel, pieces), "one_grad",
        (
            *[shape((tok, feat), bf16)] * 3, shape((3, 1, feat), f32), vec, vec, own_shape, *sends,
        ),
        (order, at, block_in, tables, dq, dhere, dback, *qkv_list),
        [SM, SM] + [VM] * (5 + sum(pieces)),
        scratch=[pltpu.VMEM((count, tok, width), f32)],
    )
    back, (bias_grad, attn_gain_grad, attn_bias_grad, own), parts = (
        results[:3], results[3:7], results[7:]
    )
    got = tensor_exchange([None, *parts])
    qkv_grads = call(
        functools.partial(qkv_weights_kernel, slots, halves), "qkv_weights", stacks(3, width, half),
        (one_kept, plane.across(one_sent), *back, *plane.across(back)), [VM] * 8,
    )
    qkv_a = Scatter(plane, *qkv_grads[:2], plane.down)
    qkv_b = Scatter(plane, *qkv_grads[2:], plane.up)
    qkv_total = [qkv_a.total(out_total), qkv_b.total(out_total)]
    grad_chunk = call(
        input_grad_kernel, "input_grad", sends[0],
        (at, block_in, by_slice(attn_gain), mid_grad, own, *got),
        [SM] + [VM] * (4 + len(got)),
    )
    grad_blocks = tensor_gather(grad_chunk)
    input_grad = call(
        join_kernel, "input_grad_rows", shape((tok, model), bf16), (at, *grad_blocks),
        [SM] + [VM] * peers,
    )
    gate_up_grad, down_grad = call(
        ffn_out_kernel, "ffn_out", (shape((2, width, hid), f32), shape((hid, width), f32)),
        (ffn_total,), [VM],
    )

    small = jnp.concatenate(
        [
            v.reshape(-1)
            for v in (attn_gain_grad, attn_bias_grad, ffn_gain_grad, ffn_bias_grad, bias_grad)
        ]
    )
    small = plane.total(tie(small, got))
    vectors = small[: 4 * model].reshape(4, model)
    vectors = vectors + sum(tensor_swap(vectors, j) for j in range(1, peers))
    qkv_bias_grad = small[4 * model :].reshape(3, feat)

    return (
        block_out,
        input_grad,
        vectors[0],
        vectors[1],
        jnp.concatenate(qkv_total, axis=2),
        qkv_bias_grad,
        jnp.concatenate(out_total, axis=0),
        vectors[2],
        vectors[3],
        gate_up_grad,
        down_grad,
    )


def solution(mesh):
    in_specs = (
        P(("fsdp", "context"), None),
        P("fsdp", None),
        P(),
        P(),
        P(None, ("fsdp", "context"), "tensor"),
        P(None, "tensor"),
        P("tensor", ("fsdp", "context")),
        P(),
        P(),
        P(None, ("fsdp", "context"), "tensor"),
        P("tensor", ("fsdp", "context")),
        P(("fsdp", "context"), None),
    )
    out_specs = (
        P(("fsdp", "context"), None),
        P(("fsdp", "context"), None),
        P(),
        P(),
        P(None, ("fsdp", "context"), "tensor"),
        P(None, "tensor"),
        P("tensor", ("fsdp", "context")),
        P(),
        P(),
        P(None, ("fsdp", "context"), "tensor"),
        P("tensor", ("fsdp", "context")),
    )
    return jax.shard_map(
        on_device, mesh=mesh, in_specs=in_specs, out_specs=out_specs, check_vma=False
    )
```

time: 470 us -> 393 us (0.84)
  starting transfers between devices: 136 us -> 67.3 us
  waiting for transfers between devices: 152 us -> 191 us
  local copies, waits for them, and re-layouts: 43.6 us -> 15.9 us
  other arithmetic: 17.5 us -> 7.38 us
  Pallas kernels: 104 us -> 96.7 us
    ppermute x27 -> x21, starting transfers between devices: 83.8 us -> 39.7 us  [tensor_swap(): return lax.ppermute(value, 'tensor', [(i, i ^ j) for i in range(peers)])]
    ppermute x27 -> x21, waiting for transfers between devices: 61.3 us -> 96.4 us  [tensor_swap(): return lax.ppermute(value, 'tensor', [(i, i ^ j) for i in range(peers)])]
    ppermute x1, waiting for transfers between devices: 0.01 us -> 24.1 us  [on_device(): lax.ppermute(dearly, 'context', [(i + 1, i) for i in range(plane.context...]
    all_gather x1 -> x0, local copies, waits for them, and re-layouts: 21.1 us -> none  [on_device(): ffn_all = lax.all_gather(ffn_shard, PLANE, axis=0, tiled=False)]
    ppermute x48 -> x30, waiting for transfers between devices: 54.1 us -> 38.6 us  [swap(): return lax.ppermute(value, 'fsdp', pairs)]
    ppermute x48 -> x30, starting transfers between devices: 26.7 us -> 11.8 us  [swap(): return lax.ppermute(value, 'fsdp', pairs)]
    ppermute x14 -> x8, starting transfers between devices: 20.4 us -> 10.5 us  [swap(): return lax.ppermute(value, 'context', pairs)]
    ppermute x14 -> x8, waiting for transfers between devices: 36.3 us -> 26.9 us  [swap(): return lax.ppermute(value, 'context', pairs)]
  transfers between devices with their start and end apart: 93 -> 64, of which waited for: 23 -> 26; matrix products, arithmetic and copies ran while one was open for 9% -> 3% of each run, Pallas kernels for 17% -> 20%
where the time goes in v2:
time: 393 us; the launch traced here: 392 us
  waiting for transfers between devices  191 us (49%)
  Pallas kernels  96.7 us (25%)
  starting transfers between devices  67.3 us (17%)
  local copies, waits for them, and re-layouts  15.9 us (4%)
  between operations  14.5 us (4%)
  other arithmetic  7.38 us (2%)
    ppermute x21, waiting for transfers between devices, tensor_swap(): return lax.ppermute(value, 'tensor', [(i, i ^ j) for i in range(peers)])  96.4 us
    pallas_call x16, Pallas kernels, call(): pl.pallas_call(kernel, out_shape=outs, in_specs=specs, out_specs=jax.tree...  86 us
    ppermute x21, starting transfers between devices, tensor_swap(): return lax.ppermute(value, 'tensor', [(i, i ^ j) for i in range(peers)])  39.7 us
    ppermute x30, waiting for transfers between devices, swap(): return lax.ppermute(value, 'fsdp', pairs)  38.6 us
    ppermute x8, waiting for transfers between devices, swap(): return lax.ppermute(value, 'context', pairs)  26.9 us
    ppermute x1, waiting for transfers between devices, on_device(): lax.ppermute(dearly, 'context', [(i + 1, i) for i in range(plane.context...  24.1 us
    unnamed x125, local copies, waits for them, and re-layouts  13.8 us
    ppermute x30, starting transfers between devices, swap(): return lax.ppermute(value, 'fsdp', pairs)  11.8 us
  transfers between devices with their start and end apart: 64, of which 26 were waited for; matrix products, arithmetic and copies ran while one was open for 3% of the time, Pallas kernels for 20%

profile of v2, /device:TPU:0, one launch (start us, length us, event | category | flops | bytes accessed | tf_op | source)
XLA Modules:
  0.0 392.4 jit_solution(4884334982280854431)
XLA Ops:
  7.2 3.0 collective-permute-start.3
  11.7 3.2 ffn_shard.1
  14.9 13.1 %collective-permute-done.3.refs_4_ = bf16[3,256,512]{2,1,0:T(8,128)(2,1)S(1)} collective-permute-done((bf16[3,256,512]{2,1,0:T(8,128)(2,1)}, bf16[3,256,512]{2,1,0:T(8,128)(2,1)S(1)}, u32[]{:S(2)}, u32[]{:S(2)}) %collective-permute-start.3) | collective-permute-done | bytes 786464 | tf_op jit(solution)/shard_map/ppermute | solution.py:88
  33.8 2.7 cotangent_rows.1
  36.5 3.3 norm_one.1
  42.1 18.8 %collective-permute-done.4.refs_5_ = bf16[3,256,256]{2,1,0:T(8,128)(2,1)S(1)} collective-permute-done((bf16[3,256,256]{2,1,0:T(8,128)(2,1)S(1)}, bf16[3,256,256]{2,1,0:T(8,128)(2,1)S(1)}, u32[]{:S(2)}, u32[]{:S(2)}) %collective-permute-start.4) | collective-permute-done | bytes 393248 | tf_op jit(solution)/shard_map/ppermute | solution.py:85
  66.0 5.9 %qkv.1 = (bf16[256,512]{1,0:T(8,128)(2,1)}, bf16[2,256,512]{2,1,0:T(8,128)(2,1)}) custom-call(bf16[4,256,256]{2,1,0:T(8,128)(2,1)} %get-tuple-element.80.kept_ref.refs_0_, bf16[4,256,256]{2,1,0:T(8,128)(2,1)} %get-tuple-element.81.sent_ref, f32[3,1,512]{2,1,0:T(1,128)} %reshape.324.bias_ref, f32[3,256,128]{2,1,0:T(8,128)} %pad_maximum_fusion.2.table_ref, ...), custom_call_target="tpu_custom_call" | custom-call | flops 11500000256 | tf_op jit(solution)/shard_map/qkv/pallas_call | solution.py:41
  71.9 3.6 collective-permute-start.9
  77.0 7.6 %collective-permute-done.14.refs_5_.refs_9_ = bf16[512,256]{1,0:T(8,128)(2,1)S(1)} collective-permute-done((bf16[512,256]{1,0:T(8,128)(2,1)}, bf16[512,256]{1,0:T(8,128)(2,1)S(1)}, u32[]{:S(2)}, u32[]{:S(2)}) %collective-permute-start.14) | collective-permute-done | bytes 262176 | tf_op jit(solution)/shard_map/ppermute | solution.py:88
  87.7 8.5 %attend.1 = (bf16[256,512]{1,0:T(8,128)(2,1)}, f32[8,256,1]{2,1,0:T(8,128)}, f32[8,64,256]{2,1,0:T(8,128)}, bf16[8,64,256]{2,1,0:T(8,128)(2,1)}, bf16[8,64,256]{...) custom-call(s32[8]{0:T(128)} %iota_xor_fusion.order_ref, s32[4]{0:T(128)} %iota_xor_fusion.1.at_ref, ...), custom_call_target="tpu_custom_call" | custom-call | tf_op jit(solution)/shard_map/attend/pallas_call | solution.py:41
  97.8 2.7 collective-permute-start.18
  100.7 8.0 %collective-permute-done.17.refs_0_ = bf16[8,64,256]{2,1,0:T(8,128)(2,1)S(1)} collective-permute-done((bf16[8,64,256]{2,1,0:T(8,128)(2,1)}, bf16[8,64,256]{2,1,0:T(8,128)(2,1)S(1)}, u32[]{:S(2)}, u32[]{:S(2)}) %collective-permute-start.17) | collective-permute-done | bytes 262176 | tf_op jit(solution)/shard_map/ppermute | solution.py:146
  108.7 10.7 %collective-permute-done.18.refs_1_ = bf16[8,64,256]{2,1,0:T(8,128)(2,1)S(1)} collective-permute-done((bf16[8,64,256]{2,1,0:T(8,128)(2,1)}, bf16[8,64,256]{2,1,0:T(8,128)(2,1)S(1)}, u32[]{:S(2)}, u32[]{:S(2)}) %collective-permute-start.18) | collective-permute-done | bytes 262176 | tf_op jit(solution)/shard_map/ppermute | solution.py:146
  120.2 2.7 mid.1
  122.9 4.2 %collective-permute-start.20 = (bf16[8,64,256]{2,1,0:T(8,128)(2,1)}, bf16[8,64,256]{2,1,0:T(8,128)(2,1)S(1)}, u32[]{:S(2)}, u32[]{:S(2)}) collective-permute-start(bf16[8,64,256]{2,1,0:T(8,128)(2,1)} %get-tuple-element.93.refs_0_), channel_id=1, source_target_pairs={{0,1},{1,0},{2,3},{3,2},{4,5},{5,4},{6,7},{7,6},{8,9},{9,8},{10,11... | collective-permute-start | bytes 786440 | tf_op jit(solution)/shard_map/ppermute | solution.py:146
  129.4 6.4 %collective-permute-done.20.refs_1_ = bf16[8,64,256]{2,1,0:T(8,128)(2,1)S(1)} collective-permute-done((bf16[8,64,256]{2,1,0:T(8,128)(2,1)}, bf16[8,64,256]{2,1,0:T(8,128)(2,1)S(1)}, u32[]{:S(2)}, u32[]{:S(2)}) %collective-permute-start.20) | collective-permute-done | bytes 262176 | tf_op jit(solution)/shard_map/ppermute | solution.py:146
  135.8 12.5 %collective-permute-done.21.refs_2_ = bf16[8,64,256]{2,1,0:T(8,128)(2,1)S(1)} collective-permute-done((bf16[8,64,256]{2,1,0:T(8,128)(2,1)}, bf16[8,64,256]{2,1,0:T(8,128)(2,1)S(1)}, u32[]{:S(2)}, u32[]{:S(2)}) %collective-permute-start.21) | collective-permute-done | bytes 262176 | tf_op jit(solution)/shard_map/ppermute | solution.py:146
  149.2 15.5 %ffn.1 = (bf16[4,256,256]{2,1,0:T(8,128)(2,1)}, bf16[4,256,256]{2,1,0:T(8,128)(2,1)}, bf16[256,1408]{1,0:T(8,128)(2,1)}, bf16[256,1408]{1,0:T(8,128)(2,1)}, bf16...) custom-call(s32[8]{0:T(128)} %iota_xor_fusion.order_ref, ...), custom_call_target="tpu_custom_call" | custom-call | tf_op jit(solution)/shard_map/ffn/pallas_call | solution.py:41
  165.8 2.4 collective-permute-done.24.refs_3_
  168.3 3.4 collective-permute-start.28
  175.0 6.8 %down.1 = bf16[256,2048]{1,0:T(8,128)(2,1)} custom-call(s32[4]{0:T(128)} %iota_xor_fusion.1.at_ref, bf16[256,1408]{1,0:T(8,128)(2,1)} %get-tuple-element.95.hidden_ref.refs_8_, bf16[8,768,1408]{2,1,0:T(8,128)(2,1)} %bitcast.33, f32[8,64,256]{2,1,0:T(8,128)} %get-tuple-element.96.mid_ref), custom_call_target="tpu_custom_call" | custom-call | tf_op jit(solution)/shard_map/down/pallas_call | solution.py:41
  183.0 10.6 %ffn_weights.1 = bf16[3072,1408]{1,0:T(8,128)(2,1)} custom-call(s32[4]{0:T(128)} %pad_add_fusion.place_ref, bf16[4,256,256]{2,1,0:T(8,128)(2,1)} %get-tuple-element.98.refs_0_, bf16[4,256,256]{2,1,0:T(8,128)(2,1)} %copy-done.15, bf16[4,256,256]{2,1,0:T(8,128)(2,1)} %get-tuple-element.100.refs_2_, bf16[4,256,256]{2,1,0:T(8,128)(2,1)} %copy-done.14, ...), custom_call_target="tpu_custom_call" | custom-call | tf_op jit(solution)/shard_map/ffn_weights/pallas_call | solution.py:651
  194.3 3.2 mid_back.1
  197.6 4.1 %collective-permute-start.31 = (bf16[8,64,256]{2,1,0:T(8,128)(2,1)}, bf16[8,64,256]{2,1,0:T(8,128)(2,1)S(1)}, u32[]{:S(2)}, u32[]{:S(2)}) collective-permute-start(bf16[8,64,256]{2,1,0:T(8,128)(2,1)} %get-tuple-element.110.refs_0_), channel_id=1, source_target_pairs={{0,1},{1,0},{2,3},{3,2},{4,5},{5,4},{6,7},{7,6},{8,9},{9,8},{10,11... | collective-permute-start | bytes 786440 | tf_op jit(solution)/shard_map/ppermute | solution.py:146
  204.1 7.6 %collective-permute-done.31.refs_1_ = bf16[8,64,256]{2,1,0:T(8,128)(2,1)S(1)} collective-permute-done((bf16[8,64,256]{2,1,0:T(8,128)(2,1)}, bf16[8,64,256]{2,1,0:T(8,128)(2,1)S(1)}, u32[]{:S(2)}, u32[]{:S(2)}) %collective-permute-start.31) | collective-permute-done | bytes 262176 | tf_op jit(solution)/shard_map/ppermute | solution.py:146
  211.7 11.5 %collective-permute-done.32.refs_2_ = bf16[8,64,256]{2,1,0:T(8,128)(2,1)S(1)} collective-permute-done((bf16[8,64,256]{2,1,0:T(8,128)(2,1)}, bf16[8,64,256]{2,1,0:T(8,128)(2,1)S(1)}, u32[]{:S(2)}, u32[]{:S(2)}) %collective-permute-start.32) | collective-permute-done | bytes 262176 | tf_op jit(solution)/shard_map/ppermute | solution.py:146
  224.1 10.0 %attend_back.1 = (bf16[4,256,256]{2,1,0:T(8,128)(2,1)}, bf16[4,256,256]{2,1,0:T(8,128)(2,1)}, bf16[256,512]{1,0:T(8,128)(2,1)}, f32[2,256,512]{2,1,0:T(8,128)}, bf16[2,256,512]{2,1,0:T(8,128)(2,1)}) custom-call(s32[8]{0:T(128)} %iota_xor_fusion.order_ref, s32[4]{0:T(128)} %iota_xor_fusion.1.at_ref, f32[256,512]{1,0:T(8,128)} %and_select_fusion.hide_ref, ...), custom_call_target="tpu_custom_call" | custom-call | flops 230000001024 | tf_op jit(solution)/shard_map/attend_back/pallas_call | solution.py:41
  236.2 24.1 %collective-permute-done.34.dback_ref = bf16[2,256,512]{2,1,0:T(8,128)(2,1)S(1)} collective-permute-done((bf16[2,256,512]{2,1,0:T(8,128)(2,1)}, bf16[2,256,512]{2,1,0:T(8,128)(2,1)S(1)}, u32[]{:S(2)}, u32[]{:S(2)}) %collective-permute-start.34) | collective-permute-done | bytes 524320 | tf_op jit(solution)/shard_map/ppermute | solution.py:693
  261.2 7.7 %one_grad.1 = (bf16[256,512]{1,0:T(8,128)(2,1)}, bf16[256,512]{1,0:T(8,128)(2,1)}, bf16[256,512]{1,0:T(8,128)(2,1)}, f32[3,1,512]{2,1,0:T(1,128)}, f32[8,1,256]{...) custom-call(s32[8]{0:T(128)} %iota_xor_fusion.order_ref, ...), custom_call_target="tpu_custom_call" | custom-call | tf_op jit(solution)/shard_map/one_grad/pallas_call | solution.py:41
  269.6 4.6 %collective-permute-start.35 = (bf16[8,64,256]{2,1,0:T(8,128)(2,1)}, bf16[8,64,256]{2,1,0:T(8,128)(2,1)S(1)}, u32[]{:S(2)}, u32[]{:S(2)}) collective-permute-start(bf16[8,64,256]{2,1,0:T(8,128)(2,1)} %get-tuple-element.115), channel_id=1, source_target_pairs={{0,1},{1,0},{2,3},{3,2},{4,5},{5,4},{6,7},{7,6},{8,9},{9,8},{10,11... | collective-permute-start | bytes 786440 | tf_op jit(solution)/shard_map/ppermute | solution.py:146
  278.0 3.6 collective-permute-done.35.refs_0_
  281.6 13.0 %collective-permute-done.36.refs_1_ = bf16[8,64,256]{2,1,0:T(8,128)(2,1)S(1)} collective-permute-done((bf16[8,64,256]{2,1,0:T(8,128)(2,1)}, bf16[8,64,256]{2,1,0:T(8,128)(2,1)S(1)}, u32[]{:S(2)}, u32[]{:S(2)}) %collective-permute-start.36) | collective-permute-done | bytes 262176 | tf_op jit(solution)/shard_map/ppermute | solution.py:146
  296.3 2.8 out_weights.1
  299.1 2.0 collective-permute-start.55
  301.7 3.0 input_grad.1.refs_0_
  304.8 4.0 %collective-permute-done.55 = bf16[2,256,256]{2,1,0:T(8,128)(2,1)S(1)} collective-permute-done((bf16[2,256,256]{2,1,0:T(8,128)(2,1)}, bf16[2,256,256]{2,1,0:T(8,128)(2,1)S(1)}, u32[]{:S(2)}, u32[]{:S(2)}) %collective-permute-start.55) | collective-permute-done | bytes 262176 | tf_op jit(solution)/shard_map/ppermute | solution.py:85
  311.5 2.9 collective-permute-start.38
  317.2 4.4 %qkv_weights.1 = (bf16[2,3,256,256]{3,2,1,0:T(8,128)(2,1)}, bf16[2,3,256,256]{3,2,1,0:T(8,128)(2,1)}, bf16[2,3,256,256]{3,2,1,0:T(8,128)(2,1)}, bf16[2,3,256,256]{3,2,1,0:T(8,128)(2,1)}) custom-call(bf16[4,256,256]{2,1,0:T(8,128)(2,1)} %get-tuple-element.80.kept_ref.refs_0_, bf16[4,256,256]{2,1,0:T(8,128)(2,1)} %copy-done.12, ...), custom_call_target="tpu_custom_call" | custom-call | tf_op jit(solution)/shard_map/qkv_weights/pallas_call | solution.py:41
  321.6 2.0 collective-permute-start.44
  324.7 2.2 collective-permute-start.46
  327.7 11.8 %collective-permute-done.44 = f32[4,2048]{1,0:T(4,128)S(1)} collective-permute-done((f32[4,2048]{1,0:T(4,128)S(1)}, f32[4,2048]{1,0:T(4,128)S(1)}, u32[]{:S(2)}, u32[]{:S(2)}) %collective-permute-start.44) | collective-permute-done | bytes 32800 | tf_op jit(solution)/shard_map/ppermute | solution.py:146
  340.3 11.2 %collective-permute-done.45 = f32[4,2048]{1,0:T(4,128)S(1)} collective-permute-done((f32[4,2048]{1,0:T(4,128)S(1)}, f32[4,2048]{1,0:T(4,128)S(1)}, u32[]{:S(2)}, u32[]{:S(2)}) %collective-permute-start.45) | collective-permute-done | bytes 32800 | tf_op jit(solution)/shard_map/ppermute | solution.py:146
  353.9 10.6 %collective-permute-done.57 = bf16[2,3,256,256]{3,2,1,0:T(8,128)(2,1)S(1)} collective-permute-done((bf16[2,3,256,256]{3,2,1,0:T(8,128)(2,1)S(1)}, bf16[2,3,256,256]{3,2,1,0:T(8,128)(2,1)S(1)}, u32[]{:S(2)}, u32[]{:S(2)}) %collective-permute-start.57) | collective-permute-done | bytes 786464 | tf_op jit(solution)/shard_map/ppermute | solution.py:88
  367.6 2.2 input_grad_rows.1
  369.8 2.6 collective-permute-done.58
  375.8 4.0 %ffn_out.1 = (f32[2,256,1408]{2,1,0:T(8,128)}, f32[1408,256]{1,0:T(8,128)}) custom-call(bf16[768,1408]{1,0:T(8,128)(2,1)} %reduce-scatter.2.cloned.1.call-done.total_ref), custom_call_target="tpu_custom_call" | custom-call | tf_op jit(solution)/shard_map/ffn_out/pallas_call | solution.py:41
  379.8 3.8 all-reduce.2.cloned.1.call-done
  383.6 2.3 copy.34
  (269 shorter events, 60.9 us)
Async XLA Ops:
  7.2 141.2 %all-gather.3.cloned.1.call-start = ((), (), s32[]{:S(2)}) async-start(), calls=%async_computation.3 | async-start | bytes 19464192 | tf_op jit(solution)/shard_map/all_gather | solution.py:606
  7.2 20.8 %collective-permute-start.3 = (bf16[3,256,512]{2,1,0:T(8,128)(2,1)}, bf16[3,256,512]{2,1,0:T(8,128)(2,1)S(1)}, u32[]{:S(2)}, u32[]{:S(2)}) collective-permute-start(bf16[3,256,512]{2,1,0:T(8,128)(2,1)} %refs_0_.4), channel_id=1, source_target_pairs={{0,16},{8,24},{16,0},{24,8},{1,17},{9,25},{17,1},{25,9},{2,18},{10... | collective-permute-start | bytes 2359304 | tf_op jit(solution)/shard_map/ppermute | solution.py:88
  10.2 19.2 %collective-permute-start = (bf16[3,256,512]{2,1,0:T(8,128)(2,1)}, bf16[3,256,512]{2,1,0:T(8,128)(2,1)S(1)}, u32[]{:S(2)}, u32[]{:S(2)}) collective-permute-start(bf16[3,256,512]{2,1,0:T(8,128)(2,1)} %refs_0_.4), channel_id=1, source_target_pairs={{0,4},{4,0},{1,5},{5,1},{2,6},{6,2},{3,7},{7,3},{8,12},{12,8},{9,1... | collective-permute-start | bytes 2359304 | tf_op jit(solution)/shard_map/ppermute | solution.py:85
  29.5 346.4 %reduce-scatter.2.cloned.1.call-start = ((), (), s32[]{:S(2)}) async-start(), calls=%async_computation.2 | async-start | bytes 10813440 | tf_op jit(solution)/shard_map/reduce_scatter | solution.py:670
  29.5 32.5 %collective-permute-start.1 = (bf16[3,256,512]{2,1,0:T(8,128)(2,1)S(1)}, bf16[3,256,512]{2,1,0:T(8,128)(2,1)S(1)}, u32[]{:S(2)}, u32[]{:S(2)}) collective-permute-start(bf16[3,256,512]{2,1,0:T(8,128)(2,1)S(1)} %copy-done.2), channel_id=1, source_target_pairs={{0,8},{8,0},{16,24},{24,16},{1,9},{9,1},{17,25},{25,17},{2,10},{10... | collective-permute-start | bytes 2359304 | tf_op jit(solution)/shard_map/ppermute | solution.py:88
  29.6 11.9 %collective-permute-start.10 = (bf16[512,256]{1,0:T(8,128)(2,1)}, bf16[512,256]{1,0:T(8,128)(2,1)}, u32[]{:S(2)}, u32[]{:S(2)}) collective-permute-start(bf16[512,256]{1,0:T(8,128)(2,1)} %refs_4_), channel_id=1, source_target_pairs={{0,4},{4,0},{1,5},{5,1},{2,6},{6,2},{3,7},{7,3},{8,12},{12,8},{9,1... | collective-permute-start | bytes 786440 | tf_op jit(solution)/shard_map/ppermute | solution.py:85
  40.8 20.1 %collective-permute-start.4 = (bf16[3,256,256]{2,1,0:T(8,128)(2,1)S(1)}, bf16[3,256,256]{2,1,0:T(8,128)(2,1)S(1)}, u32[]{:S(2)}, u32[]{:S(2)}) collective-permute-start(bf16[3,256,256]{2,1,0:T(8,128)(2,1)S(1)} %slice.107), channel_id=1, source_target_pairs={{0,4},{4,0},{1,5},{5,1},{2,6},{6,2},{3,7},{7,3},{8,12},{12,8},{9,1... | collective-permute-start | bytes 1179656 | tf_op jit(solution)/shard_map/ppermute | solution.py:85
  41.2 20.0 %collective-permute-start.5 = (bf16[3,256,256]{2,1,0:T(8,128)(2,1)S(1)}, bf16[3,256,256]{2,1,0:T(8,128)(2,1)S(1)}, u32[]{:S(2)}, u32[]{:S(2)}) collective-permute-start(bf16[3,256,256]{2,1,0:T(8,128)(2,1)S(1)} %slice.108), channel_id=1, source_target_pairs={{0,16},{8,24},{16,0},{24,8},{1,17},{9,25},{17,1},{25,9},{2,18},{10... | collective-permute-start | bytes 1179656 | tf_op jit(solution)/shard_map/ppermute | solution.py:88
  41.5 22.5 %collective-permute-start.2 = (bf16[3,256,512]{2,1,0:T(8,128)(2,1)S(1)}, bf16[3,256,512]{2,1,0:T(8,128)(2,1)S(1)}, u32[]{:S(2)}, u32[]{:S(2)}) collective-permute-start(bf16[3,256,512]{2,1,0:T(8,128)(2,1)S(1)} %collective-permute-done.refs_1_), channel_id=1, source_target_pairs={{0,8},{8,0},{16,24},{24,16},{1,9},{9,1},{17,25},{25,17},{2,10},{10... | collective-permute-start | bytes 2359304 | tf_op jit(solution)/shard_map/ppermute | solution.py:88
  41.6 22.5 %collective-permute-start.6 = (bf16[3,256,512]{2,1,0:T(8,128)(2,1)S(1)}, bf16[3,256,512]{2,1,0:T(8,128)(2,1)S(1)}, u32[]{:S(2)}, u32[]{:S(2)}) collective-permute-start(bf16[3,256,512]{2,1,0:T(8,128)(2,1)S(1)} %collective-permute-done.3.refs_4_), channel_id=1, source_target_pairs={{0,8},{8,0},{16,24},{24,16},{1,9},{9,1},{17,25},{25,17},{2,10},{10... | collective-permute-start | bytes 2359304 | tf_op jit(solution)/shard_map/ppermute | solution.py:88
  62.0 15.0 %collective-permute-start.13 = (bf16[512,256]{1,0:T(8,128)(2,1)}, bf16[512,256]{1,0:T(8,128)(2,1)S(1)}, u32[]{:S(2)}, u32[]{:S(2)}) collective-permute-start(bf16[512,256]{1,0:T(8,128)(2,1)} %refs_4_), channel_id=1, source_target_pairs={{0,16},{8,24},{16,0},{24,8},{1,17},{9,25},{17,1},{25,9},{2,18},{10... | collective-permute-start | bytes 786440 | tf_op jit(solution)/shard_map/ppermute | solution.py:88
  62.6 21.9 %collective-permute-start.14 = (bf16[512,256]{1,0:T(8,128)(2,1)}, bf16[512,256]{1,0:T(8,128)(2,1)S(1)}, u32[]{:S(2)}, u32[]{:S(2)}) collective-permute-start(bf16[512,256]{1,0:T(8,128)(2,1)} %collective-permute-done.10.refs_1_.refs_5_), channel_id=1, source_target_pairs={{0,16},{8,24},{16,0},{24,8},{1,17},{9,25},{17,1},{25,9},{2,18},{10... | collective-permute-start | bytes 786440 | tf_op jit(solution)/shard_map/ppermute | solution.py:88
  71.9 15.0 %collective-permute-start.9 = (bf16[2,256,512]{2,1,0:T(8,128)(2,1)}, bf16[2,256,512]{2,1,0:T(8,128)(2,1)S(1)}, u32[]{:S(2)}, u32[]{:S(2)}) collective-permute-start(bf16[2,256,512]{2,1,0:T(8,128)(2,1)} %get-tuple-element.86.here_ref), channel_id=1, source_target_pairs={{0,4},{1,5},{2,6},{3,7},{8,12},{9,13},{10,14},{11,15},{16,20},{17,... | collective-permute-start | bytes 1572872 | tf_op jit(solution)/shard_map/ppermute | solution.py:614
  96.3 12.4 %collective-permute-start.17 = (bf16[8,64,256]{2,1,0:T(8,128)(2,1)}, bf16[8,64,256]{2,1,0:T(8,128)(2,1)S(1)}, u32[]{:S(2)}, u32[]{:S(2)}) collective-permute-start(bf16[8,64,256]{2,1,0:T(8,128)(2,1)} %get-tuple-element.90), channel_id=1, source_target_pairs={{0,1},{1,0},{2,3},{3,2},{4,5},{5,4},{6,7},{7,6},{8,9},{9,8},{10,11... | collective-permute-start | bytes 786440 | tf_op jit(solution)/shard_map/ppermute | solution.py:146
  97.8 21.6 %collective-permute-start.18 = (bf16[8,64,256]{2,1,0:T(8,128)(2,1)}, bf16[8,64,256]{2,1,0:T(8,128)(2,1)S(1)}, u32[]{:S(2)}, u32[]{:S(2)}) collective-permute-start(bf16[8,64,256]{2,1,0:T(8,128)(2,1)} %get-tuple-element.91), channel_id=1, source_target_pairs={{0,2},{1,3},{2,0},{3,1},{4,6},{5,7},{6,4},{7,5},{8,10},{9,11},{10,... | collective-permute-start | bytes 786440 | tf_op jit(solution)/shard_map/ppermute | solution.py:146
  100.5 18.9 %collective-permute-start.19 = (bf16[8,64,256]{2,1,0:T(8,128)(2,1)}, bf16[8,64,256]{2,1,0:T(8,128)(2,1)S(1)}, u32[]{:S(2)}, u32[]{:S(2)}) collective-permute-start(bf16[8,64,256]{2,1,0:T(8,128)(2,1)} %get-tuple-element.92), channel_id=1, source_target_pairs={{0,3},{1,2},{2,1},{3,0},{4,7},{5,6},{6,5},{7,4},{8,11},{9,10},{10,... | collective-permute-start | bytes 786440 | tf_op jit(solution)/shard_map/ppermute | solution.py:146
  122.9 13.0 %collective-permute-start.20 = (bf16[8,64,256]{2,1,0:T(8,128)(2,1)}, bf16[8,64,256]{2,1,0:T(8,128)(2,1)S(1)}, u32[]{:S(2)}, u32[]{:S(2)}) collective-permute-start(bf16[8,64,256]{2,1,0:T(8,128)(2,1)} %get-tuple-element.93.refs_0_), channel_id=1, source_target_pairs={{0,1},{1,0},{2,3},{3,2},{4,5},{5,4},{6,7},{7,6},{8,9},{9,8},{10,11... | collective-permute-start | bytes 786440 | tf_op jit(solution)/shard_map/ppermute | solution.py:146
  127.0 21.4 %collective-permute-start.21 = (bf16[8,64,256]{2,1,0:T(8,128)(2,1)}, bf16[8,64,256]{2,1,0:T(8,128)(2,1)S(1)}, u32[]{:S(2)}, u32[]{:S(2)}) collective-permute-start(bf16[8,64,256]{2,1,0:T(8,128)(2,1)} %get-tuple-element.93.refs_0_), channel_id=1, source_target_pairs={{0,2},{1,3},{2,0},{3,1},{4,6},{5,7},{6,4},{7,5},{8,10},{9,11},{10,... | collective-permute-start | bytes 786440 | tf_op jit(solution)/shard_map/ppermute | solution.py:146
  128.0 20.4 %collective-permute-start.22 = (bf16[8,64,256]{2,1,0:T(8,128)(2,1)}, bf16[8,64,256]{2,1,0:T(8,128)(2,1)S(1)}, u32[]{:S(2)}, u32[]{:S(2)}) collective-permute-start(bf16[8,64,256]{2,1,0:T(8,128)(2,1)} %get-tuple-element.93.refs_0_), channel_id=1, source_target_pairs={{0,3},{1,2},{2,1},{3,0},{4,7},{5,6},{6,5},{7,4},{8,11},{9,10},{10,... | collective-permute-start | bytes 786440 | tf_op jit(solution)/shard_map/ppermute | solution.py:146
  165.3 16.5 %collective-permute-start.26 = (bf16[256,1408]{1,0:T(8,128)(2,1)}, bf16[256,1408]{1,0:T(8,128)(2,1)S(1)}, u32[]{:S(2)}, u32[]{:S(2)}) collective-permute-start(bf16[256,1408]{1,0:T(8,128)(2,1)} %get-tuple-element.103.refs_6_), channel_id=1, source_target_pairs={{0,8},{8,0},{16,24},{24,16},{1,9},{9,1},{17,25},{25,17},{2,10},{10... | collective-permute-start | bytes 2162696 | tf_op jit(solution)/shard_map/ppermute | solution.py:88
  165.8 16.1 %collective-permute-start.27 = (bf16[256,1408]{1,0:T(8,128)(2,1)}, bf16[256,1408]{1,0:T(8,128)(2,1)S(1)}, u32[]{:S(2)}, u32[]{:S(2)}) collective-permute-start(bf16[256,1408]{1,0:T(8,128)(2,1)} %get-tuple-element.95.hidden_ref.refs_8_), channel_id=1, source_target_pairs={{0,8},{8,0},{16,24},{24,16},{1,9},{9,1},{17,25},{25,17},{2,10},{10... | collective-permute-start | bytes 2162696 | tf_op jit(solution)/shard_map/ppermute | solution.py:88
  168.3 25.3 %collective-permute-start.28 = (bf16[8,64,256]{2,1,0:T(8,128)(2,1)}, bf16[8,64,256]{2,1,0:T(8,128)(2,1)S(1)}, u32[]{:S(2)}, u32[]{:S(2)}) collective-permute-start(bf16[8,64,256]{2,1,0:T(8,128)(2,1)} %get-tuple-element.105), channel_id=1, source_target_pairs={{0,1},{1,0},{2,3},{3,2},{4,5},{5,4},{6,7},{7,6},{8,9},{9,8},{10,11... | collective-permute-start | bytes 786440 | tf_op jit(solution)/shard_map/ppermute | solution.py:146
  171.7 22.0 %collective-permute-start.29 = (bf16[8,64,256]{2,1,0:T(8,128)(2,1)}, bf16[8,64,256]{2,1,0:T(8,128)(2,1)}, u32[]{:S(2)}, u32[]{:S(2)}) collective-permute-start(bf16[8,64,256]{2,1,0:T(8,128)(2,1)} %get-tuple-element.106), channel_id=1, source_target_pairs={{0,2},{1,3},{2,0},{3,1},{4,6},{5,7},{6,4},{7,5},{8,10},{9,11},{10,... | collective-permute-start | bytes 786440 | tf_op jit(solution)/shard_map/ppermute | solution.py:146
  172.8 20.8 %collective-permute-start.30 = (bf16[8,64,256]{2,1,0:T(8,128)(2,1)}, bf16[8,64,256]{2,1,0:T(8,128)(2,1)}, u32[]{:S(2)}, u32[]{:S(2)}) collective-permute-start(bf16[8,64,256]{2,1,0:T(8,128)(2,1)} %get-tuple-element.107), channel_id=1, source_target_pairs={{0,3},{1,2},{2,1},{3,0},{4,7},{5,6},{6,5},{7,4},{8,11},{9,10},{10,... | collective-permute-start | bytes 786440 | tf_op jit(solution)/shard_map/ppermute | solution.py:146
  197.6 14.2 %collective-permute-start.31 = (bf16[8,64,256]{2,1,0:T(8,128)(2,1)}, bf16[8,64,256]{2,1,0:T(8,128)(2,1)S(1)}, u32[]{:S(2)}, u32[]{:S(2)}) collective-permute-start(bf16[8,64,256]{2,1,0:T(8,128)(2,1)} %get-tuple-element.110.refs_0_), channel_id=1, source_target_pairs={{0,1},{1,0},{2,3},{3,2},{4,5},{5,4},{6,7},{7,6},{8,9},{9,8},{10,11... | collective-permute-start | bytes 786440 | tf_op jit(solution)/shard_map/ppermute | solution.py:146
  201.6 21.6 %collective-permute-start.32 = (bf16[8,64,256]{2,1,0:T(8,128)(2,1)}, bf16[8,64,256]{2,1,0:T(8,128)(2,1)S(1)}, u32[]{:S(2)}, u32[]{:S(2)}) collective-permute-start(bf16[8,64,256]{2,1,0:T(8,128)(2,1)} %get-tuple-element.110.refs_0_), channel_id=1, source_target_pairs={{0,2},{1,3},{2,0},{3,1},{4,6},{5,7},{6,4},{7,5},{8,10},{9,11},{10,... | collective-permute-start | bytes 786440 | tf_op jit(solution)/shard_map/ppermute | solution.py:146
  202.5 20.7 %collective-permute-start.33 = (bf16[8,64,256]{2,1,0:T(8,128)(2,1)}, bf16[8,64,256]{2,1,0:T(8,128)(2,1)S(1)}, u32[]{:S(2)}, u32[]{:S(2)}) collective-permute-start(bf16[8,64,256]{2,1,0:T(8,128)(2,1)} %get-tuple-element.110.refs_0_), channel_id=1, source_target_pairs={{0,3},{1,2},{2,1},{3,0},{4,7},{5,6},{6,5},{7,4},{8,11},{9,10},{10,... | collective-permute-start | bytes 786440 | tf_op jit(solution)/shard_map/ppermute | solution.py:146
  204.1 179.5 %all-reduce.2.cloned.1.call-start = ((), (), s32[]{:S(2)}) async-start(), calls=%async_computation.1 | async-start | bytes 2097152 | tf_op jit(solution)/shard_map/psum | solution.py:669
  234.1 26.3 %collective-permute-start.34 = (bf16[2,256,512]{2,1,0:T(8,128)(2,1)}, bf16[2,256,512]{2,1,0:T(8,128)(2,1)S(1)}, u32[]{:S(2)}, u32[]{:S(2)}) collective-permute-start(bf16[2,256,512]{2,1,0:T(8,128)(2,1)} %get-tuple-element.113), channel_id=1, source_target_pairs={{4,0},{5,1},{6,2},{7,3},{12,8},{13,9},{14,10},{15,11},{20,16},{21,... | collective-permute-start | bytes 1572872 | tf_op jit(solution)/shard_map/ppermute | solution.py:693
  235.7 59.7 %collective-permute-start.51 = (bf16[256,512]{1,0:T(8,128)(2,1)S(1)}, bf16[256,512]{1,0:T(8,128)(2,1)S(1)}, u32[]{:S(2)}, u32[]{:S(2)}) collective-permute-start(bf16[256,512]{1,0:T(8,128)(2,1)S(1)} %copy-done.38), channel_id=1, source_target_pairs={{0,8},{8,0},{16,24},{24,16},{1,9},{9,1},{17,25},{25,17},{2,10},{10... | collective-permute-start | bytes 786440 | tf_op jit(solution)/shard_map/ppermute | solution.py:88
  235.7 59.6 %collective-permute-start.52 = (bf16[4,256,256]{2,1,0:T(8,128)(2,1)}, bf16[4,256,256]{2,1,0:T(8,128)(2,1)S(1)}, u32[]{:S(2)}, u32[]{:S(2)}) collective-permute-start(bf16[4,256,256]{2,1,0:T(8,128)(2,1)} %get-tuple-element.131), channel_id=1, source_target_pairs={{0,8},{8,0},{16,24},{24,16},{1,9},{9,1},{17,25},{25,17},{2,10},{10... | collective-permute-start | bytes 1572872 | tf_op jit(solution)/shard_map/ppermute | solution.py:88
  269.6 12.0 %collective-permute-start.35 = (bf16[8,64,256]{2,1,0:T(8,128)(2,1)}, bf16[8,64,256]{2,1,0:T(8,128)(2,1)S(1)}, u32[]{:S(2)}, u32[]{:S(2)}) collective-permute-start(bf16[8,64,256]{2,1,0:T(8,128)(2,1)} %get-tuple-element.115), channel_id=1, source_target_pairs={{0,1},{1,0},{2,3},{3,2},{4,5},{5,4},{6,7},{7,6},{8,9},{9,8},{10,11... | collective-permute-start | bytes 786440 | tf_op jit(solution)/shard_map/ppermute | solution.py:146
  274.2 20.4 %collective-permute-start.36 = (bf16[8,64,256]{2,1,0:T(8,128)(2,1)}, bf16[8,64,256]{2,1,0:T(8,128)(2,1)S(1)}, u32[]{:S(2)}, u32[]{:S(2)}) collective-permute-start(bf16[8,64,256]{2,1,0:T(8,128)(2,1)} %get-tuple-element.116), channel_id=1, source_target_pairs={{0,2},{1,3},{2,0},{3,1},{4,6},{5,7},{6,4},{7,5},{8,10},{9,11},{10,... | collective-permute-start | bytes 786440 | tf_op jit(solution)/shard_map/ppermute | solution.py:146
  275.0 19.6 %collective-permute-start.37 = (bf16[8,64,256]{2,1,0:T(8,128)(2,1)}, bf16[8,64,256]{2,1,0:T(8,128)(2,1)S(1)}, u32[]{:S(2)}, u32[]{:S(2)}) collective-permute-start(bf16[8,64,256]{2,1,0:T(8,128)(2,1)} %get-tuple-element.117), channel_id=1, source_target_pairs={{0,3},{1,2},{2,1},{3,0},{4,7},{5,6},{6,5},{7,4},{8,11},{9,10},{10,... | collective-permute-start | bytes 786440 | tf_op jit(solution)/shard_map/ppermute | solution.py:146
  295.3 14.0 %collective-permute-start.47 = (bf16[4,256,256]{2,1,0:T(8,128)(2,1)S(1)}, bf16[4,256,256]{2,1,0:T(8,128)(2,1)S(1)}, u32[]{:S(2)}, u32[]{:S(2)}) collective-permute-start(bf16[4,256,256]{2,1,0:T(8,128)(2,1)S(1)} %copy-done.46), channel_id=1, source_target_pairs={{0,8},{8,0},{16,24},{24,16},{1,9},{9,1},{17,25},{25,17},{2,10},{10... | collective-permute-start | bytes 1572872 | tf_op jit(solution)/shard_map/ppermute | solution.py:88
  299.1 9.7 %collective-permute-start.55 = (bf16[2,256,256]{2,1,0:T(8,128)(2,1)}, bf16[2,256,256]{2,1,0:T(8,128)(2,1)S(1)}, u32[]{:S(2)}, u32[]{:S(2)}) collective-permute-start(bf16[2,256,256]{2,1,0:T(8,128)(2,1)} %get-tuple-element.138), channel_id=1, source_target_pairs={{0,4},{4,0},{1,5},{5,1},{2,6},{6,2},{3,7},{7,3},{8,12},{12,8},{9,1... | collective-permute-start | bytes 786440 | tf_op jit(solution)/shard_map/ppermute | solution.py:85
  301.1 9.8 %collective-permute-start.53 = (bf16[2,256,256]{2,1,0:T(8,128)(2,1)}, bf16[2,256,256]{2,1,0:T(8,128)(2,1)S(1)}, u32[]{:S(2)}, u32[]{:S(2)}) collective-permute-start(bf16[2,256,256]{2,1,0:T(8,128)(2,1)} %get-tuple-element.134), channel_id=1, source_target_pairs={{0,16},{8,24},{16,0},{24,8},{1,17},{9,25},{17,1},{25,9},{2,18},{10... | collective-permute-start | bytes 786440 | tf_op jit(solution)/shard_map/ppermute | solution.py:88
  301.1 10.4 %collective-permute-start.48 = (bf16[256,512]{1,0:T(8,128)(2,1)S(1)}, bf16[256,512]{1,0:T(8,128)(2,1)S(1)}, u32[]{:S(2)}, u32[]{:S(2)}) collective-permute-start(bf16[256,512]{1,0:T(8,128)(2,1)S(1)} %copy-done.30), channel_id=1, source_target_pairs={{0,8},{8,0},{16,24},{24,16},{1,9},{9,1},{17,25},{25,17},{2,10},{10... | collective-permute-start | bytes 786440 | tf_op jit(solution)/shard_map/ppermute | solution.py:88
  309.4 14.9 %collective-permute-start.56 = (bf16[1,256,256]{2,1,0:T(8,128)(2,1)S(1)}, bf16[1,256,256]{2,1,0:T(8,128)(2,1)S(1)}, u32[]{:S(2)}, u32[]{:S(2)}) collective-permute-start(bf16[1,256,256]{2,1,0:T(8,128)(2,1)S(1)} %add_convert_fusion.2), channel_id=1, source_target_pairs={{0,16},{8,24},{16,0},{24,8},{1,17},{9,25},{17,1},{25,9},{2,18},{10... | collective-permute-start | bytes 393224 | tf_op jit(solution)/shard_map/ppermute | solution.py:88
  310.9 10.7 %collective-permute-start.43 = (f32[9728]{0:T(1024)S(1)}, f32[9728]{0:T(1024)S(1)}, u32[]{:S(2)}, u32[]{:S(2)}) collective-permute-start(f32[9728]{0:T(1024)S(1)} %add.129), channel_id=1, source_target_pairs={{0,16},{8,24},{16,0},{24,8},{1,17},{9,25},{17,1},{25,9},{2,18},{10... | collective-permute-start | bytes 116744 | tf_op jit(solution)/shard_map/ppermute | solution.py:88
  311.5 55.3 %collective-permute-start.38 = (bf16[8,64,256]{2,1,0:T(8,128)(2,1)}, bf16[8,64,256]{2,1,0:T(8,128)(2,1)}, u32[]{:S(2)}, u32[]{:S(2)}) collective-permute-start(bf16[8,64,256]{2,1,0:T(8,128)(2,1)} %input_grad.1.refs_0_), channel_id=1, source_target_pairs={{0,1},{1,0},{2,3},{3,2},{4,5},{5,4},{6,7},{7,6},{8,9},{9,8},{10,11... | collective-permute-start | bytes 786440 | tf_op jit(solution)/shard_map/ppermute | solution.py:146
  314.5 52.4 %collective-permute-start.39 = (bf16[8,64,256]{2,1,0:T(8,128)(2,1)}, bf16[8,64,256]{2,1,0:T(8,128)(2,1)}, u32[]{:S(2)}, u32[]{:S(2)}) collective-permute-start(bf16[8,64,256]{2,1,0:T(8,128)(2,1)} %input_grad.1.refs_0_), channel_id=1, source_target_pairs={{0,2},{1,3},{2,0},{3,1},{4,6},{5,7},{6,4},{7,5},{8,10},{9,11},{10,... | collective-permute-start | bytes 786440 | tf_op jit(solution)/shard_map/ppermute | solution.py:146
  321.6 17.9 %collective-permute-start.44 = (f32[4,2048]{1,0:T(4,128)S(1)}, f32[4,2048]{1,0:T(4,128)S(1)}, u32[]{:S(2)}, u32[]{:S(2)}) collective-permute-start(f32[4,2048]{1,0:T(4,128)S(1)} %reshape.330), channel_id=1, source_target_pairs={{0,1},{1,0},{2,3},{3,2},{4,5},{5,4},{6,7},{7,6},{8,9},{9,8},{10,11... | collective-permute-start | bytes 98312 | tf_op jit(solution)/shard_map/ppermute | solution.py:146
  324.3 27.2 %collective-permute-start.45 = (f32[4,2048]{1,0:T(4,128)S(1)}, f32[4,2048]{1,0:T(4,128)S(1)}, u32[]{:S(2)}, u32[]{:S(2)}) collective-permute-start(f32[4,2048]{1,0:T(4,128)S(1)} %reshape.330), channel_id=1, source_target_pairs={{0,2},{1,3},{2,0},{3,1},{4,6},{5,7},{6,4},{7,5},{8,10},{9,11},{10,... | collective-permute-start | bytes 98312 | tf_op jit(solution)/shard_map/ppermute | solution.py:146
  324.7 27.1 %collective-permute-start.46 = (f32[4,2048]{1,0:T(4,128)S(1)}, f32[4,2048]{1,0:T(4,128)S(1)}, u32[]{:S(2)}, u32[]{:S(2)}) collective-permute-start(f32[4,2048]{1,0:T(4,128)S(1)} %reshape.330), channel_id=1, source_target_pairs={{0,3},{1,2},{2,1},{3,0},{4,7},{5,6},{6,5},{7,4},{8,11},{9,10},{10,... | collective-permute-start | bytes 98312 | tf_op jit(solution)/shard_map/ppermute | solution.py:146
  339.5 27.3 %collective-permute-start.40 = (bf16[8,64,256]{2,1,0:T(8,128)(2,1)S(1)}, bf16[8,64,256]{2,1,0:T(8,128)(2,1)S(1)}, u32[]{:S(2)}, u32[]{:S(2)}) collective-permute-start(bf16[8,64,256]{2,1,0:T(8,128)(2,1)S(1)} %copy-done.48), channel_id=1, source_target_pairs={{0,3},{1,2},{2,1},{3,0},{4,7},{5,6},{6,5},{7,4},{8,11},{9,10},{10,... | collective-permute-start | bytes 786440 | tf_op jit(solution)/shard_map/ppermute | solution.py:146
  351.5 13.0 %collective-permute-start.57 = (bf16[2,3,256,256]{3,2,1,0:T(8,128)(2,1)S(1)}, bf16[2,3,256,256]{3,2,1,0:T(8,128)(2,1)S(1)}, u32[]{:S(2)}, u32[]{:S(2)}) collective-permute-start(bf16[2,3,256,256]{3,2,1,0:T(8,128)(2,1)S(1)} %copy-done.45), channel_id=1, source_target_pairs={{0,16},{8,24},{16,0},{24,8},{1,17},{9,25},{17,1},{25,9},{2,18},{10... | collective-permute-start | bytes 2359304 | tf_op jit(solution)/shard_map/ppermute | solution.py:88
  351.7 14.7 %collective-permute-start.59 = (bf16[2,3,256,256]{3,2,1,0:T(8,128)(2,1)S(1)}, bf16[2,3,256,256]{3,2,1,0:T(8,128)(2,1)S(1)}, u32[]{:S(2)}, u32[]{:S(2)}) collective-permute-start(bf16[2,3,256,256]{3,2,1,0:T(8,128)(2,1)S(1)} %copy-done.44), channel_id=1, source_target_pairs={{0,4},{4,0},{1,5},{5,1},{2,6},{6,2},{3,7},{7,3},{8,12},{12,8},{9,1... | collective-permute-start | bytes 2359304 | tf_op jit(solution)/shard_map/ppermute | solution.py:85
  (76 other events, 656.9 us)
Sparse Core Ops, SparseCore 0:
  29.6 108.1 all-gather.2
  204.2 101.0 reduce-scatter.1
  307.7 75.8 all-reduce.1

commit v3 on v2

--- a/solution.py
+++ b/solution.py
@@ -24,7 +24,10 @@
     return jax.ShapeDtypeStruct(tuple(dims), dtype)
 
 
-WEIGHT = dict(qkv=10, mid=20, mid_back=60, attend_back=200, input_grad=20, input_grad_rows=20)
+WEIGHT = dict(
+    norm_one=5, cotangent_rows=5, qkv=10, mid=250, mid_back=60, attend_back=200, block_out=5,
+    input_grad=8, input_grad_rows=8,
+)
 
 
 def params(name):
@@ -79,66 +82,39 @@
         squeeze = lambda d: (d & low) | ((d >> 1) & ~low)
         return squeeze(self.me) ^ squeeze(k)
 
-    def swap(self, value, bit):
-        if bit < self.context:
-            pairs = [(i, i ^ bit) for i in range(self.context)]
-            return lax.ppermute(value, "context", pairs)
-        step = bit // self.context
-        pairs = [(i, i ^ step) for i in range(self.fsdp)]
-        return lax.ppermute(value, "fsdp", pairs)
+    def swap(self, value, mask):
+        pairs = [(i, i ^ mask) for i in range(self.count)]
+        return lax.ppermute(value, ("fsdp", "context"), pairs)
 
     def across(self, value):
         return jax.tree.map(lambda v: self.swap(v, self.core), value)
 
-    def gather(self, shard, order, *after):
-        slots = {0: shard}
-        for bit in order + [self.core]:
-            for k in list(slots):
-                wait = after if k and bit != self.core else ()
-                slots[k ^ bit] = self.swap(tie(slots[k], wait) if wait else slots[k], bit)
+    def gather(self, shard, *after):
+        slots = {k: self.swap(shard, k) if k else shard for k in self.kept}
+        for k in self.kept:
+            value = tie(slots[k], after) if after and k == self.kept[-1] else slots[k]
+            slots[k ^ self.core] = self.across(value)
         return slots
-
-    def gather_halves(self, shard, *prepared):
-        if len(self.up) != 2:
-            return {k: (v,) for k, v in self.gather(shard, self.up).items()}
-        y, x = self.up
-        half = shard.shape[-1] // 2
-        over_x, over_y = self.swap(shard, x), self.swap(shard, y)
-        first, second = tie((over_x[..., :half], over_y[..., half:]), prepared)
-        both = (self.swap(first, y), self.swap(second, x))
-        slots = {0: (shard,), x: (over_x,), y: (over_y,), x ^ y: both}
-        return slots | {k ^ self.core: self.across(v) for k, v in slots.items()}
 
     def halves(self, order):
         slots = sorted(self.kept, key=lambda k: tuple(not k & bit for bit in order))
         return slots[: len(slots) // 2], slots[len(slots) // 2 :]
 
-    def total(self, value):
-        bit = 1
-        while bit < self.count:
+    def chip_total(self, value):
+        for bit in self.up:
             value = value + self.swap(value, bit)
-            bit *= 2
         return value
 
 
-class Scatter:
-    def __init__(self, plane, first, second, order):
-        self.plane, self.order = plane, list(order)
-        self.low, self.terms = first, [second]
-
-    def step(self, *after):
-        got = self.plane.swap(tie(self.low, after), self.order.pop(0))
-        self.terms.append(got)
-        if self.order:
-            rest = got.shape[0] // 2
-            self.low = sum(t[:rest].astype(f32) for t in self.terms).astype(bf16)
-            self.terms = [t[rest:] for t in self.terms]
-        return got
-
-    def total(self, *after):
-        while self.order:
-            self.step(*after)
-        return sum(t[0].astype(f32) for t in self.terms)
+def scatter(plane, first, second, order):
+    low, terms = first, [second]
+    for bit in order:
+        terms.append(plane.swap(low, bit))
+        rest = terms[-1].shape[0] // 2
+        if rest:
+            pick = lambda t: t[t.shape[0] - 2 * rest :][:rest].astype(f32)
+            low = sum(pick(t) for t in terms).astype(bf16)
+    return terms
 
 
 def tensor_swap(value, j):
@@ -202,24 +178,15 @@
     return jnp.concatenate(parts, axis=1)
 
 
-def take(refs, lengths):
-    groups, at = [], 0
-    for n in lengths:
-        groups.append(refs[at : at + n])
-        at += n
-    return groups, refs[at:]
-
-
-def qkv_kernel(slots, pieces, kept_ref, sent_ref, bias_ref, table_ref, *refs):
-    weights, (q_ref, kv_ref) = take(refs, pieces)
+def qkv_kernel(slots, kept_ref, sent_ref, bias_ref, table_ref, *refs):
+    weights, (q_ref, kv_ref) = refs[:-2], refs[-2:]
     feat = q_ref.shape[1]
     x = {k: ref[i] for ref, which in zip((kept_ref, sent_ref), slots) for i, k in enumerate(which)}
     for cols in tiles(feat):
         for j in range(3):
             total = bias_ref[j, :, cols]
-            for k, parts in enumerate(weights):
-                part, at = parts[cols.start * len(parts) // feat], cols.start % (feat // len(parts))
-                total = total + dot(x[k], part[j, :, at : at + cols.stop - cols.start])
+            for k, weight in enumerate(weights):
+                total = total + dot(x[k], weight[j, :, cols])
             if j < 2:
                 total = spin(total, table_ref[...], 1)
             if j == 0:
@@ -317,10 +284,9 @@
 
 def ffn_kernel(slots, peers, order_ref, *refs):
     blocks = refs[:peers]
-    cot_ref, all_ref, kept_ref, sent_ref, hidden_ref, gate_grad_ref, up_grad_ref, own_ref = refs[
-        peers : peers + 8
-    ]
-    sends, (gate, up, down, sems, x_ref, pre_ref) = refs[peers + 8 : -6], refs[-6:]
+    cot_ref, all_ref, kept_ref, sent_ref, three_ref, own_ref = refs[peers : peers + 6]
+    gate_grad_ref, up_grad_ref, hidden_ref = (three_ref.at[i] for i in range(3))
+    sends, (gate, up, down, sems, x_ref, pre_ref) = refs[peers + 6 : -6], refs[-6:]
     copies = [fetch(all_ref, i, ref, sems.at[i]) for i, ref in enumerate((gate, up, down))]
     rows, width = own_ref.shape[1:]
     for j, ref in enumerate(blocks):
@@ -361,24 +327,28 @@
         ref[n] = total[(j + 1) * rows : (j + 2) * rows].astype(bf16)
 
 
-def down_kernel(at_ref, hidden_ref, all_ref, mid_ref, out_ref, down, sem):
+def down_kernel(three_ref, all_ref, own_ref, *refs):
+    sends, (down, sem) = refs[:-2], refs[-2:]
+    hidden_ref = three_ref.at[2]
     for copy in fetch(all_ref, 2, down, sem):
         copy.wait()
-    count, rows, width = mid_ref.shape
+    count, _, width = own_ref.shape
     for n in range(count):
-        at = slice(n * width, (n + 1) * width)
-        total = dot(hidden_ref[...], down[at], NT)
-        for j in range(at_ref.shape[0]):
-            block = total[j * rows : (j + 1) * rows]
-            block = block + mid_ref[n] if j == 0 else block
-            out_ref[pl.ds(pl.multiple_of(at_ref[j] * rows, rows), rows), at] = block.astype(bf16)
+        cut(n, dot(hidden_ref[...], down[n * width : (n + 1) * width], NT), own_ref, sends)
+
+
+def block_out_kernel(mid_ref, own_ref, *refs):
+    total = mid_ref[...] + own_ref[...]
+    for ref in refs[:-1]:
+        total = total + ref[...].astype(f32)
+    refs[-1][...] = total.astype(bf16)
 
 
 def ffn_weights_kernel(place_ref, *refs):
-    x, cot, grads, out_ref = refs[:2], refs[2:4], refs[4:10], refs[10]
+    x, cot, grads, out_ref = refs[:2], refs[2:4], refs[4:6], refs[6]
     width = x[0].shape[2]
     for i, left in enumerate((x, x, cot)):
-        total = dot(left[0][0], grads[2 * i][...], TN) + dot(left[1][0], grads[2 * i + 1][...], TN)
+        total = dot(left[0][0], grads[0][i], TN) + dot(left[1][0], grads[1][i], TN)
         out_ref[i * width : (i + 1) * width] = total.astype(bf16)
 
 
@@ -457,67 +427,74 @@
             dhere_ref[i - 1, :, cols] = both[rows:]
 
 
-def out_weights_kernel(slots, halves, *refs):
-    att, low, outs = refs[:2], refs[2:4], refs[4:]
+def one_grad_kernel(
+    order_ref, at_ref, x_ref, table_ref, dq_ref, dhere_ref, dback_ref, *refs
+):
+    count = order_ref.shape[0]
+    weights, refs = refs[:count], refs[count:]
+    ffn_gain_ref, ffn_bias_ref, back_ref, small_ref, own_ref = refs[:5]
+    sends, part_ref = refs[5:-1], refs[-1]
+    width = own_ref.shape[2]
+    back_refs = [back_ref.at[j] for j in range(3)]
+    back_refs[0][...] = dq_ref[...]
+    dk = dhere_ref[0] + dback_ref[0].astype(f32)
+    back_refs[1][...] = spin(dk, table_ref[...], -1).astype(bf16)
+    back_refs[2][...] = (dhere_ref[1] + dback_ref[1].astype(f32)).astype(bf16)
+    row = 4 * count
+    for ref in back_refs:
+        bias = jnp.sum(ref[...].astype(f32), axis=0, keepdims=True)
+        for at in range(0, ref.shape[1], width):
+            small_ref[row : row + 1] = bias[:, at : at + width]
+            row += 1
+    for k, weight in enumerate(weights):
+        part_ref[order_ref[k]] = sum(dot(ref[...], weight[j], NT) for j, ref in enumerate(back_refs))
+    normal, _ = row_stats(split(x_ref[...].astype(f32), count))
+    small_ref[:count] = token_sum(part_ref[...] * normal)[:, 0]
+    small_ref[count : 2 * count] = token_sum(part_ref[...])[:, 0]
+    small_ref[2 * count : 3 * count] = ffn_gain_ref[:, 0]
+    small_ref[3 * count : 4 * count] = ffn_bias_ref[:, 0]
+    hand_out(at_ref, part_ref, own_ref, sends)
+
+
+def attention_weights_kernel(slots, halves, *refs):
+    x, back, low, att, outs = refs[:2], refs[2:4], refs[4:6], refs[6:8], refs[8:]
     part = att[0].shape[1] // 2
     for h, both in enumerate(halves):
         cols = slice(h * part, (h + 1) * part)
         for ref, which in zip(outs[2 * h :], both):
             for i, k in enumerate(which):
                 at = slots[0].index(k)
-                total = dot(att[0][:, cols], low[0][at], TN) + dot(att[1][:, cols], low[1][at], TN)
-                ref[i] = total.astype(bf16)
-
-
-def one_grad_kernel(
-    pieces, order_ref, at_ref, x_ref, table_ref, dq_ref, dhere_ref, dback_ref, *refs
-):
-    weights, refs = take(refs, pieces)
-    *back_refs, bias_ref, gain_grad_ref, norm_bias_ref, own_ref = refs[:7]
-    sends, part_ref = refs[7:-1], refs[-1]
-    back_refs[0][...] = dq_ref[...]
-    dk = dhere_ref[0] + dback_ref[0].astype(f32)
-    back_refs[1][...] = spin(dk, table_ref[...], -1).astype(bf16)
-    back_refs[2][...] = (dhere_ref[1] + dback_ref[1].astype(f32)).astype(bf16)
-    for j, ref in enumerate(back_refs):
-        bias_ref[j] = jnp.sum(ref[...].astype(f32), axis=0, keepdims=True)
-    for k, parts in enumerate(weights):
-        total, at = None, 0
-        for part in parts:
-            size = part.shape[2]
-            for j, ref in enumerate(back_refs):
-                term = dot(ref[:, at : at + size], part[j], NT)
-                total = term if total is None else total + term
-            at += size
-        part_ref[order_ref[k]] = total
-    normal, _ = row_stats(split(x_ref[...].astype(f32), len(weights)))
-    gain_grad_ref[...] = token_sum(part_ref[...] * normal)
-    norm_bias_ref[...] = token_sum(part_ref[...])
-    hand_out(at_ref, part_ref, own_ref, sends)
-
-
-def qkv_weights_kernel(slots, halves, *refs):
-    x, grads, outs = refs[:2], refs[2:8], refs[8:]
-    part = grads[0].shape[1] // 2
-    for h, both in enumerate(halves):
+                for j in range(4):
+                    left = x if j < 3 else low
+                    right = [b[j, :, cols] for b in back] if j < 3 else [a[:, cols] for a in att]
+                    total = dot(left[0][at], right[0], TN) + dot(left[1][at], right[1], TN)
+                    ref[i, j] = total.astype(bf16)
+
+
+def attention_out_kernel(terms, *refs):
+    qkv_ref, out_ref = refs[-2:]
+    part = qkv_ref.shape[2] // 2
+    for h in range(2):
         cols = slice(h * part, (h + 1) * part)
-        for ref, which in zip(outs[2 * h :], both):
-            for i, k in enumerate(which):
-                at = slots[0].index(k)
-                for j in range(3):
-                    total = dot(x[0][at], grads[j][:, cols], TN)
-                    total = total + dot(x[1][at], grads[3 + j][:, cols], TN)
-                    ref[i, j] = total.astype(bf16)
-
-
-def input_grad_kernel(at_ref, x_ref, gain_ref, mid_grad_ref, own_ref, *refs):
-    rows = own_ref.shape[1]
+        for j in range(4):
+            total = sum(ref[ref.shape[0] - 1, j].astype(f32) for ref in refs[h * terms : (h + 1) * terms])
+            if j < 3:
+                qkv_ref[j, :, cols] = total
+            else:
+                out_ref[cols, :] = total.T
+
+
+def input_grad_kernel(at_ref, x_ref, gain_ref, mid_grad_ref, own_ref, small_ref, *refs):
+    parts, out_ref = refs[:-1], refs[-1]
+    count, rows, width = own_ref.shape
     total = own_ref[...]
-    for ref in refs[:-1]:
+    for ref in parts:
         total = total + ref[...].astype(f32)
     block = x_ref[pl.ds(pl.multiple_of(at_ref[0] * rows, rows), rows), :].astype(f32)
-    normal, inv = row_stats(split(block, own_ref.shape[0]))
-    refs[-1][...] = (mid_grad_ref[...] + norm_back(normal, inv, total, gain_ref[...])).astype(bf16)
+    normal, inv = row_stats(split(block, count))
+    grad = mid_grad_ref[...] + norm_back(normal, inv, total, gain_ref[...])
+    out_ref[: count * rows] = grad.astype(bf16).reshape(count * rows, width)
+    out_ref[count * rows :] = small_ref[: 4 * count].astype(bf16)
 
 
 def join_kernel(at_ref, *refs):
@@ -527,6 +504,20 @@
         at = pl.ds(pl.multiple_of(at_ref[j] * rows, rows), rows)
         for n in range(slices):
             out_ref[at, n * width : (n + 1) * width] = ref[n]
+
+
+def join_grad_kernel(at_ref, small_ref, *refs):
+    blocks, (out_ref, total_ref) = refs[:-2], refs[-2:]
+    width = small_ref.shape[1]
+    count = out_ref.shape[1] // width
+    rows = out_ref.shape[0] // len(blocks)
+    total_ref[...] = small_ref[...]
+    for j, ref in enumerate(blocks):
+        at = pl.ds(pl.multiple_of(at_ref[j] * rows, rows), rows)
+        for n in range(count):
+            out_ref[at, n * width : (n + 1) * width] = ref[n * rows : (n + 1) * rows]
+        if j:
+            total_ref[: 4 * count] += ref[count * rows :].astype(f32)
 
 
 def on_device(
@@ -592,24 +583,22 @@
         scratch=[slices],
     )
 
-    qkv_slots = plane.gather_halves(qkv_weight, one_kept, one_sent, tables, hide, cot)
-    pieces = [len(qkv_slots[k]) for k in range(count)]
-    qkv_list = [piece for k in range(count) for piece in qkv_slots[k]]
-    first = (qkv_slots[plane.up[0]], qkv_slots[plane.up[-1]])
-    passed = qkv_slots[plane.up[0] ^ plane.up[-1]]
+    qkv_slots = plane.gather(qkv_weight)
+    qkv_list = [qkv_slots[k] for k in range(count)]
     ffn_shard = call(
         pack_kernel, "ffn_shard", shape((3 * width, hid), bf16), (gate_up_weight, down_weight),
         [VM, VM],
     )
-    out_slots = plane.gather(tie(out_weight, ffn_shard), plane.up, passed)
+    out_slots = plane.gather(tie(out_weight, ffn_shard))
     out_list = [out_slots[k] for k in range(count)]
+    first = (qkv_slots[plane.up[0]], qkv_slots[plane.up[-1]])
     ffn_all = lax.all_gather(tie(ffn_shard, first), PLANE, axis=0, tiled=False)
 
     queries, here = call(
-        functools.partial(qkv_kernel, slots, pieces), "qkv",
+        functools.partial(qkv_kernel, slots), "qkv",
         (shape((tok, feat), bf16), shape((2, tok, feat), bf16)),
         (one_kept, one_sent, qkv_bias.reshape(3, 1, feat), tables, *qkv_list),
-        [VM] * (4 + sum(pieces)),
+        [VM] * (4 + count),
     )
     early = lax.ppermute(here, "context", [(i, i + 1) for i in range(plane.context - 1)])
     sends = [shape((count, chunk, width), bf16)] * (peers - 1)
@@ -622,6 +611,8 @@
         scratch=[pltpu.VMEM((count, tok, width), f32)],
     )
     got = tensor_exchange([None] + parts)
+    cot_got, one_got, att_got = plane.across((cot_sent, one_sent, attended))
+    own = tie(own, cot_got, one_got, att_got)
     mid, normed_chunk = call(
         mid_kernel, "mid", (own_shape, sends[0]),
         (at, block_in, by_slice(ffn_gain), by_slice(ffn_bias), own, *got),
@@ -629,11 +620,10 @@
     )
     normed_two = tensor_gather(normed_chunk)
 
-    hid_shape = shape((tok, hid), bf16)
     buffer = pltpu.VMEM((model, hid), bf16)
-    two_kept, two_sent, hidden, gate_grad, up_grad, grad_own, *grad_parts = call(
+    two_kept, two_sent, three, grad_own, *grad_parts = call(
         functools.partial(ffn_kernel, slots, peers), "ffn",
-        (*slice_pair, hid_shape, hid_shape, hid_shape, own_shape, *sends),
+        (*slice_pair, shape((3, tok, hid), bf16), own_shape, *sends),
         (order, *normed_two, cot, ffn_all), [SM] + [VM] * (peers + 1) + [HB],
         scratch=[buffer] * 3
         + [
@@ -642,36 +632,29 @@
         ],
     )
     got = tensor_exchange([None] + grad_parts)
-    two_got, cot_got, hidden_got, gate_got, up_got = plane.across(
-        (two_sent, cot_sent, hidden, gate_grad, up_grad)
-    )
+    two_got, three_got = plane.across((two_sent, three))
     place = jnp.stack([plane.rank(k) for k in plane.kept])
     of_slot = pl.BlockSpec((1, tok, width), lambda i, place: (i, 0, 0))
-    whole = pl.BlockSpec((tok, hid), lambda i, place: (0, 0))
+    whole = pl.BlockSpec((3, tok, hid), lambda i, place: (0, 0, 0))
     ffn_grads = pl.pallas_call(
         ffn_weights_kernel,
         grid_spec=pltpu.PrefetchScalarGridSpec(
             num_scalar_prefetch=1,
             grid=(count // 2,),
-            in_specs=[of_slot] * 4 + [whole] * 6,
+            in_specs=[of_slot] * 4 + [whole] * 2,
             out_specs=pl.BlockSpec((3 * width, hid), lambda i, place: (place[i], 0)),
         ),
         out_shape=shape((count // 2 * 3 * width, hid), bf16),
         **params("ffn_weights"),
-    )(
-        place, two_kept, two_got, cot_kept, cot_got,
-        gate_grad, gate_got, up_grad, up_got, hidden, hidden_got,
-    )
-    block_part = call(
-        down_kernel, "down", shape((tok, model), bf16), (at, hidden, ffn_all, mid),
-        [SM, VM, HB, VM], scratch=[buffer, pltpu.SemaphoreType.DMA((count,))],
-    )
-    block_out = lax.psum(block_part, "tensor")
+    )(place, two_kept, two_got, cot_kept, cot_got, three, three_got)
+    down_own, *down_parts = call(
+        down_kernel, "down", (own_shape, *sends), (three, ffn_all), [VM, HB],
+        scratch=[buffer, pltpu.SemaphoreType.DMA((count,))],
+    )
     ffn_total = lax.psum_scatter(
-        tie(ffn_grads, block_part),
-        PLANE, scatter_dimension=0, axis_index_groups=plane.groups, tiled=True,
-    )
-    grad_own = tie(grad_own, ffn_grads, block_part)
+        ffn_grads, PLANE, scatter_dimension=0, axis_index_groups=plane.groups, tiled=True
+    )
+    grad_own = tie(grad_own, ffn_grads, down_own)
     vec = shape((count, 1, width), f32)
     mid_grad, low_chunk, ffn_gain_grad, ffn_bias_grad = call(
         mid_back_kernel, "mid_back", (own_shape, sends[0], vec, vec),
@@ -679,6 +662,12 @@
         [VM] * (4 + len(got)),
     )
     low_blocks = tensor_gather(low_chunk)
+    down_got = tensor_exchange([None, *tie(down_parts, low_blocks)])
+    out_chunk = call(
+        block_out_kernel, "block_out", sends[0], (mid, down_own, *down_got),
+        [VM] * (2 + len(down_got)),
+    )
+    out_blocks = tensor_gather(out_chunk)
 
     low_kept, low_sent, dq, dhere, dearly = call(
         functools.partial(attend_back_kernel, slots, peers), "attend_back",
@@ -690,71 +679,66 @@
         [SM, SM] + [VM] * (6 + peers + count),
         scratch=[pltpu.VMEM((tok, feat), bf16)],
     )
+    low_got = plane.across(low_sent)
     dback = lax.ppermute(dearly, "context", [(i + 1, i) for i in range(plane.context - 1)])
+    small_shape = shape((4 * count + 3 * feat // width, width), f32)
+    back, small, own, *parts = call(
+        one_grad_kernel, "one_grad",
+        (
+            shape((3, tok, feat), bf16), small_shape, own_shape, *sends,
+        ),
+        (
+            order, at, block_in, tables, dq, tie(dhere, out_blocks, low_got), dback, *qkv_list,
+            ffn_gain_grad, ffn_bias_grad,
+        ),
+        [SM, SM] + [VM] * (7 + count),
+        scratch=[pltpu.VMEM((count, tok, width), f32)],
+    )
+    got = tensor_exchange([None, *parts])
     halves = (plane.halves(plane.down), plane.halves(plane.up))
-    half = feat // 2
-    stacks = lambda *dims: (shape((count // 4,) + dims, bf16),) * 4
-    out_grads = call(
-        functools.partial(out_weights_kernel, slots, halves), "out_weights", stacks(half, width),
-        (attended, plane.across(attended), low_kept, plane.across(low_sent)), [VM] * 4,
-    )
-    out_a = Scatter(plane, *out_grads[:2], plane.down)
-    out_b = Scatter(plane, *out_grads[2:], plane.up)
-    out_total = [out_a.total(dback), out_b.total(dback)]
-    results = call(
-        functools.partial(one_grad_kernel, pieces), "one_grad",
-        (
-            *[shape((tok, feat), bf16)] * 3, shape((3, 1, feat), f32), vec, vec, own_shape, *sends,
-        ),
-        (order, at, block_in, tables, dq, dhere, dback, *qkv_list),
-        [SM, SM] + [VM] * (5 + sum(pieces)),
-        scratch=[pltpu.VMEM((count, tok, width), f32)],
-    )
-    back, (bias_grad, attn_gain_grad, attn_bias_grad, own), parts = (
-        results[:3], results[3:7], results[7:]
-    )
-    got = tensor_exchange([None, *parts])
-    qkv_grads = call(
-        functools.partial(qkv_weights_kernel, slots, halves), "qkv_weights", stacks(3, width, half),
-        (one_kept, plane.across(one_sent), *back, *plane.across(back)), [VM] * 8,
-    )
-    qkv_a = Scatter(plane, *qkv_grads[:2], plane.down)
-    qkv_b = Scatter(plane, *qkv_grads[2:], plane.up)
-    qkv_total = [qkv_a.total(out_total), qkv_b.total(out_total)]
+    back_got = plane.across(back)
+    small = plane.chip_total(small)
+    weight_grads = call(
+        functools.partial(attention_weights_kernel, slots, halves), "attention_weights",
+        (shape((count // 4, 4, width, feat // 2), bf16),) * 4,
+        (one_kept, one_got, tie(back, small), back_got, low_kept, low_got, attended, att_got), [VM] * 8,
+    )
+    terms_a = scatter(plane, *weight_grads[:2], plane.down)
+    terms_b = scatter(plane, *weight_grads[2:], plane.up)
     grad_chunk = call(
-        input_grad_kernel, "input_grad", sends[0],
-        (at, block_in, by_slice(attn_gain), mid_grad, own, *got),
-        [SM] + [VM] * (4 + len(got)),
+        input_grad_kernel, "input_grad", shape((count * chunk + 4 * count, width), bf16),
+        (at, block_in, by_slice(attn_gain), mid_grad, own, small, *got),
+        [SM] + [VM] * (5 + len(got)),
     )
     grad_blocks = tensor_gather(grad_chunk)
-    input_grad = call(
-        join_kernel, "input_grad_rows", shape((tok, model), bf16), (at, *grad_blocks),
-        [SM] + [VM] * peers,
-    )
     gate_up_grad, down_grad = call(
         ffn_out_kernel, "ffn_out", (shape((2, width, hid), f32), shape((hid, width), f32)),
         (ffn_total,), [VM],
     )
-
-    small = jnp.concatenate(
-        [
-            v.reshape(-1)
-            for v in (attn_gain_grad, attn_bias_grad, ffn_gain_grad, ffn_bias_grad, bias_grad)
-        ]
-    )
-    small = plane.total(tie(small, got))
-    vectors = small[: 4 * model].reshape(4, model)
-    vectors = vectors + sum(tensor_swap(vectors, j) for j in range(1, peers))
-    qkv_bias_grad = small[4 * model :].reshape(3, feat)
-
+    block_out = call(
+        join_kernel, "block_out_rows", shape((tok, model), bf16), (at, *out_blocks),
+        [SM] + [VM] * peers,
+    )
+    input_grad, small = call(
+        join_grad_kernel, "input_grad_rows", (shape((tok, model), bf16), small_shape),
+        (at, small, *tie(grad_blocks, block_out, down_grad)), [SM] + [VM] * (1 + peers),
+    )
+
+    terms = (*terms_a, *terms_b)
+    qkv_grad, out_grad = call(
+        functools.partial(attention_out_kernel, len(terms_a)), "attention_out",
+        (shape((3, width, feat), f32), shape((feat, width), f32)), terms, [VM] * len(terms),
+    )
+    small = small + plane.across(small)
+    vectors = small[: 4 * count].reshape(4, model)
     return (
         block_out,
         input_grad,
         vectors[0],
         vectors[1],
-        jnp.concatenate(qkv_total, axis=2),
-        qkv_bias_grad,
-        jnp.concatenate(out_total, axis=0),
+        qkv_grad,
+        small[4 * count :].reshape(3, feat),
+        out_grad,
         vectors[2],
         vectors[3],
         gate_up_grad,

time: 393 us -> 359 us (0.913)
  waiting for transfers between devices: 191 us -> 150 us
  Pallas kernels: 96.7 us -> 104 us
    ppermute x1, waiting for transfers between devices: 24.1 us -> 0.01 us  [on_device(): lax.ppermute(dearly, 'context', [(i + 1, i) for i in range(plane.context...]
    ppermute x38 -> x28, waiting for transfers between devices: 65.5 us -> 44.5 us  [swap(): return lax.ppermute(value, ('fsdp', 'context'), pairs)]
    ppermute x1, waiting for transfers between devices: 0.82 us -> 17.5 us  [on_device(): lax.ppermute(here, 'context', [(i, i + 1) for i in range(plane.context -...]
    ppermute x21 -> x24, waiting for transfers between devices: 96.4 us -> 84.7 us  [tensor_swap(): return lax.ppermute(value, 'tensor', [(i, i ^ j) for i in range(peers)])]
    pallas_call x16 -> x18, Pallas kernels: 86 us -> 93.5 us  [call(): pl.pallas_call(kernel, out_shape=outs, in_specs=specs, out_specs=jax.tree...]
    ppermute x21 -> x24, starting transfers between devices: 39.7 us -> 43.2 us  [tensor_swap(): return lax.ppermute(value, 'tensor', [(i, i ^ j) for i in range(peers)])]
    ppermute x38 -> x28, starting transfers between devices: 22.3 us -> 19.1 us  [swap(): return lax.ppermute(value, ('fsdp', 'context'), pairs)]
    unnamed x125 -> x93, local copies, waits for them, and re-layouts: 13.8 us -> 10.8 us
  transfers between devices with their start and end apart: 64 -> 56, of which waited for: 26 -> 21; matrix products, arithmetic and copies ran while one was open for 3% -> 3% of each run, Pallas kernels for 20% -> 24%
where the time goes in v3:
time: 359 us
  waiting for transfers between devices  150 us (42%)
  Pallas kernels  104 us (29%)
  starting transfers between devices  67 us (19%)
  between operations  14.5 us (4%)
  local copies, waits for them, and re-layouts  12.2 us (3%)
  other arithmetic  10.2 us (3%)
    pallas_call x18, Pallas kernels, call(): pl.pallas_call(kernel, out_shape=outs, in_specs=specs, out_specs=jax.tree...  93.5 us
    ppermute x24, waiting for transfers between devices, tensor_swap(): return lax.ppermute(value, 'tensor', [(i, i ^ j) for i in range(peers)])  84.7 us
    ppermute x28, waiting for transfers between devices, swap(): return lax.ppermute(value, ('fsdp', 'context'), pairs)  44.5 us
    ppermute x24, starting transfers between devices, tensor_swap(): return lax.ppermute(value, 'tensor', [(i, i ^ j) for i in range(peers)])  43.2 us
    ppermute x28, starting transfers between devices, swap(): return lax.ppermute(value, ('fsdp', 'context'), pairs)  19.1 us
    ppermute x1, waiting for transfers between devices, on_device(): lax.ppermute(here, 'context', [(i, i + 1) for i in range(plane.context -...  17.5 us
    unnamed x93, local copies, waits for them, and re-layouts  10.8 us
    pallas_call x1, Pallas kernels, on_device(): pl.pallas_call(ffn_weights_kernel, grid_spec=pltpu.PrefetchScalarGridSpec...  10.7 us
  transfers between devices with their start and end apart: 56, of which 21 were waited for; matrix products, arithmetic and copies ran while one was open for 3% of the time, Pallas kernels for 24%

profile of v3, /device:TPU:0, one launch (start us, length us, event | category | flops | bytes accessed | tf_op | source)
XLA Modules:
  0.0 358.6 jit_solution(796440792978996869)
XLA Ops:
  7.2 4.0 %collective-permute-start.4 = (bf16[3,256,512]{2,1,0:T(8,128)(2,1)}, bf16[3,256,512]{2,1,0:T(8,128)(2,1)S(1)}, u32[]{:S(2)}, u32[]{:S(2)}) collective-permute-start(bf16[3,256,512]{2,1,0:T(8,128)(2,1)} %refs_0_.4), channel_id=1, source_target_pairs={{0,20},{4,16},{8,28},{12,24},{16,4},{20,0},{24,12},{28,8},{1,21},{... | collective-permute-start | bytes 2359304 | tf_op jit(solution)/shard_map/ppermute | solution.py:87
  11.8 3.2 ffn_shard.1
  15.0 2.8 collective-permute-start.12
  18.8 3.1 norm_one.1
  21.9 25.3 %collective-permute-done.3.refs_4_ = bf16[3,256,512]{2,1,0:T(8,128)(2,1)S(1)} collective-permute-done((bf16[3,256,512]{2,1,0:T(8,128)(2,1)}, bf16[3,256,512]{2,1,0:T(8,128)(2,1)S(1)}, u32[]{:S(2)}, u32[]{:S(2)}) %collective-permute-start.3) | collective-permute-done | bytes 786464 | tf_op jit(solution)/shard_map/ppermute | solution.py:87
  56.5 7.1 %qkv.1 = (bf16[256,512]{1,0:T(8,128)(2,1)}, bf16[2,256,512]{2,1,0:T(8,128)(2,1)}) custom-call(bf16[4,256,256]{2,1,0:T(8,128)(2,1)} %get-tuple-element.75.kept_ref.refs_0_, bf16[4,256,256]{2,1,0:T(8,128)(2,1)} %get-tuple-element.76.sent_ref, f32[3,1,512]{2,1,0:T(1,128)} %reshape.289.bias_ref, f32[3,256,128]{2,1,0:T(8,128)} %pad_maximum_fusion.table_ref, ...), custom_call_target="tpu_custom_call" | custom-call | flops 11500000256 | tf_op jit(solution)/shard_map/qkv/pallas_call | solution.py:44
  64.0 3.1 collective-permute-start.7
  67.2 2.7 cotangent_rows.1
  72.7 17.5 %collective-permute-done.7.early_ref = bf16[2,256,512]{2,1,0:T(8,128)(2,1)S(1)} collective-permute-done((bf16[2,256,512]{2,1,0:T(8,128)(2,1)}, bf16[2,256,512]{2,1,0:T(8,128)(2,1)S(1)}, u32[]{:S(2)}, u32[]{:S(2)}) %collective-permute-start.7) | collective-permute-done | bytes 524320 | tf_op jit(solution)/shard_map/ppermute | solution.py:603
  91.0 7.4 %attend.1 = (bf16[256,512]{1,0:T(8,128)(2,1)}, f32[8,256,1]{2,1,0:T(8,128)}, f32[8,64,256]{2,1,0:T(8,128)}, bf16[8,64,256]{2,1,0:T(8,128)(2,1)}, bf16[8,64,256]{...) custom-call(s32[8]{0:T(128)} %iota_xor_fusion.order_ref, s32[4]{0:T(128)} %iota_xor_fusion.1.at_ref, ...), custom_call_target="tpu_custom_call" | custom-call | tf_op jit(solution)/shard_map/attend/pallas_call | solution.py:44
  100.2 2.7 collective-permute-start.19
  102.9 9.6 %collective-permute-done.18.refs_0_ = bf16[8,64,256]{2,1,0:T(8,128)(2,1)S(1)} collective-permute-done((bf16[8,64,256]{2,1,0:T(8,128)(2,1)}, bf16[8,64,256]{2,1,0:T(8,128)(2,1)S(1)}, u32[]{:S(2)}, u32[]{:S(2)}) %collective-permute-start.18) | collective-permute-done | bytes 262176 | tf_op jit(solution)/shard_map/ppermute | solution.py:122
  112.6 9.1 %collective-permute-done.19.refs_1_ = bf16[8,64,256]{2,1,0:T(8,128)(2,1)S(1)} collective-permute-done((bf16[8,64,256]{2,1,0:T(8,128)(2,1)}, bf16[8,64,256]{2,1,0:T(8,128)(2,1)S(1)}, u32[]{:S(2)}, u32[]{:S(2)}) %collective-permute-start.19) | collective-permute-done | bytes 262176 | tf_op jit(solution)/shard_map/ppermute | solution.py:122
  122.5 2.7 mid.1
  125.2 2.5 collective-permute-start.23
  127.8 4.3 %collective-permute-start.22 = (bf16[8,64,256]{2,1,0:T(8,128)(2,1)}, bf16[8,64,256]{2,1,0:T(8,128)(2,1)S(1)}, u32[]{:S(2)}, u32[]{:S(2)}) collective-permute-start(bf16[8,64,256]{2,1,0:T(8,128)(2,1)} %get-tuple-element.88.refs_0_), channel_id=1, source_target_pairs={{0,2},{1,3},{2,0},{3,1},{4,6},{5,7},{6,4},{7,5},{8,10},{9,11},{10,... | collective-permute-start | bytes 786440 | tf_op jit(solution)/shard_map/ppermute | solution.py:122
  132.2 2.1 collective-permute-done.23.refs_3_
  134.2 16.7 %collective-permute-done.22.refs_2_ = bf16[8,64,256]{2,1,0:T(8,128)(2,1)S(1)} collective-permute-done((bf16[8,64,256]{2,1,0:T(8,128)(2,1)}, bf16[8,64,256]{2,1,0:T(8,128)(2,1)S(1)}, u32[]{:S(2)}, u32[]{:S(2)}) %collective-permute-start.22) | collective-permute-done | bytes 262176 | tf_op jit(solution)/shard_map/ppermute | solution.py:122
  151.0 3.7 %all-gather.3.cloned.1.call-done = bf16[6144,1408]{1,0:T(8,128)(2,1)} async-done(((bf16[768,1408]{1,0:T(8,128)(2,1)}), bf16[6144,1408]{1,0:T(8,128)(2,1)}) %all-gather.3.cloned.1.call-update) | async-done | bytes 17301520 | tf_op jit(solution)/shard_map/all_gather | solution.py:595
  154.7 15.4 %ffn.1 = (bf16[4,256,256]{2,1,0:T(8,128)(2,1)}, bf16[4,256,256]{2,1,0:T(8,128)(2,1)}, bf16[3,256,1408]{2,1,0:T(8,128)(2,1)}, f32[8,64,256]{2,1,0:T(8,128)}, bf16...) custom-call(s32[8]{0:T(128)} %iota_xor_fusion.order_ref, ...), custom_call_target="tpu_custom_call" | custom-call | tf_op jit(solution)/shard_map/ffn/pallas_call | solution.py:44
  172.2 2.4 collective-permute-start.27
  175.7 7.2 %down.1 = (f32[8,64,256]{2,1,0:T(8,128)}, bf16[8,64,256]{2,1,0:T(8,128)(2,1)}, bf16[8,64,256]{2,1,0:T(8,128)(2,1)}, bf16[8,64,256]{2,1,0:T(8,128)(2,1)}) custom-call(bf16[3,256,1408]{2,1,0:T(8,128)(2,1)} %get-tuple-element.91.three_ref.refs_4_, bf16[8,768,1408]{2,1,0:T(8,128)(2,1)} %bitcast.29), custom_call_target="tpu_custom_call" | custom-call | tf_op jit(solution)/shard_map/down/pallas_call | solution.py:44
  184.4 10.7 %ffn_weights.1 = bf16[3072,1408]{1,0:T(8,128)(2,1)} custom-call(s32[4]{0:T(128)} %pad_add_fusion.place_ref, bf16[4,256,256]{2,1,0:T(8,128)(2,1)} %get-tuple-element.97.refs_0_, bf16[4,256,256]{2,1,0:T(8,128)(2,1)} %copy-done.14, bf16[4,256,256]{2,1,0:T(8,128)(2,1)} %get-tuple-element.99.refs_2_, bf16[4,256,256]{2,1,0:T(8,128)(2,1)} %copy-done.11, ...), custom_call_target="tpu_custom_call" | custom-call | tf_op jit(solution)/shard_map/ffn_weights/pallas_call | solution.py:639
  196.0 3.3 mid_back.1
  199.3 3.3 collective-permute-start.31
  202.6 1.8 collective-permute-start.30
  204.4 6.2 %collective-permute-done.31.refs_3_ = bf16[8,64,256]{2,1,0:T(8,128)(2,1)S(1)} collective-permute-done((bf16[8,64,256]{2,1,0:T(8,128)(2,1)}, bf16[8,64,256]{2,1,0:T(8,128)(2,1)S(1)}, u32[]{:S(2)}, u32[]{:S(2)}) %collective-permute-start.31) | collective-permute-done | bytes 262176 | tf_op jit(solution)/shard_map/ppermute | solution.py:122
  210.6 15.1 %collective-permute-done.30.refs_2_ = bf16[8,64,256]{2,1,0:T(8,128)(2,1)S(1)} collective-permute-done((bf16[8,64,256]{2,1,0:T(8,128)(2,1)}, bf16[8,64,256]{2,1,0:T(8,128)(2,1)S(1)}, u32[]{:S(2)}, u32[]{:S(2)}) %collective-permute-start.30) | collective-permute-done | bytes 262176 | tf_op jit(solution)/shard_map/ppermute | solution.py:122
  226.4 3.3 collective-permute-start.33
  230.2 10.0 %attend_back.1 = (bf16[4,256,256]{2,1,0:T(8,128)(2,1)}, bf16[4,256,256]{2,1,0:T(8,128)(2,1)}, bf16[256,512]{1,0:T(8,128)(2,1)}, f32[2,256,512]{2,1,0:T(8,128)}, bf16[2,256,512]{2,1,0:T(8,128)(2,1)}) custom-call(s32[8]{0:T(128)} %iota_xor_fusion.order_ref, s32[4]{0:T(128)} %iota_xor_fusion.1.at_ref, f32[256,512]{1,0:T(8,128)} %and_select_fusion.hide_ref, ...), custom_call_target="tpu_custom_call" | custom-call | flops 230000001024 | tf_op jit(solution)/shard_map/attend_back/pallas_call | solution.py:44
  241.9 6.6 %collective-permute-done.33.refs_1_ = bf16[8,64,256]{2,1,0:T(8,128)(2,1)} collective-permute-done((bf16[8,64,256]{2,1,0:T(8,128)(2,1)}, bf16[8,64,256]{2,1,0:T(8,128)(2,1)}, u32[]{:S(2)}, u32[]{:S(2)}) %collective-permute-start.33) | collective-permute-done | bytes 262176 | tf_op jit(solution)/shard_map/ppermute | solution.py:122
  248.4 2.3 block_out.1.refs_0_
  250.7 2.4 collective-permute-start.37
  253.1 4.5 %collective-permute-start.36 = (bf16[8,64,256]{2,1,0:T(8,128)(2,1)}, bf16[8,64,256]{2,1,0:T(8,128)(2,1)S(1)}, u32[]{:S(2)}, u32[]{:S(2)}) collective-permute-start(bf16[8,64,256]{2,1,0:T(8,128)(2,1)} %block_out.1.refs_0_), channel_id=1, source_target_pairs={{0,2},{1,3},{2,0},{3,1},{4,6},{5,7},{6,4},{7,5},{8,10},{9,11},{10,... | collective-permute-start | bytes 786440 | tf_op jit(solution)/shard_map/ppermute | solution.py:122
  259.3 16.7 %collective-permute-done.36.refs_2_ = bf16[8,64,256]{2,1,0:T(8,128)(2,1)S(1)} collective-permute-done((bf16[8,64,256]{2,1,0:T(8,128)(2,1)}, bf16[8,64,256]{2,1,0:T(8,128)(2,1)S(1)}, u32[]{:S(2)}, u32[]{:S(2)}) %collective-permute-start.36) | collective-permute-done | bytes 262176 | tf_op jit(solution)/shard_map/ppermute | solution.py:122
  276.9 8.0 %one_grad.1 = (bf16[3,256,512]{2,1,0:T(8,128)(2,1)}, f32[38,256]{1,0:T(8,128)}, f32[8,64,256]{2,1,0:T(8,128)}, bf16[8,64,256]{2,1,0:T(8,128)(2,1)}, bf16[8,64,25...) custom-call(s32[8]{0:T(128)} %iota_xor_fusion.order_ref, s32[4]{0:T(128)} %iota_xor_fusion.1.at_ref, ...), custom_call_target="tpu_custom_call" | custom-call | tf_op jit(solution)/shard_map/one_grad/pallas_call | solution.py:44
  286.0 3.2 collective-permute-start.43
  292.7 3.4 collective-permute-done.41
  297.6 5.6 %attention_weights.1 = (bf16[2,4,256,256]{3,2,1,0:T(8,128)(2,1)}, bf16[2,4,256,256]{3,2,1,0:T(8,128)(2,1)}, bf16[2,4,256,256]{3,2,1,0:T(8,128)(2,1)}, bf16[2,4,256,256]{3,2,1,0:T(8,128)(2,1)}) custom-call(bf16[4,256,256]{2,1,0:T(8,128)(2,1)} %get-tuple-element.75.kept_ref.refs_0_, bf16[4,256,256]{2,1,0:T(8,128)(2,1)} %collective-permute-done.16.refs_1_, ...), custom_call_target="tpu_custom_call" | custom-call | tf_op jit(solution)/shard_map/attention_weights/pallas_call | solution.py:44
  304.7 2.2 block_out_rows.1
  309.0 3.1 input_grad.1.refs_0_
  312.1 2.7 collective-permute-start.47
  314.8 3.8 %collective-permute-start.46 = (bf16[544,256]{1,0:T(8,128)(2,1)}, bf16[544,256]{1,0:T(8,128)(2,1)S(1)}, u32[]{:S(2)}, u32[]{:S(2)}) collective-permute-start(bf16[544,256]{1,0:T(8,128)(2,1)} %input_grad.1.refs_0_), channel_id=1, source_target_pairs={{0,2},{1,3},{2,0},{3,1},{4,6},{5,7},{6,4},{7,5},{8,10},{9,11},{10,... | collective-permute-start | bytes 835592 | tf_op jit(solution)/shard_map/ppermute | solution.py:122
  318.6 8.7 %collective-permute-done.50.refs_1_ = bf16[2,4,256,256]{3,2,1,0:T(8,128)(2,1)S(1)} collective-permute-done((bf16[2,4,256,256]{3,2,1,0:T(8,128)(2,1)}, bf16[2,4,256,256]{3,2,1,0:T(8,128)(2,1)S(1)}, u32[]{:S(2)}, u32[]{:S(2)}) %collective-permute-start.50) | collective-permute-done | bytes 1048608 | tf_op jit(solution)/shard_map/ppermute | solution.py:87
  329.4 3.3 collective-permute-done.52.refs_4_
  333.9 4.0 %ffn_out.1 = (f32[2,256,1408]{2,1,0:T(8,128)}, f32[1408,256]{1,0:T(8,128)}) custom-call(bf16[768,1408]{1,0:T(8,128)(2,1)} %reduce-scatter.2.cloned.1.call-done.total_ref), custom_call_target="tpu_custom_call" | custom-call | tf_op jit(solution)/shard_map/ffn_out/pallas_call | solution.py:44
  339.6 2.3 input_grad_rows.1
  344.6 4.1 %attention_out.1 = (f32[3,256,512]{2,1,0:T(8,128)}, f32[512,256]{1,0:T(8,128)}) custom-call(bf16[2,4,256,256]{3,2,1,0:T(8,128)(2,1)} %get-tuple-element.132.refs_0_, bf16[2,4,256,256]{3,2,1,0:T(8,128)(2,1)} %copy-done.2, bf16[1,4,256,256]{3,2,1,0:T(8,128)(2,1)} %copy-done.13, bf16[2,4,256,256]{3,2,1,0:T(8,128)(2,1)} %get-tuple-element.134.refs_3_, ...), custom_call_target="tpu_custom_call" | custom-call | tf_op jit(solution)/shard_map/attention_out/pallas_call | solution.py:44
  (205 shorter events, 48.9 us)
Async XLA Ops:
  7.2 147.5 %all-gather.3.cloned.1.call-start = ((), (), s32[]{:S(2)}) async-start(), calls=%async_computation.2 | async-start | bytes 19464192 | tf_op jit(solution)/shard_map/all_gather | solution.py:595
  7.2 41.5 %collective-permute-start.4 = (bf16[3,256,512]{2,1,0:T(8,128)(2,1)}, bf16[3,256,512]{2,1,0:T(8,128)(2,1)S(1)}, u32[]{:S(2)}, u32[]{:S(2)}) collective-permute-start(bf16[3,256,512]{2,1,0:T(8,128)(2,1)} %refs_0_.4), channel_id=1, source_target_pairs={{0,20},{4,16},{8,28},{12,24},{16,4},{20,0},{24,12},{28,8},{1,21},{... | collective-permute-start | bytes 2359304 | tf_op jit(solution)/shard_map/ppermute | solution.py:87
  11.2 36.0 %collective-permute-start.3 = (bf16[3,256,512]{2,1,0:T(8,128)(2,1)}, bf16[3,256,512]{2,1,0:T(8,128)(2,1)S(1)}, u32[]{:S(2)}, u32[]{:S(2)}) collective-permute-start(bf16[3,256,512]{2,1,0:T(8,128)(2,1)} %refs_0_.4), channel_id=1, source_target_pairs={{0,16},{4,20},{8,24},{12,28},{16,0},{20,4},{24,8},{28,12},{1,17},{... | collective-permute-start | bytes 2359304 | tf_op jit(solution)/shard_map/ppermute | solution.py:87
  11.7 42.8 %collective-permute-start.1 = (bf16[3,256,512]{2,1,0:T(8,128)(2,1)}, bf16[3,256,512]{2,1,0:T(8,128)(2,1)S(1)}, u32[]{:S(2)}, u32[]{:S(2)}) collective-permute-start(bf16[3,256,512]{2,1,0:T(8,128)(2,1)} %refs_0_.4), channel_id=1, source_target_pairs={{0,8},{4,12},{8,0},{12,4},{16,24},{20,28},{24,16},{28,20},{1,9},{5... | collective-permute-start | bytes 2359304 | tf_op jit(solution)/shard_map/ppermute | solution.py:87
  11.7 35.5 %collective-permute-start = (bf16[3,256,512]{2,1,0:T(8,128)(2,1)}, bf16[3,256,512]{2,1,0:T(8,128)(2,1)S(1)}, u32[]{:S(2)}, u32[]{:S(2)}) collective-permute-start(bf16[3,256,512]{2,1,0:T(8,128)(2,1)} %refs_0_.4), channel_id=1, source_target_pairs={{0,4},{4,0},{8,12},{12,8},{16,20},{20,16},{24,28},{28,24},{1,5},{5... | collective-permute-start | bytes 2359304 | tf_op jit(solution)/shard_map/ppermute | solution.py:87
  15.0 38.0 %collective-permute-start.12 = (bf16[512,256]{1,0:T(8,128)(2,1)}, bf16[512,256]{1,0:T(8,128)(2,1)}, u32[]{:S(2)}, u32[]{:S(2)}) collective-permute-start(bf16[512,256]{1,0:T(8,128)(2,1)} %refs_4_), channel_id=1, source_target_pairs={{0,20},{4,16},{8,28},{12,24},{16,4},{20,0},{24,12},{28,8},{1,21},{... | collective-permute-start | bytes 786440 | tf_op jit(solution)/shard_map/ppermute | solution.py:87
  47.3 286.7 %reduce-scatter.2.cloned.1.call-start = ((), (), s32[]{:S(2)}) async-start(), calls=%async_computation.1 | async-start | bytes 10813440 | tf_op jit(solution)/shard_map/reduce_scatter | solution.py:654
  48.2 8.0 %collective-permute-start.2 = (bf16[3,256,512]{2,1,0:T(8,128)(2,1)S(1)}, bf16[3,256,512]{2,1,0:T(8,128)(2,1)}, u32[]{:S(2)}, u32[]{:S(2)}) collective-permute-start(bf16[3,256,512]{2,1,0:T(8,128)(2,1)S(1)} %collective-permute-done.refs_1_), channel_id=1, source_target_pairs={{0,8},{4,12},{8,0},{12,4},{16,24},{20,28},{24,16},{28,20},{1,9},{5... | collective-permute-start | bytes 2359304 | tf_op jit(solution)/shard_map/ppermute | solution.py:87
  53.1 11.0 %collective-permute-start.11 = (bf16[512,256]{1,0:T(8,128)(2,1)}, bf16[512,256]{1,0:T(8,128)(2,1)S(1)}, u32[]{:S(2)}, u32[]{:S(2)}) collective-permute-start(bf16[512,256]{1,0:T(8,128)(2,1)} %refs_4_), channel_id=1, source_target_pairs={{0,16},{4,20},{8,24},{12,28},{16,0},{20,4},{24,8},{28,12},{1,17},{... | collective-permute-start | bytes 786440 | tf_op jit(solution)/shard_map/ppermute | solution.py:87
  54.5 15.3 %collective-permute-start.9 = (bf16[512,256]{1,0:T(8,128)(2,1)}, bf16[512,256]{1,0:T(8,128)(2,1)}, u32[]{:S(2)}, u32[]{:S(2)}) collective-permute-start(bf16[512,256]{1,0:T(8,128)(2,1)} %refs_4_), channel_id=1, source_target_pairs={{0,8},{4,12},{8,0},{12,4},{16,24},{20,28},{24,16},{28,20},{1,9},{5... | collective-permute-start | bytes 786440 | tf_op jit(solution)/shard_map/ppermute | solution.py:87
  54.6 15.3 %collective-permute-start.8 = (bf16[512,256]{1,0:T(8,128)(2,1)}, bf16[512,256]{1,0:T(8,128)(2,1)}, u32[]{:S(2)}, u32[]{:S(2)}) collective-permute-start(bf16[512,256]{1,0:T(8,128)(2,1)} %refs_4_), channel_id=1, source_target_pairs={{0,4},{4,0},{8,12},{12,8},{16,20},{20,16},{24,28},{28,24},{1,5},{5... | collective-permute-start | bytes 786440 | tf_op jit(solution)/shard_map/ppermute | solution.py:87
  56.0 46.9 %collective-permute-start.16 = (bf16[4,256,256]{2,1,0:T(8,128)(2,1)}, bf16[4,256,256]{2,1,0:T(8,128)(2,1)}, u32[]{:S(2)}, u32[]{:S(2)}) collective-permute-start(bf16[4,256,256]{2,1,0:T(8,128)(2,1)} %get-tuple-element.76.sent_ref), channel_id=1, source_target_pairs={{0,8},{4,12},{8,0},{12,4},{16,24},{20,28},{24,16},{28,20},{1,9},{5... | collective-permute-start | bytes 1572872 | tf_op jit(solution)/shard_map/ppermute | solution.py:87
  56.2 14.2 %collective-permute-start.14 = (bf16[512,256]{1,0:T(8,128)(2,1)}, bf16[512,256]{1,0:T(8,128)(2,1)}, u32[]{:S(2)}, u32[]{:S(2)}) collective-permute-start(bf16[512,256]{1,0:T(8,128)(2,1)} %collective-permute-done.12.refs_5_.refs_9_), channel_id=1, source_target_pairs={{0,8},{4,12},{8,0},{12,4},{16,24},{20,28},{24,16},{28,20},{1,9},{5... | collective-permute-start | bytes 786440 | tf_op jit(solution)/shard_map/ppermute | solution.py:87
  64.0 26.2 %collective-permute-start.7 = (bf16[2,256,512]{2,1,0:T(8,128)(2,1)}, bf16[2,256,512]{2,1,0:T(8,128)(2,1)S(1)}, u32[]{:S(2)}, u32[]{:S(2)}) collective-permute-start(bf16[2,256,512]{2,1,0:T(8,128)(2,1)} %get-tuple-element.78.here_ref), channel_id=1, source_target_pairs={{0,4},{1,5},{2,6},{3,7},{8,12},{9,13},{10,14},{11,15},{16,20},{17,... | collective-permute-start | bytes 1572872 | tf_op jit(solution)/shard_map/ppermute | solution.py:603
  69.9 33.0 %collective-permute-start.15 = (bf16[4,256,256]{2,1,0:T(8,128)(2,1)}, bf16[4,256,256]{2,1,0:T(8,128)(2,1)S(1)}, u32[]{:S(2)}, u32[]{:S(2)}) collective-permute-start(bf16[4,256,256]{2,1,0:T(8,128)(2,1)} %get-tuple-element.81), channel_id=1, source_target_pairs={{0,8},{4,12},{8,0},{12,4},{16,24},{20,28},{24,16},{28,20},{1,9},{5... | collective-permute-start | bytes 1572872 | tf_op jit(solution)/shard_map/ppermute | solution.py:87
  98.4 14.1 %collective-permute-start.18 = (bf16[8,64,256]{2,1,0:T(8,128)(2,1)}, bf16[8,64,256]{2,1,0:T(8,128)(2,1)S(1)}, u32[]{:S(2)}, u32[]{:S(2)}) collective-permute-start(bf16[8,64,256]{2,1,0:T(8,128)(2,1)} %get-tuple-element.84), channel_id=1, source_target_pairs={{0,1},{1,0},{2,3},{3,2},{4,5},{5,4},{6,7},{7,6},{8,9},{9,8},{10,11... | collective-permute-start | bytes 786440 | tf_op jit(solution)/shard_map/ppermute | solution.py:122
  100.2 21.5 %collective-permute-start.19 = (bf16[8,64,256]{2,1,0:T(8,128)(2,1)}, bf16[8,64,256]{2,1,0:T(8,128)(2,1)S(1)}, u32[]{:S(2)}, u32[]{:S(2)}) collective-permute-start(bf16[8,64,256]{2,1,0:T(8,128)(2,1)} %get-tuple-element.85), channel_id=1, source_target_pairs={{0,2},{1,3},{2,0},{3,1},{4,6},{5,7},{6,4},{7,5},{8,10},{9,11},{10,... | collective-permute-start | bytes 786440 | tf_op jit(solution)/shard_map/ppermute | solution.py:122
  102.9 18.8 %collective-permute-start.20 = (bf16[8,64,256]{2,1,0:T(8,128)(2,1)}, bf16[8,64,256]{2,1,0:T(8,128)(2,1)S(1)}, u32[]{:S(2)}, u32[]{:S(2)}) collective-permute-start(bf16[8,64,256]{2,1,0:T(8,128)(2,1)} %get-tuple-element.86), channel_id=1, source_target_pairs={{0,3},{1,2},{2,1},{3,0},{4,7},{5,6},{6,5},{7,4},{8,11},{9,10},{10,... | collective-permute-start | bytes 786440 | tf_op jit(solution)/shard_map/ppermute | solution.py:122
  125.2 9.0 %collective-permute-start.23 = (bf16[8,64,256]{2,1,0:T(8,128)(2,1)}, bf16[8,64,256]{2,1,0:T(8,128)(2,1)S(1)}, u32[]{:S(2)}, u32[]{:S(2)}) collective-permute-start(bf16[8,64,256]{2,1,0:T(8,128)(2,1)} %get-tuple-element.88.refs_0_), channel_id=1, source_target_pairs={{0,3},{1,2},{2,1},{3,0},{4,7},{5,6},{6,5},{7,4},{8,11},{9,10},{10,... | collective-permute-start | bytes 786440 | tf_op jit(solution)/shard_map/ppermute | solution.py:122
  127.8 23.2 %collective-permute-start.22 = (bf16[8,64,256]{2,1,0:T(8,128)(2,1)}, bf16[8,64,256]{2,1,0:T(8,128)(2,1)S(1)}, u32[]{:S(2)}, u32[]{:S(2)}) collective-permute-start(bf16[8,64,256]{2,1,0:T(8,128)(2,1)} %get-tuple-element.88.refs_0_), channel_id=1, source_target_pairs={{0,2},{1,3},{2,0},{3,1},{4,6},{5,7},{6,4},{7,5},{8,10},{9,11},{10,... | collective-permute-start | bytes 786440 | tf_op jit(solution)/shard_map/ppermute | solution.py:122
  132.1 18.9 %collective-permute-start.21 = (bf16[8,64,256]{2,1,0:T(8,128)(2,1)}, bf16[8,64,256]{2,1,0:T(8,128)(2,1)S(1)}, u32[]{:S(2)}, u32[]{:S(2)}) collective-permute-start(bf16[8,64,256]{2,1,0:T(8,128)(2,1)} %get-tuple-element.88.refs_0_), channel_id=1, source_target_pairs={{0,1},{1,0},{2,3},{3,2},{4,5},{5,4},{6,7},{7,6},{8,9},{9,8},{10,11... | collective-permute-start | bytes 786440 | tf_op jit(solution)/shard_map/ppermute | solution.py:122
  170.1 12.8 %collective-permute-start.25 = (bf16[3,256,1408]{2,1,0:T(8,128)(2,1)}, bf16[3,256,1408]{2,1,0:T(8,128)(2,1)S(1)}, u32[]{:S(2)}, u32[]{:S(2)}) collective-permute-start(bf16[3,256,1408]{2,1,0:T(8,128)(2,1)} %get-tuple-element.91.three_ref.refs_4_), channel_id=1, source_target_pairs={{0,8},{4,12},{8,0},{12,4},{16,24},{20,28},{24,16},{28,20},{1,9},{5... | collective-permute-start | bytes 6488072 | tf_op jit(solution)/shard_map/ppermute | solution.py:87
  170.4 12.5 %collective-permute-start.24 = (bf16[4,256,256]{2,1,0:T(8,128)(2,1)}, bf16[4,256,256]{2,1,0:T(8,128)(2,1)S(1)}, u32[]{:S(2)}, u32[]{:S(2)}) collective-permute-start(bf16[4,256,256]{2,1,0:T(8,128)(2,1)} %get-tuple-element.98), channel_id=1, source_target_pairs={{0,8},{4,12},{8,0},{12,4},{16,24},{20,28},{24,16},{28,20},{1,9},{5... | collective-permute-start | bytes 1572872 | tf_op jit(solution)/shard_map/ppermute | solution.py:87
  170.7 24.4 %collective-permute-start.26 = (bf16[8,64,256]{2,1,0:T(8,128)(2,1)}, bf16[8,64,256]{2,1,0:T(8,128)(2,1)S(1)}, u32[]{:S(2)}, u32[]{:S(2)}) collective-permute-start(bf16[8,64,256]{2,1,0:T(8,128)(2,1)} %get-tuple-element.101), channel_id=1, source_target_pairs={{0,1},{1,0},{2,3},{3,2},{4,5},{5,4},{6,7},{7,6},{8,9},{9,8},{10,11... | collective-permute-start | bytes 786440 | tf_op jit(solution)/shard_map/ppermute | solution.py:122
  172.2 22.9 %collective-permute-start.27 = (bf16[8,64,256]{2,1,0:T(8,128)(2,1)}, bf16[8,64,256]{2,1,0:T(8,128)(2,1)S(1)}, u32[]{:S(2)}, u32[]{:S(2)}) collective-permute-start(bf16[8,64,256]{2,1,0:T(8,128)(2,1)} %get-tuple-element.102), channel_id=1, source_target_pairs={{0,2},{1,3},{2,0},{3,1},{4,6},{5,7},{6,4},{7,5},{8,10},{9,11},{10,... | collective-permute-start | bytes 786440 | tf_op jit(solution)/shard_map/ppermute | solution.py:122
  174.6 20.6 %collective-permute-start.28 = (bf16[8,64,256]{2,1,0:T(8,128)(2,1)}, bf16[8,64,256]{2,1,0:T(8,128)(2,1)S(1)}, u32[]{:S(2)}, u32[]{:S(2)}) collective-permute-start(bf16[8,64,256]{2,1,0:T(8,128)(2,1)} %get-tuple-element.103), channel_id=1, source_target_pairs={{0,3},{1,2},{2,1},{3,0},{4,7},{5,6},{6,5},{7,4},{8,11},{9,10},{10,... | collective-permute-start | bytes 786440 | tf_op jit(solution)/shard_map/ppermute | solution.py:122
  199.3 11.4 %collective-permute-start.31 = (bf16[8,64,256]{2,1,0:T(8,128)(2,1)}, bf16[8,64,256]{2,1,0:T(8,128)(2,1)S(1)}, u32[]{:S(2)}, u32[]{:S(2)}) collective-permute-start(bf16[8,64,256]{2,1,0:T(8,128)(2,1)} %get-tuple-element.104.refs_0_), channel_id=1, source_target_pairs={{0,3},{1,2},{2,1},{3,0},{4,7},{5,6},{6,5},{7,4},{8,11},{9,10},{10,... | collective-permute-start | bytes 786440 | tf_op jit(solution)/shard_map/ppermute | solution.py:122
  202.6 23.2 %collective-permute-start.30 = (bf16[8,64,256]{2,1,0:T(8,128)(2,1)}, bf16[8,64,256]{2,1,0:T(8,128)(2,1)S(1)}, u32[]{:S(2)}, u32[]{:S(2)}) collective-permute-start(bf16[8,64,256]{2,1,0:T(8,128)(2,1)} %get-tuple-element.104.refs_0_), channel_id=1, source_target_pairs={{0,2},{1,3},{2,0},{3,1},{4,6},{5,7},{6,4},{7,5},{8,10},{9,11},{10,... | collective-permute-start | bytes 786440 | tf_op jit(solution)/shard_map/ppermute | solution.py:122
  204.4 21.4 %collective-permute-start.29 = (bf16[8,64,256]{2,1,0:T(8,128)(2,1)}, bf16[8,64,256]{2,1,0:T(8,128)(2,1)S(1)}, u32[]{:S(2)}, u32[]{:S(2)}) collective-permute-start(bf16[8,64,256]{2,1,0:T(8,128)(2,1)} %get-tuple-element.104.refs_0_), channel_id=1, source_target_pairs={{0,1},{1,0},{2,3},{3,2},{4,5},{5,4},{6,7},{7,6},{8,9},{9,8},{10,11... | collective-permute-start | bytes 786440 | tf_op jit(solution)/shard_map/ppermute | solution.py:122
  225.7 16.1 %collective-permute-start.32 = (bf16[8,64,256]{2,1,0:T(8,128)(2,1)}, bf16[8,64,256]{2,1,0:T(8,128)(2,1)}, u32[]{:S(2)}, u32[]{:S(2)}) collective-permute-start(bf16[8,64,256]{2,1,0:T(8,128)(2,1)} %get-tuple-element.105), channel_id=1, source_target_pairs={{0,1},{1,0},{2,3},{3,2},{4,5},{5,4},{6,7},{7,6},{8,9},{9,8},{10,11... | collective-permute-start | bytes 786440 | tf_op jit(solution)/shard_map/ppermute | solution.py:122
  226.4 22.1 %collective-permute-start.33 = (bf16[8,64,256]{2,1,0:T(8,128)(2,1)}, bf16[8,64,256]{2,1,0:T(8,128)(2,1)}, u32[]{:S(2)}, u32[]{:S(2)}) collective-permute-start(bf16[8,64,256]{2,1,0:T(8,128)(2,1)} %get-tuple-element.106), channel_id=1, source_target_pairs={{0,2},{1,3},{2,0},{3,1},{4,6},{5,7},{6,4},{7,5},{8,10},{9,11},{10,... | collective-permute-start | bytes 786440 | tf_op jit(solution)/shard_map/ppermute | solution.py:122
  229.7 18.7 %collective-permute-start.34 = (bf16[8,64,256]{2,1,0:T(8,128)(2,1)}, bf16[8,64,256]{2,1,0:T(8,128)(2,1)}, u32[]{:S(2)}, u32[]{:S(2)}) collective-permute-start(bf16[8,64,256]{2,1,0:T(8,128)(2,1)} %get-tuple-element.107), channel_id=1, source_target_pairs={{0,3},{1,2},{2,1},{3,0},{4,7},{5,6},{6,5},{7,4},{8,11},{9,10},{10,... | collective-permute-start | bytes 786440 | tf_op jit(solution)/shard_map/ppermute | solution.py:122
  240.2 35.8 %collective-permute-start.38 = (bf16[4,256,256]{2,1,0:T(8,128)(2,1)}, bf16[4,256,256]{2,1,0:T(8,128)(2,1)S(1)}, u32[]{:S(2)}, u32[]{:S(2)}) collective-permute-start(bf16[4,256,256]{2,1,0:T(8,128)(2,1)} %get-tuple-element.111), channel_id=1, source_target_pairs={{0,8},{4,12},{8,0},{12,4},{16,24},{20,28},{24,16},{28,20},{1,9},{5... | collective-permute-start | bytes 1572872 | tf_op jit(solution)/shard_map/ppermute | solution.py:87
  240.3 35.8 %collective-permute-start.39 = (bf16[2,256,512]{2,1,0:T(8,128)(2,1)}, bf16[2,256,512]{2,1,0:T(8,128)(2,1)S(1)}, u32[]{:S(2)}, u32[]{:S(2)}) collective-permute-start(bf16[2,256,512]{2,1,0:T(8,128)(2,1)} %get-tuple-element.113), channel_id=1, source_target_pairs={{4,0},{5,1},{6,2},{7,3},{12,8},{13,9},{14,10},{15,11},{20,16},{21,... | collective-permute-start | bytes 1572872 | tf_op jit(solution)/shard_map/ppermute | solution.py:683
  250.7 8.6 %collective-permute-start.37 = (bf16[8,64,256]{2,1,0:T(8,128)(2,1)}, bf16[8,64,256]{2,1,0:T(8,128)(2,1)S(1)}, u32[]{:S(2)}, u32[]{:S(2)}) collective-permute-start(bf16[8,64,256]{2,1,0:T(8,128)(2,1)} %block_out.1.refs_0_), channel_id=1, source_target_pairs={{0,3},{1,2},{2,1},{3,0},{4,7},{5,6},{6,5},{7,4},{8,11},{9,10},{10,... | collective-permute-start | bytes 786440 | tf_op jit(solution)/shard_map/ppermute | solution.py:122
  253.1 22.9 %collective-permute-start.36 = (bf16[8,64,256]{2,1,0:T(8,128)(2,1)}, bf16[8,64,256]{2,1,0:T(8,128)(2,1)S(1)}, u32[]{:S(2)}, u32[]{:S(2)}) collective-permute-start(bf16[8,64,256]{2,1,0:T(8,128)(2,1)} %block_out.1.refs_0_), channel_id=1, source_target_pairs={{0,2},{1,3},{2,0},{3,1},{4,6},{5,7},{6,4},{7,5},{8,10},{9,11},{10,... | collective-permute-start | bytes 786440 | tf_op jit(solution)/shard_map/ppermute | solution.py:122
  257.6 18.4 %collective-permute-start.35 = (bf16[8,64,256]{2,1,0:T(8,128)(2,1)}, bf16[8,64,256]{2,1,0:T(8,128)(2,1)S(1)}, u32[]{:S(2)}, u32[]{:S(2)}) collective-permute-start(bf16[8,64,256]{2,1,0:T(8,128)(2,1)} %block_out.1.refs_0_), channel_id=1, source_target_pairs={{0,1},{1,0},{2,3},{3,2},{4,5},{5,4},{6,7},{7,6},{8,9},{9,8},{10,11... | collective-permute-start | bytes 786440 | tf_op jit(solution)/shard_map/ppermute | solution.py:122
  284.9 11.8 %collective-permute-start.49 = (bf16[3,256,512]{2,1,0:T(8,128)(2,1)}, bf16[3,256,512]{2,1,0:T(8,128)(2,1)S(1)}, u32[]{:S(2)}, u32[]{:S(2)}) collective-permute-start(bf16[3,256,512]{2,1,0:T(8,128)(2,1)} %get-tuple-element.130.refs_2_), channel_id=1, source_target_pairs={{0,8},{4,12},{8,0},{12,4},{16,24},{20,28},{24,16},{28,20},{1,9},{5... | collective-permute-start | bytes 2359304 | tf_op jit(solution)/shard_map/ppermute | solution.py:87
  286.0 22.1 %collective-permute-start.42 = (bf16[8,64,256]{2,1,0:T(8,128)(2,1)}, bf16[8,64,256]{2,1,0:T(8,128)(2,1)S(1)}, u32[]{:S(2)}, u32[]{:S(2)}) collective-permute-start(bf16[8,64,256]{2,1,0:T(8,128)(2,1)} %get-tuple-element.119), channel_id=1, source_target_pairs={{0,1},{1,0},{2,3},{3,2},{4,5},{5,4},{6,7},{7,6},{8,9},{9,8},{10,11... | collective-permute-start | bytes 786440 | tf_op jit(solution)/shard_map/ppermute | solution.py:122
  286.0 22.1 %collective-permute-start.43 = (bf16[8,64,256]{2,1,0:T(8,128)(2,1)}, bf16[8,64,256]{2,1,0:T(8,128)(2,1)S(1)}, u32[]{:S(2)}, u32[]{:S(2)}) collective-permute-start(bf16[8,64,256]{2,1,0:T(8,128)(2,1)} %get-tuple-element.120), channel_id=1, source_target_pairs={{0,2},{1,3},{2,0},{3,1},{4,6},{5,7},{6,4},{7,5},{8,10},{9,11},{10,... | collective-permute-start | bytes 786440 | tf_op jit(solution)/shard_map/ppermute | solution.py:122
  289.2 18.9 %collective-permute-start.44 = (bf16[8,64,256]{2,1,0:T(8,128)(2,1)}, bf16[8,64,256]{2,1,0:T(8,128)(2,1)S(1)}, u32[]{:S(2)}, u32[]{:S(2)}) collective-permute-start(bf16[8,64,256]{2,1,0:T(8,128)(2,1)} %get-tuple-element.121), channel_id=1, source_target_pairs={{0,3},{1,2},{2,1},{3,0},{4,7},{5,6},{6,5},{7,4},{8,11},{9,10},{10,... | collective-permute-start | bytes 786440 | tf_op jit(solution)/shard_map/ppermute | solution.py:122
  303.2 24.1 %collective-permute-start.50 = (bf16[2,4,256,256]{3,2,1,0:T(8,128)(2,1)}, bf16[2,4,256,256]{3,2,1,0:T(8,128)(2,1)S(1)}, u32[]{:S(2)}, u32[]{:S(2)}) collective-permute-start(bf16[2,4,256,256]{3,2,1,0:T(8,128)(2,1)} %get-tuple-element.133), channel_id=1, source_target_pairs={{0,16},{4,20},{8,24},{12,28},{16,0},{20,4},{24,8},{28,12},{1,17},{... | collective-permute-start | bytes 3145736 | tf_op jit(solution)/shard_map/ppermute | solution.py:87
  307.0 25.7 %collective-permute-start.52 = (bf16[2,4,256,256]{3,2,1,0:T(8,128)(2,1)}, bf16[2,4,256,256]{3,2,1,0:T(8,128)(2,1)S(1)}, u32[]{:S(2)}, u32[]{:S(2)}) collective-permute-start(bf16[2,4,256,256]{3,2,1,0:T(8,128)(2,1)} %get-tuple-element.135), channel_id=1, source_target_pairs={{0,4},{4,0},{8,12},{12,8},{16,20},{20,16},{24,28},{28,24},{1,5},{5... | collective-permute-start | bytes 3145736 | tf_op jit(solution)/shard_map/ppermute | solution.py:87
  312.1 25.8 %collective-permute-start.47 = (bf16[544,256]{1,0:T(8,128)(2,1)}, bf16[544,256]{1,0:T(8,128)(2,1)S(1)}, u32[]{:S(2)}, u32[]{:S(2)}) collective-permute-start(bf16[544,256]{1,0:T(8,128)(2,1)} %input_grad.1.refs_0_), channel_id=1, source_target_pairs={{0,3},{1,2},{2,1},{3,0},{4,7},{5,6},{6,5},{7,4},{8,11},{9,10},{10,... | collective-permute-start | bytes 835592 | tf_op jit(solution)/shard_map/ppermute | solution.py:122
  314.8 24.0 %collective-permute-start.46 = (bf16[544,256]{1,0:T(8,128)(2,1)}, bf16[544,256]{1,0:T(8,128)(2,1)S(1)}, u32[]{:S(2)}, u32[]{:S(2)}) collective-permute-start(bf16[544,256]{1,0:T(8,128)(2,1)} %input_grad.1.refs_0_), channel_id=1, source_target_pairs={{0,2},{1,3},{2,0},{3,1},{4,6},{5,7},{6,4},{7,5},{8,10},{9,11},{10,... | collective-permute-start | bytes 835592 | tf_op jit(solution)/shard_map/ppermute | solution.py:122
  318.5 20.2 %collective-permute-start.45 = (bf16[544,256]{1,0:T(8,128)(2,1)}, bf16[544,256]{1,0:T(8,128)(2,1)S(1)}, u32[]{:S(2)}, u32[]{:S(2)}) collective-permute-start(bf16[544,256]{1,0:T(8,128)(2,1)} %input_grad.1.refs_0_), channel_id=1, source_target_pairs={{0,1},{1,0},{2,3},{3,2},{4,5},{5,4},{6,7},{7,6},{8,9},{9,8},{10,11... | collective-permute-start | bytes 835592 | tf_op jit(solution)/shard_map/ppermute | solution.py:122
  328.3 13.8 %collective-permute-start.51 = (bf16[1,4,256,256]{3,2,1,0:T(8,128)(2,1)}, bf16[1,4,256,256]{3,2,1,0:T(8,128)(2,1)S(1)}, u32[]{:S(2)}, u32[]{:S(2)}) collective-permute-start(bf16[1,4,256,256]{3,2,1,0:T(8,128)(2,1)} %add_convert_fusion.1), channel_id=1, source_target_pairs={{0,4},{4,0},{8,12},{12,8},{16,20},{20,16},{24,28},{28,24},{1,5},{5... | collective-permute-start | bytes 1572872 | tf_op jit(solution)/shard_map/ppermute | solution.py:87
  333.9 9.9 %collective-permute-start.53 = (bf16[1,4,256,256]{3,2,1,0:T(8,128)(2,1)}, bf16[1,4,256,256]{3,2,1,0:T(8,128)(2,1)S(1)}, u32[]{:S(2)}, u32[]{:S(2)}) collective-permute-start(bf16[1,4,256,256]{3,2,1,0:T(8,128)(2,1)} %add_convert_fusion), channel_id=1, source_target_pairs={{0,16},{4,20},{8,24},{12,28},{16,0},{20,4},{24,8},{28,12},{1,17},{... | collective-permute-start | bytes 1572872 | tf_op jit(solution)/shard_map/ppermute | solution.py:87
  (52 other events, 432.1 us)
Sparse Core Ops, SparseCore 0:
  47.4 107.2 all-gather.2
  204.5 100.1 reduce-scatter.1

commit v4 on v3

--- a/solution.py
+++ b/solution.py
@@ -30,10 +30,13 @@
 )
 
 
+VMEM = dict(one_grad=32, attention_weights=24, input_grad=24, input_grad_rows=24, outputs=24)
+
+
 def params(name):
     return dict(
         name=name,
-        compiler_params=pltpu.CompilerParams(vmem_limit_bytes=56 * 2**20),
+        compiler_params=pltpu.CompilerParams(vmem_limit_bytes=VMEM.get(name, 56) * 2**20),
         cost_estimate=pl.CostEstimate(
             flops=int(1.15e9 * WEIGHT.get(name, 0)), bytes_accessed=0, transcendentals=0
         ),
@@ -96,6 +99,19 @@
             slots[k ^ self.core] = self.across(value)
         return slots
 
+    def near(self, shard):
+        return {0: shard} | {bit: self.swap(shard, bit) for bit in self.up}
+
+    def pass_on(self, slots, *after):
+        first = tie(slots[self.up[0]], after)
+        slots = dict(slots)
+        for k in self.kept:
+            if k not in slots:
+                source = k & -k
+                value = first if source == self.up[0] else slots[source]
+                slots[k] = self.swap(value, k ^ source)
+        return slots | {k ^ self.core: self.across(v) for k, v in slots.items()}
+
     def halves(self, order):
         slots = sorted(self.kept, key=lambda k: tuple(not k & bit for bit in order))
         return slots[: len(slots) // 2], slots[len(slots) // 2 :]
@@ -154,14 +170,22 @@
             ref[i] = from_ref[order_ref[k]]
 
 
-def norm_kernel(slots, order_ref, x_ref, gain_ref, bias_ref, kept_ref, sent_ref, normed):
-    normal, _ = row_stats(split(x_ref[...].astype(f32), normed.shape[0]))
+def norm_kernel(
+    slots, order_ref, at_ref, x_ref, gain_ref, bias_ref, flat_ref, kept_ref, sent_ref, chunk_ref, normed
+):
+    count, _, width = normed.shape
+    rows = chunk_ref.shape[0]
+    chunk_ref[...] = x_ref[pl.ds(pl.multiple_of(at_ref[0] * rows, rows), rows), :]
+    normal, _ = row_stats(split(x_ref[...].astype(f32), count))
     normed[...] = (normal * gain_ref[...] + bias_ref[...]).astype(bf16)
     by_slot(slots, order_ref, normed, kept_ref, sent_ref)
-
-
-def reorder_kernel(slots, order_ref, at_ref, x_ref, out_ref, kept_ref, sent_ref, slices):
+    for k in range(count):
+        flat_ref[:, k * width : (k + 1) * width] = normed[order_ref[k]]
+
+
+def reorder_kernel(slots, order_ref, at_ref, x_ref, out_ref, kept_ref, sent_ref, chunk_ref, slices):
     rows = x_ref.shape[0] // at_ref.shape[0]
+    chunk_ref[...] = x_ref[pl.ds(pl.multiple_of(at_ref[0] * rows, rows), rows), :]
     for j in range(at_ref.shape[0]):
         block = x_ref[pl.ds(pl.multiple_of(at_ref[j] * rows, rows), rows), :]
         out_ref[j * rows : (j + 1) * rows, :] = block
@@ -178,15 +202,14 @@
     return jnp.concatenate(parts, axis=1)
 
 
-def qkv_kernel(slots, kept_ref, sent_ref, bias_ref, table_ref, *refs):
+def qkv_kernel(x_ref, bias_ref, table_ref, *refs):
     weights, (q_ref, kv_ref) = refs[:-2], refs[-2:]
-    feat = q_ref.shape[1]
-    x = {k: ref[i] for ref, which in zip((kept_ref, sent_ref), slots) for i, k in enumerate(which)}
+    feat, width = q_ref.shape[1], weights[0].shape[1]
     for cols in tiles(feat):
         for j in range(3):
             total = bias_ref[j, :, cols]
             for k, weight in enumerate(weights):
-                total = total + dot(x[k], weight[j, :, cols])
+                total = total + dot(x_ref[:, k * width : (k + 1) * width], weight[j, :, cols])
             if j < 2:
                 total = spin(total, table_ref[...], 1)
             if j == 0:
@@ -209,18 +232,19 @@
     scale = HD**-0.5
     for pair in range(feat // (2 * HD)):
         cols = slice(pair * 2 * HD, (pair + 1) * 2 * HD)
-        q = q_ref[:, cols]
-        k = jnp.concatenate([early_ref[0, :, cols], here_ref[0, :, cols]], axis=0)
-        v = jnp.concatenate([early_ref[1, :, cols], here_ref[1, :, cols]], axis=0)
+        q = q_ref[:, cols] * scale
         out = []
         for h in range(2):
-            mask = head_mask(rows, h)
-            scores = dot(jnp.where(mask, q, 0), k, NT) * scale + hide_ref[...]
-            top = jnp.max(scores, axis=-1, keepdims=True)
-            exps = jnp.exp(scores - top)
-            total = jnp.sum(exps, axis=-1, keepdims=True)
+            mine = jnp.where(head_mask(rows, h), q, 0)
+            first = dot(mine, early_ref[0, :, cols], NT) + hide_ref[:, :rows]
+            second = dot(mine, here_ref[0, :, cols], NT) + hide_ref[:, rows:]
+            top = jnp.max(jnp.maximum(first, second), axis=-1, keepdims=True)
+            first, second = jnp.exp(first - top), jnp.exp(second - top)
+            total = jnp.sum(first + second, axis=-1, keepdims=True)
             log_ref[2 * pair + h] = top + jnp.log(total)
-            out.append(dot((exps / total).astype(bf16), v))
+            mixed = dot(first.astype(bf16), early_ref[1, :, cols])
+            mixed = mixed + dot(second.astype(bf16), here_ref[1, :, cols])
+            out.append(mixed * (1.0 / total))
         att_ref[:, cols] = jnp.where(head_mask(rows, 0), out[0], out[1]).astype(bf16)
     for k in range(count):
         part_ref[order_ref[k]] = dot(att_ref[...], weights[k][...])
@@ -244,14 +268,12 @@
     down_ref[...] = total_ref[2 * width :].astype(f32).T
 
 
-def mid_kernel(at_ref, x_ref, gain_ref, bias_ref, own_ref, *refs):
+def mid_kernel(x_ref, gain_ref, bias_ref, own_ref, *refs):
     mid_ref, normed_ref = refs[-2:]
-    rows = own_ref.shape[1]
     total = own_ref[...]
     for ref in refs[:-2]:
         total = total + ref[...].astype(f32)
-    block = x_ref[pl.ds(pl.multiple_of(at_ref[0] * rows, rows), rows), :].astype(f32)
-    mid = split(block, own_ref.shape[0]) + total
+    mid = split(x_ref[...].astype(f32), own_ref.shape[0]) + total
     mid_ref[...] = mid
     normal, _ = row_stats(mid)
     normed_ref[...] = (normal * gain_ref[...] + bias_ref[...]).astype(bf16)
@@ -314,10 +336,17 @@
             hidden_grad * up_pre * sigma * (1.0 + gate_pre * (1.0 - sigma))
         ).astype(bf16)
         up_grad_ref[:, cols] = (hidden_grad * silu).astype(bf16)
-    for n in range(own_ref.shape[0]):
-        at = slice(n * width, (n + 1) * width)
-        total = dot(gate_grad_ref[...], gate[at], NT) + dot(up_grad_ref[...], up[at], NT)
-        cut(n, total, own_ref, sends)
+    two_grad = lambda at: dot(gate_grad_ref[...], gate[at], NT) + dot(up_grad_ref[...], up[at], NT)
+    cut_all(two_grad, own_ref, sends)
+
+
+def cut_all(product, own_ref, sends):
+    count, _, width = own_ref.shape
+    group = max(1, 1024 // width)
+    for start in range(0, count, group):
+        total = product(slice(start * width, (start + group) * width))
+        for n in range(group):
+            cut(start + n, total[:, n * width : (n + 1) * width], own_ref, sends)
 
 
 def cut(n, total, own_ref, sends):
@@ -332,9 +361,7 @@
     hidden_ref = three_ref.at[2]
     for copy in fetch(all_ref, 2, down, sem):
         copy.wait()
-    count, _, width = own_ref.shape
-    for n in range(count):
-        cut(n, dot(hidden_ref[...], down[n * width : (n + 1) * width], NT), own_ref, sends)
+    cut_all(lambda at: dot(hidden_ref[...], down[at], NT), own_ref, sends)
 
 
 def block_out_kernel(mid_ref, own_ref, *refs):
@@ -345,11 +372,17 @@
 
 
 def ffn_weights_kernel(place_ref, *refs):
-    x, cot, grads, out_ref = refs[:2], refs[2:4], refs[4:6], refs[6]
-    width = x[0].shape[2]
+    x, cot, grads, out_ref, both = refs[:2], refs[2:4], refs[4:6], refs[6], refs[7]
+    tok, width = x[0].shape[1:]
+
+    @pl.when(pl.program_id(0) == 0)
+    def _():
+        for c, ref in enumerate(grads):
+            both[:, c * tok : (c + 1) * tok, :] = ref[...]
+
     for i, left in enumerate((x, x, cot)):
-        total = dot(left[0][0], grads[0][i], TN) + dot(left[1][0], grads[1][i], TN)
-        out_ref[i * width : (i + 1) * width] = total.astype(bf16)
+        left = jnp.concatenate([left[0][0], left[1][0]], axis=0)
+        out_ref[i * width : (i + 1) * width] = dot(left, both[i], TN).astype(bf16)
 
 
 def norm_back(normal, inv, grad, gain):
@@ -362,7 +395,7 @@
     return jnp.sum(x3, axis=1, keepdims=True)
 
 
-def mid_back_kernel(mid_ref, cot_ref, gain_ref, own_ref, *refs):
+def mid_back_kernel(cot_ref, mid_ref, gain_ref, own_ref, *refs):
     grad_ref, low_ref, gain_grad_ref, bias_grad_ref = refs[-4:]
     total = own_ref[...]
     for ref in refs[:-4]:
@@ -370,7 +403,7 @@
     normal, inv = row_stats(mid_ref[...])
     gain_grad_ref[...] = token_sum(total * normal)
     bias_grad_ref[...] = token_sum(total)
-    cot = split(cot_ref[: mid_ref.shape[1]].astype(f32), mid_ref.shape[0])
+    cot = split(cot_ref[...].astype(f32), mid_ref.shape[0])
     grad = cot + norm_back(normal, inv, total, gain_ref[...])
     grad_ref[...] = grad
     low_ref[...] = grad.astype(bf16)
@@ -471,27 +504,43 @@
                     ref[i, j] = total.astype(bf16)
 
 
-def attention_out_kernel(terms, *refs):
-    qkv_ref, out_ref = refs[-2:]
+def outputs_kernel(terms, own_ref, other_ref, *refs):
+    parts, outs = refs[: 2 * terms], refs[2 * terms :]
+    vector_refs, (bias_ref, qkv_ref, out_ref) = outs[:-3], outs[-3:]
     part = qkv_ref.shape[2] // 2
     for h in range(2):
         cols = slice(h * part, (h + 1) * part)
         for j in range(4):
-            total = sum(ref[ref.shape[0] - 1, j].astype(f32) for ref in refs[h * terms : (h + 1) * terms])
+            group = parts[h * terms : (h + 1) * terms]
+            total = sum(ref[ref.shape[0] - 1, j].astype(f32) for ref in group)
             if j < 3:
                 qkv_ref[j, :, cols] = total
             else:
                 out_ref[cols, :] = total.T
-
-
-def input_grad_kernel(at_ref, x_ref, gain_ref, mid_grad_ref, own_ref, small_ref, *refs):
+    small = own_ref[...] + other_ref[...]
+    rows, width = vector_refs[0].shape[0], small.shape[1]
+    count = rows * vector_refs[0].shape[1] // width
+    per = width // vector_refs[0].shape[1]
+    for v, ref in enumerate(vector_refs):
+        for n in range(count):
+            for i in range(per):
+                lanes = slice(i * ref.shape[1], (i + 1) * ref.shape[1])
+                row = v * count + n
+                ref[n * per + i : n * per + i + 1] = small[row : row + 1, lanes]
+    row = len(vector_refs) * count
+    for j in range(3):
+        for at in range(0, bias_ref.shape[1], width):
+            bias_ref[j : j + 1, at : at + width] = small[row : row + 1]
+            row += 1
+
+
+def input_grad_kernel(x_ref, gain_ref, mid_grad_ref, own_ref, small_ref, *refs):
     parts, out_ref = refs[:-1], refs[-1]
     count, rows, width = own_ref.shape
     total = own_ref[...]
     for ref in parts:
         total = total + ref[...].astype(f32)
-    block = x_ref[pl.ds(pl.multiple_of(at_ref[0] * rows, rows), rows), :].astype(f32)
-    normal, inv = row_stats(split(block, count))
+    normal, inv = row_stats(split(x_ref[...].astype(f32), count))
     grad = mid_grad_ref[...] + norm_back(normal, inv, total, gain_ref[...])
     out_ref[: count * rows] = grad.astype(bf16).reshape(count * rows, width)
     out_ref[count * rows :] = small_ref[: 4 * count].astype(bf16)
@@ -572,35 +621,36 @@
     slots = (plane.kept, plane.sent)
     slice_pair = (shape((count // 2, tok, width), bf16),) * 2
     slices = pltpu.VMEM((count, tok, width), bf16)
-    one_kept, one_sent = call(
-        functools.partial(norm_kernel, slots), "norm_one", slice_pair,
-        (order, block_in, by_slice(attn_gain), by_slice(attn_bias)), [SM] + [VM] * 3,
+    one_flat, one_kept, one_sent, in_chunk = call(
+        functools.partial(norm_kernel, slots), "norm_one",
+        (shape((tok, model), bf16), *slice_pair, shape((chunk, model), bf16)),
+        (order, at, block_in, by_slice(attn_gain), by_slice(attn_bias)), [SM, SM] + [VM] * 3,
         scratch=[slices],
     )
-    cot, cot_kept, cot_sent = call(
+    cot, cot_kept, cot_sent, cot_chunk = call(
         functools.partial(reorder_kernel, slots), "cotangent_rows",
-        (shape((tok, model), bf16), *slice_pair), (order, at, out_cotangent), [SM, SM, VM],
+        (shape((tok, model), bf16), *slice_pair, shape((chunk, model), bf16)), (order, at, out_cotangent), [SM, SM, VM],
         scratch=[slices],
     )
 
-    qkv_slots = plane.gather(qkv_weight)
+    bias_rows = qkv_bias.reshape(3, 1, feat)
+    ffn_shard = call(
+        pack_kernel, "ffn_shard", shape((3 * width, hid), bf16),
+        (gate_up_weight, down_weight), [VM, VM],
+    )
+    qkv_slots = plane.gather(qkv_weight, ffn_shard, one_flat, bias_rows, tables, hide)
     qkv_list = [qkv_slots[k] for k in range(count)]
-    ffn_shard = call(
-        pack_kernel, "ffn_shard", shape((3 * width, hid), bf16), (gate_up_weight, down_weight),
-        [VM, VM],
-    )
-    out_slots = plane.gather(tie(out_weight, ffn_shard))
-    out_list = [out_slots[k] for k in range(count)]
+    out_near = plane.near(tie(out_weight, ffn_shard))
     first = (qkv_slots[plane.up[0]], qkv_slots[plane.up[-1]])
     ffn_all = lax.all_gather(tie(ffn_shard, first), PLANE, axis=0, tiled=False)
 
     queries, here = call(
-        functools.partial(qkv_kernel, slots), "qkv",
-        (shape((tok, feat), bf16), shape((2, tok, feat), bf16)),
-        (one_kept, one_sent, qkv_bias.reshape(3, 1, feat), tables, *qkv_list),
-        [VM] * (4 + count),
+        qkv_kernel, "qkv", (shape((tok, feat), bf16), shape((2, tok, feat), bf16)),
+        (one_flat, bias_rows, tables, *qkv_list), [VM] * (3 + count),
     )
     early = lax.ppermute(here, "context", [(i, i + 1) for i in range(plane.context - 1)])
+    out_slots = plane.pass_on(out_near, queries)
+    out_list = [out_slots[k] for k in range(count)]
     sends = [shape((count, chunk, width), bf16)] * (peers - 1)
     own_shape = shape((count, chunk, width), f32)
     attended, logs, own, *parts = call(
@@ -615,8 +665,7 @@
     own = tie(own, cot_got, one_got, att_got)
     mid, normed_chunk = call(
         mid_kernel, "mid", (own_shape, sends[0]),
-        (at, block_in, by_slice(ffn_gain), by_slice(ffn_bias), own, *got),
-        [SM] + [VM] * (4 + len(got)),
+        (in_chunk, by_slice(ffn_gain), by_slice(ffn_bias), own, *got), [VM] * (4 + len(got)),
     )
     normed_two = tensor_gather(normed_chunk)
 
@@ -643,25 +692,25 @@
             grid=(count // 2,),
             in_specs=[of_slot] * 4 + [whole] * 2,
             out_specs=pl.BlockSpec((3 * width, hid), lambda i, place: (place[i], 0)),
+            scratch_shapes=[pltpu.VMEM((3, 2 * tok, hid), bf16)],
         ),
         out_shape=shape((count // 2 * 3 * width, hid), bf16),
         **params("ffn_weights"),
     )(place, two_kept, two_got, cot_kept, cot_got, three, three_got)
-    down_own, *down_parts = call(
-        down_kernel, "down", (own_shape, *sends), (three, ffn_all), [VM, HB],
-        scratch=[buffer, pltpu.SemaphoreType.DMA((count,))],
-    )
     ffn_total = lax.psum_scatter(
         ffn_grads, PLANE, scatter_dimension=0, axis_index_groups=plane.groups, tiled=True
     )
-    grad_own = tie(grad_own, ffn_grads, down_own)
+    grad_own = tie(grad_own, ffn_grads)
     vec = shape((count, 1, width), f32)
     mid_grad, low_chunk, ffn_gain_grad, ffn_bias_grad = call(
         mid_back_kernel, "mid_back", (own_shape, sends[0], vec, vec),
-        (mid, cot, by_slice(ffn_gain), grad_own, *got),
-        [VM] * (4 + len(got)),
+        (cot_chunk, mid, by_slice(ffn_gain), grad_own, *got), [VM] * (4 + len(got)),
     )
     low_blocks = tensor_gather(low_chunk)
+    down_own, *down_parts = call(
+        down_kernel, "down", (own_shape, *sends), (tie(three, low_chunk), ffn_all), [VM, HB],
+        scratch=[buffer, pltpu.SemaphoreType.DMA((count,))],
+    )
     down_got = tensor_exchange([None, *tie(down_parts, low_blocks)])
     out_chunk = call(
         block_out_kernel, "block_out", sends[0], (mid, down_own, *down_got),
@@ -707,8 +756,7 @@
     terms_b = scatter(plane, *weight_grads[2:], plane.up)
     grad_chunk = call(
         input_grad_kernel, "input_grad", shape((count * chunk + 4 * count, width), bf16),
-        (at, block_in, by_slice(attn_gain), mid_grad, own, small, *got),
-        [SM] + [VM] * (5 + len(got)),
+        (in_chunk, by_slice(attn_gain), mid_grad, own, small, *got), [VM] * (5 + len(got)),
     )
     grad_blocks = tensor_gather(grad_chunk)
     gate_up_grad, down_grad = call(
@@ -725,19 +773,23 @@
     )
 
     terms = (*terms_a, *terms_b)
-    qkv_grad, out_grad = call(
-        functools.partial(attention_out_kernel, len(terms_a)), "attention_out",
-        (shape((3, width, feat), f32), shape((feat, width), f32)), terms, [VM] * len(terms),
-    )
-    small = small + plane.across(small)
-    vectors = small[: 4 * count].reshape(4, model)
+    lanes = min(width, 128)
+    *vectors, bias_grad, qkv_grad, out_grad = call(
+        functools.partial(outputs_kernel, len(terms_a)), "outputs",
+        (
+            *[shape((model // lanes, lanes), f32)] * 4, shape((3, feat), f32),
+            shape((3, width, feat), f32), shape((feat, width), f32),
+        ),
+        (small, plane.across(small), *terms), [VM] * (2 + len(terms)),
+    )
+    vectors = [v.reshape(model) for v in vectors]
     return (
         block_out,
         input_grad,
         vectors[0],
         vectors[1],
         qkv_grad,
-        small[4 * count :].reshape(3, feat),
+        bias_grad,
         out_grad,
         vectors[2],
         vectors[3],

time: 359 us -> 350 us (0.975)
  Pallas kernels: 104 us -> 93.2 us
  starting transfers between devices: 67 us -> 76.7 us
  local copies, waits for them, and re-layouts: 12.2 us -> 8.61 us
    pallas_call x18, Pallas kernels: 93.5 us -> 82 us  [call(): pl.pallas_call(kernel, out_shape=outs, in_specs=specs, out_specs=jax.tree...]
    ppermute x24, starting transfers between devices: 43.2 us -> 54 us  [tensor_swap(): return lax.ppermute(value, 'tensor', [(i, i ^ j) for i in range(peers)])]
    ppermute x1, waiting for transfers between devices: 17.5 us -> 10.7 us  [on_device(): lax.ppermute(here, 'context', [(i, i + 1) for i in range(plane.context -...]
    unnamed x93 -> x126, local copies, waits for them, and re-layouts: 10.8 us -> 7.81 us
  transfers between devices with their start and end apart: 56 -> 56, of which waited for: 21 -> 21; matrix products, arithmetic and copies ran while one was open for 3% -> 3% of each run, Pallas kernels for 24% -> 21%
where the time goes in v4:
time: 350 us; the launch traced here: 349 us
  waiting for transfers between devices  147 us (42%)
  Pallas kernels  93.2 us (27%)
  starting transfers between devices  76.7 us (22%)
  between operations  14.8 us (4%)
  other arithmetic  9.32 us (3%)
  local copies, waits for them, and re-layouts  8.61 us (2%)
    ppermute x24, waiting for transfers between devices, tensor_swap(): return lax.ppermute(value, 'tensor', [(i, i ^ j) for i in range(peers)])  82.3 us
    pallas_call x18, Pallas kernels, call(): pl.pallas_call(kernel, out_shape=outs, in_specs=specs, out_specs=jax.tree...  82 us
    ppermute x24, starting transfers between devices, tensor_swap(): return lax.ppermute(value, 'tensor', [(i, i ^ j) for i in range(peers)])  54 us
    ppermute x28, waiting for transfers between devices, swap(): return lax.ppermute(value, ('fsdp', 'context'), pairs)  47.1 us
    ppermute x28, starting transfers between devices, swap(): return lax.ppermute(value, ('fsdp', 'context'), pairs)  18.5 us
    pallas_call x1, Pallas kernels, on_device(): pl.pallas_call(ffn_weights_kernel, grid_spec=pltpu.PrefetchScalarGridSpec...  11.2 us
    ppermute x1, waiting for transfers between devices, on_device(): lax.ppermute(here, 'context', [(i, i + 1) for i in range(plane.context -...  10.7 us
    unnamed x126, local copies, waits for them, and re-layouts  7.81 us
  transfers between devices with their start and end apart: 56, of which 21 were waited for; matrix products, arithmetic and copies ran while one was open for 3% of the time, Pallas kernels for 21%

profile of v4, /device:TPU:0, one launch (start us, length us, event | category | flops | bytes accessed | tf_op | source)
XLA Modules:
  0.0 349.4 jit_solution(12743074695620020285)
XLA Ops:
  7.2 4.0 %collective-permute-start.4 = (bf16[3,256,512]{2,1,0:T(8,128)(2,1)}, bf16[3,256,512]{2,1,0:T(8,128)(2,1)S(1)}, u32[]{:S(2)}, u32[]{:S(2)}) collective-permute-start(bf16[3,256,512]{2,1,0:T(8,128)(2,1)} %refs_0_.4), channel_id=1, source_target_pairs={{0,20},{4,16},{8,28},{12,24},{16,4},{20,0},{24,12},{28,8},{1,21},{... | collective-permute-start | bytes 2359304 | tf_op jit(solution)/shard_map/ppermute | solution.py:90
  18.6 3.2 ffn_shard.1
  22.7 3.4 norm_one.1
  26.2 3.6 %collective-permute-done.4.refs_5_ = bf16[3,256,512]{2,1,0:T(8,128)(2,1)S(1)} collective-permute-done((bf16[3,256,512]{2,1,0:T(8,128)(2,1)}, bf16[3,256,512]{2,1,0:T(8,128)(2,1)S(1)}, u32[]{:S(2)}, u32[]{:S(2)}) %collective-permute-start.4) | collective-permute-done | bytes 786464 | tf_op jit(solution)/shard_map/ppermute | solution.py:90
  29.8 16.3 %collective-permute-done.3.refs_4_ = bf16[3,256,512]{2,1,0:T(8,128)(2,1)S(1)} collective-permute-done((bf16[3,256,512]{2,1,0:T(8,128)(2,1)}, bf16[3,256,512]{2,1,0:T(8,128)(2,1)S(1)}, u32[]{:S(2)}, u32[]{:S(2)}) %collective-permute-start.3) | collective-permute-done | bytes 786464 | tf_op jit(solution)/shard_map/ppermute | solution.py:90
  50.8 6.0 %qkv.1 = (bf16[256,512]{1,0:T(8,128)(2,1)}, bf16[2,256,512]{2,1,0:T(8,128)(2,1)}) custom-call(bf16[256,2048]{1,0:T(8,128)(2,1)} %get-tuple-element.87.x_ref, f32[3,1,512]{2,1,0:T(1,128)} %reshape.289.bias_ref, f32[3,256,128]{2,1,0:T(8,128)} %pad_maximum_fusion.table_ref, bf16[3,256,512]{2,1,0:T(8,128)(2,1)} %refs_0_.4, bf16[3,256,512]{2,1,0:T(8,128)(2,1)} %copy-done.12, ...), custom_call_target="tpu_custom_call" | custom-call | flops 11500000256 | tf_op jit(solution)/shard_map/qkv/pallas_call | solution.py:47
  59.3 2.6 collective-permute-start.7
  61.9 9.3 %collective-permute-done.12.refs_5_.refs_9_ = bf16[512,256]{1,0:T(8,128)(2,1)S(1)} collective-permute-done((bf16[512,256]{1,0:T(8,128)(2,1)S(1)}, bf16[512,256]{1,0:T(8,128)(2,1)S(1)}, u32[]{:S(2)}, u32[]{:S(2)}) %collective-permute-start.12) | collective-permute-done | bytes 262176 | tf_op jit(solution)/shard_map/ppermute | solution.py:90
  71.2 2.9 cotangent_rows.1
  74.6 10.7 %collective-permute-done.7.early_ref = bf16[2,256,512]{2,1,0:T(8,128)(2,1)S(1)} collective-permute-done((bf16[2,256,512]{2,1,0:T(8,128)(2,1)}, bf16[2,256,512]{2,1,0:T(8,128)(2,1)S(1)}, u32[]{:S(2)}, u32[]{:S(2)}) %collective-permute-start.7) | collective-permute-done | bytes 524320 | tf_op jit(solution)/shard_map/ppermute | solution.py:651
  86.1 6.3 %attend.1 = (bf16[256,512]{1,0:T(8,128)(2,1)}, f32[8,256,1]{2,1,0:T(8,128)}, f32[8,64,256]{2,1,0:T(8,128)}, bf16[8,64,256]{2,1,0:T(8,128)(2,1)}, bf16[8,64,256]{...) custom-call(s32[8]{0:T(128)} %iota_xor_fusion.order_ref, s32[4]{0:T(128)} %iota_xor_fusion.1.at_ref, ...), custom_call_target="tpu_custom_call" | custom-call | tf_op jit(solution)/shard_map/attend/pallas_call | solution.py:47
  94.1 2.6 collective-permute-start.19
  97.7 8.9 %collective-permute-done.18.refs_0_ = bf16[8,64,256]{2,1,0:T(8,128)(2,1)S(1)} collective-permute-done((bf16[8,64,256]{2,1,0:T(8,128)(2,1)}, bf16[8,64,256]{2,1,0:T(8,128)(2,1)S(1)}, u32[]{:S(2)}, u32[]{:S(2)}) %collective-permute-start.18) | collective-permute-done | bytes 262176 | tf_op jit(solution)/shard_map/ppermute | solution.py:138
  106.6 9.1 %collective-permute-done.19.refs_1_ = bf16[8,64,256]{2,1,0:T(8,128)(2,1)S(1)} collective-permute-done((bf16[8,64,256]{2,1,0:T(8,128)(2,1)}, bf16[8,64,256]{2,1,0:T(8,128)(2,1)S(1)}, u32[]{:S(2)}, u32[]{:S(2)}) %collective-permute-start.19) | collective-permute-done | bytes 262176 | tf_op jit(solution)/shard_map/ppermute | solution.py:138
  116.5 2.4 mid.1
  118.9 2.5 collective-permute-start.23
  121.5 4.4 %collective-permute-start.22 = (bf16[8,64,256]{2,1,0:T(8,128)(2,1)}, bf16[8,64,256]{2,1,0:T(8,128)(2,1)S(1)}, u32[]{:S(2)}, u32[]{:S(2)}) collective-permute-start(bf16[8,64,256]{2,1,0:T(8,128)(2,1)} %get-tuple-element.102.refs_0_), channel_id=1, source_target_pairs={{0,2},{1,3},{2,0},{3,1},{4,6},{5,7},{6,4},{7,5},{8,10},{9,11},{10,... | collective-permute-start | bytes 786440 | tf_op jit(solution)/shard_map/ppermute | solution.py:138
  127.9 16.7 %collective-permute-done.22.refs_2_ = bf16[8,64,256]{2,1,0:T(8,128)(2,1)S(1)} collective-permute-done((bf16[8,64,256]{2,1,0:T(8,128)(2,1)}, bf16[8,64,256]{2,1,0:T(8,128)(2,1)S(1)}, u32[]{:S(2)}, u32[]{:S(2)}) %collective-permute-start.22) | collective-permute-done | bytes 262176 | tf_op jit(solution)/shard_map/ppermute | solution.py:138
  144.6 6.6 %all-gather.3.cloned.1.call-done = bf16[6144,1408]{1,0:T(8,128)(2,1)} async-done(((bf16[768,1408]{1,0:T(8,128)(2,1)}), bf16[6144,1408]{1,0:T(8,128)(2,1)}) %all-gather.3.cloned.1.call-update) | async-done | bytes 17301520 | tf_op jit(solution)/shard_map/all_gather | solution.py:645
  151.2 15.4 %ffn.1 = (bf16[4,256,256]{2,1,0:T(8,128)(2,1)}, bf16[4,256,256]{2,1,0:T(8,128)(2,1)}, bf16[3,256,1408]{2,1,0:T(8,128)(2,1)}, f32[8,64,256]{2,1,0:T(8,128)}, bf16...) custom-call(s32[8]{0:T(128)} %iota_xor_fusion.order_ref, ...), custom_call_target="tpu_custom_call" | custom-call | tf_op jit(solution)/shard_map/ffn/pallas_call | solution.py:47
  168.8 2.4 collective-permute-start.27
  173.9 11.2 %ffn_weights.1 = bf16[3072,1408]{1,0:T(8,128)(2,1)} custom-call(s32[4]{0:T(128)} %pad_add_fusion.place_ref, bf16[4,256,256]{2,1,0:T(8,128)(2,1)} %get-tuple-element.108.refs_0_, bf16[4,256,256]{2,1,0:T(8,128)(2,1)} %copy-done.35, bf16[4,256,256]{2,1,0:T(8,128)(2,1)} %get-tuple-element.110.refs_2_, bf16[4,256,256]{2,1,0:T(8,128)(2,1)} %copy-done.34, ...), custom_call_target="tpu_custom_call" | custom-call | tf_op jit(solution)/shard_map/ffn_weights/pallas_call | solution.py:688
  185.1 5.2 %collective-permute-done.27.refs_1_ = bf16[8,64,256]{2,1,0:T(8,128)(2,1)S(1)} collective-permute-done((bf16[8,64,256]{2,1,0:T(8,128)(2,1)}, bf16[8,64,256]{2,1,0:T(8,128)(2,1)S(1)}, u32[]{:S(2)}, u32[]{:S(2)}) %collective-permute-start.27) | collective-permute-done | bytes 262176 | tf_op jit(solution)/shard_map/ppermute | solution.py:138
  191.1 3.0 mid_back.1
  194.2 2.4 collective-permute-start.31
  196.5 4.2 %collective-permute-start.30 = (bf16[8,64,256]{2,1,0:T(8,128)(2,1)}, bf16[8,64,256]{2,1,0:T(8,128)(2,1)S(1)}, u32[]{:S(2)}, u32[]{:S(2)}) collective-permute-start(bf16[8,64,256]{2,1,0:T(8,128)(2,1)} %get-tuple-element.115.refs_0_), channel_id=1, source_target_pairs={{0,2},{1,3},{2,0},{3,1},{4,6},{5,7},{6,4},{7,5},{8,10},{9,11},{10,... | collective-permute-start | bytes 786440 | tf_op jit(solution)/shard_map/ppermute | solution.py:138
  200.8 7.1 %down.1 = (f32[8,64,256]{2,1,0:T(8,128)}, bf16[8,64,256]{2,1,0:T(8,128)(2,1)}, bf16[8,64,256]{2,1,0:T(8,128)(2,1)}, bf16[8,64,256]{2,1,0:T(8,128)(2,1)}) custom-call(bf16[3,256,1408]{2,1,0:T(8,128)(2,1)} %get-tuple-element.116.refs_4_.three_ref, bf16[8,768,1408]{2,1,0:T(8,128)(2,1)} %bitcast.23), custom_call_target="tpu_custom_call" | custom-call | tf_op jit(solution)/shard_map/down/pallas_call | solution.py:47
  207.9 11.4 %collective-permute-done.30.refs_2_ = bf16[8,64,256]{2,1,0:T(8,128)(2,1)S(1)} collective-permute-done((bf16[8,64,256]{2,1,0:T(8,128)(2,1)}, bf16[8,64,256]{2,1,0:T(8,128)(2,1)S(1)}, u32[]{:S(2)}, u32[]{:S(2)}) %collective-permute-start.30) | collective-permute-done | bytes 262176 | tf_op jit(solution)/shard_map/ppermute | solution.py:138
  219.5 3.0 collective-permute-start.33
  223.9 10.0 %attend_back.1 = (bf16[4,256,256]{2,1,0:T(8,128)(2,1)}, bf16[4,256,256]{2,1,0:T(8,128)(2,1)}, bf16[256,512]{1,0:T(8,128)(2,1)}, f32[2,256,512]{2,1,0:T(8,128)}, bf16[2,256,512]{2,1,0:T(8,128)(2,1)}) custom-call(s32[8]{0:T(128)} %iota_xor_fusion.order_ref, s32[4]{0:T(128)} %iota_xor_fusion.1.at_ref, f32[256,512]{1,0:T(8,128)} %and_select_fusion.hide_ref, ...), custom_call_target="tpu_custom_call" | custom-call | flops 230000001024 | tf_op jit(solution)/shard_map/attend_back/pallas_call | solution.py:47
  235.5 5.7 %collective-permute-done.33.refs_1_ = bf16[8,64,256]{2,1,0:T(8,128)(2,1)} collective-permute-done((bf16[8,64,256]{2,1,0:T(8,128)(2,1)}, bf16[8,64,256]{2,1,0:T(8,128)(2,1)}, u32[]{:S(2)}, u32[]{:S(2)}) %collective-permute-start.33) | collective-permute-done | bytes 262176 | tf_op jit(solution)/shard_map/ppermute | solution.py:138
  241.3 2.4 block_out.1.refs_0_
  243.7 2.4 collective-permute-start.37
  246.2 4.3 %collective-permute-start.36 = (bf16[8,64,256]{2,1,0:T(8,128)(2,1)}, bf16[8,64,256]{2,1,0:T(8,128)(2,1)S(1)}, u32[]{:S(2)}, u32[]{:S(2)}) collective-permute-start(bf16[8,64,256]{2,1,0:T(8,128)(2,1)} %block_out.1.refs_0_), channel_id=1, source_target_pairs={{0,2},{1,3},{2,0},{3,1},{4,6},{5,7},{6,4},{7,5},{8,10},{9,11},{10,... | collective-permute-start | bytes 786440 | tf_op jit(solution)/shard_map/ppermute | solution.py:138
  252.4 16.7 %collective-permute-done.36.refs_2_ = bf16[8,64,256]{2,1,0:T(8,128)(2,1)S(1)} collective-permute-done((bf16[8,64,256]{2,1,0:T(8,128)(2,1)}, bf16[8,64,256]{2,1,0:T(8,128)(2,1)S(1)}, u32[]{:S(2)}, u32[]{:S(2)}) %collective-permute-start.36) | collective-permute-done | bytes 262176 | tf_op jit(solution)/shard_map/ppermute | solution.py:138
  270.1 5.4 %one_grad.1 = (bf16[3,256,512]{2,1,0:T(8,128)(2,1)S(1)}, f32[38,256]{1,0:T(8,128)S(1)}, f32[8,64,256]{2,1,0:T(8,128)S(1)}, bf16[8,64,256]{2,1,0:T(8,128)(2,1)}, ...) custom-call(s32[8]{0:T(128)S(1)} %copy-done.26, s32[4]{0:T(128)S(1)} %copy-done.24, ...), custom_call_target="tpu_custom_call" | custom-call | tf_op jit(solution)/shard_map/one_grad/pallas_call | solution.py:47
  276.3 2.9 collective-permute-start.43
  282.1 3.5 %collective-permute-done.41 = f32[38,256]{1,0:T(8,128)S(1)} collective-permute-done((f32[38,256]{1,0:T(8,128)S(1)}, f32[38,256]{1,0:T(8,128)S(1)}, u32[]{:S(2)}, u32[]{:S(2)}) %collective-permute-start.41) | collective-permute-done | bytes 38944 | tf_op jit(solution)/shard_map/ppermute | solution.py:90
  285.7 2.4 attention_weights.1
  289.5 2.3 block_out_rows.1
  293.2 4.7 %collective-permute-done.43.refs_1_ = bf16[8,64,256]{2,1,0:T(8,128)(2,1)S(1)} collective-permute-done((bf16[8,64,256]{2,1,0:T(8,128)(2,1)}, bf16[8,64,256]{2,1,0:T(8,128)(2,1)S(1)}, u32[]{:S(2)}, u32[]{:S(2)}) %collective-permute-start.43) | collective-permute-done | bytes 262176 | tf_op jit(solution)/shard_map/ppermute | solution.py:138
  299.4 2.4 collective-permute-start.47
  301.9 13.5 %collective-permute-start.46 = (bf16[544,256]{1,0:T(8,128)(2,1)S(1)}, bf16[544,256]{1,0:T(8,128)(2,1)}, u32[]{:S(2)}, u32[]{:S(2)}) collective-permute-start(bf16[544,256]{1,0:T(8,128)(2,1)S(1)} %input_grad.1.refs_0_), channel_id=1, source_target_pairs={{0,2},{1,3},{2,0},{3,1},{4,6},{5,7},{6,4},{7,5},{8,10},{9,11},{10,... | collective-permute-start | bytes 835592 | tf_op jit(solution)/shard_map/ppermute | solution.py:138
  315.4 6.6 %collective-permute-done.50.refs_1_ = bf16[2,4,256,256]{3,2,1,0:T(8,128)(2,1)S(1)} collective-permute-done((bf16[2,4,256,256]{3,2,1,0:T(8,128)(2,1)S(1)}, bf16[2,4,256,256]{3,2,1,0:T(8,128)(2,1)S(1)}, u32[]{:S(2)}, u32[]{:S(2)}) %collective-permute-start.50) | collective-permute-done | bytes 1048608 | tf_op jit(solution)/shard_map/ppermute | solution.py:90
  326.8 4.0 %ffn_out.1 = (f32[2,256,1408]{2,1,0:T(8,128)}, f32[1408,256]{1,0:T(8,128)}) custom-call(bf16[768,1408]{1,0:T(8,128)(2,1)} %reduce-scatter.2.cloned.1.call-done.total_ref), custom_call_target="tpu_custom_call" | custom-call | tf_op jit(solution)/shard_map/ffn_out/pallas_call | solution.py:47
  333.1 3.4 collective-permute-done.51.refs_2_
  336.6 3.0 collective-permute-done.53.refs_5_
  339.6 3.0 outputs.1
  (235 shorter events, 49.1 us)
Async XLA Ops:
  7.2 144.0 %all-gather.3.cloned.1.call-start = ((), (), s32[]{:S(2)}) async-start(), calls=%async_computation.2 | async-start | bytes 19464192 | tf_op jit(solution)/shard_map/all_gather | solution.py:645
  7.2 22.6 %collective-permute-start.4 = (bf16[3,256,512]{2,1,0:T(8,128)(2,1)}, bf16[3,256,512]{2,1,0:T(8,128)(2,1)S(1)}, u32[]{:S(2)}, u32[]{:S(2)}) collective-permute-start(bf16[3,256,512]{2,1,0:T(8,128)(2,1)} %refs_0_.4), channel_id=1, source_target_pairs={{0,20},{4,16},{8,28},{12,24},{16,4},{20,0},{24,12},{28,8},{1,21},{... | collective-permute-start | bytes 2359304 | tf_op jit(solution)/shard_map/ppermute | solution.py:90
  11.2 34.9 %collective-permute-start.3 = (bf16[3,256,512]{2,1,0:T(8,128)(2,1)}, bf16[3,256,512]{2,1,0:T(8,128)(2,1)S(1)}, u32[]{:S(2)}, u32[]{:S(2)}) collective-permute-start(bf16[3,256,512]{2,1,0:T(8,128)(2,1)} %refs_0_.4), channel_id=1, source_target_pairs={{0,16},{4,20},{8,24},{12,28},{16,0},{20,4},{24,8},{28,12},{1,17},{... | collective-permute-start | bytes 2359304 | tf_op jit(solution)/shard_map/ppermute | solution.py:90
  11.7 36.6 %collective-permute-start.1 = (bf16[3,256,512]{2,1,0:T(8,128)(2,1)}, bf16[3,256,512]{2,1,0:T(8,128)(2,1)S(1)}, u32[]{:S(2)}, u32[]{:S(2)}) collective-permute-start(bf16[3,256,512]{2,1,0:T(8,128)(2,1)} %refs_0_.4), channel_id=1, source_target_pairs={{0,8},{4,12},{8,0},{12,4},{16,24},{20,28},{24,16},{28,20},{1,9},{5... | collective-permute-start | bytes 2359304 | tf_op jit(solution)/shard_map/ppermute | solution.py:90
  11.7 34.4 %collective-permute-start = (bf16[3,256,512]{2,1,0:T(8,128)(2,1)}, bf16[3,256,512]{2,1,0:T(8,128)(2,1)S(1)}, u32[]{:S(2)}, u32[]{:S(2)}) collective-permute-start(bf16[3,256,512]{2,1,0:T(8,128)(2,1)} %refs_0_.4), channel_id=1, source_target_pairs={{0,4},{4,0},{8,12},{12,8},{16,20},{20,16},{24,28},{28,24},{1,5},{5... | collective-permute-start | bytes 2359304 | tf_op jit(solution)/shard_map/ppermute | solution.py:90
  46.7 280.1 %reduce-scatter.2.cloned.1.call-start = ((), (), s32[]{:S(2)}) async-start(), calls=%async_computation.1 | async-start | bytes 10813440 | tf_op jit(solution)/shard_map/reduce_scatter | solution.py:700
  46.8 12.4 %collective-permute-start.11 = (bf16[512,256]{1,0:T(8,128)(2,1)S(1)}, bf16[512,256]{1,0:T(8,128)(2,1)S(1)}, u32[]{:S(2)}, u32[]{:S(2)}) collective-permute-start(bf16[512,256]{1,0:T(8,128)(2,1)S(1)} %copy-done.39), channel_id=1, source_target_pairs={{0,16},{4,20},{8,24},{12,28},{16,0},{20,4},{24,8},{28,12},{1,17},{... | collective-permute-start | bytes 786440 | tf_op jit(solution)/shard_map/ppermute | solution.py:90
  48.3 10.9 %collective-permute-start.9 = (bf16[512,256]{1,0:T(8,128)(2,1)S(1)}, bf16[512,256]{1,0:T(8,128)(2,1)S(1)}, u32[]{:S(2)}, u32[]{:S(2)}) collective-permute-start(bf16[512,256]{1,0:T(8,128)(2,1)S(1)} %copy-done.39), channel_id=1, source_target_pairs={{0,8},{4,12},{8,0},{12,4},{16,24},{20,28},{24,16},{28,20},{1,9},{5... | collective-permute-start | bytes 786440 | tf_op jit(solution)/shard_map/ppermute | solution.py:90
  48.5 8.6 %collective-permute-start.8 = (bf16[512,256]{1,0:T(8,128)(2,1)S(1)}, bf16[512,256]{1,0:T(8,128)(2,1)S(1)}, u32[]{:S(2)}, u32[]{:S(2)}) collective-permute-start(bf16[512,256]{1,0:T(8,128)(2,1)S(1)} %copy-done.39), channel_id=1, source_target_pairs={{0,4},{4,0},{8,12},{12,8},{16,20},{20,16},{24,28},{28,24},{1,5},{5... | collective-permute-start | bytes 786440 | tf_op jit(solution)/shard_map/ppermute | solution.py:90
  57.1 14.1 %collective-permute-start.12 = (bf16[512,256]{1,0:T(8,128)(2,1)S(1)}, bf16[512,256]{1,0:T(8,128)(2,1)S(1)}, u32[]{:S(2)}, u32[]{:S(2)}) collective-permute-start(bf16[512,256]{1,0:T(8,128)(2,1)S(1)} %collective-permute-done.8.refs_1_.refs_5_), channel_id=1, source_target_pairs={{0,16},{4,20},{8,24},{12,28},{16,0},{20,4},{24,8},{28,12},{1,17},{... | collective-permute-start | bytes 786440 | tf_op jit(solution)/shard_map/ppermute | solution.py:90
  58.7 38.0 %collective-permute-start.16 = (bf16[4,256,256]{2,1,0:T(8,128)(2,1)S(1)}, bf16[4,256,256]{2,1,0:T(8,128)(2,1)S(1)}, u32[]{:S(2)}, u32[]{:S(2)}) collective-permute-start(bf16[4,256,256]{2,1,0:T(8,128)(2,1)S(1)} %copy-done.53), channel_id=1, source_target_pairs={{0,8},{4,12},{8,0},{12,4},{16,24},{20,28},{24,16},{28,20},{1,9},{5... | collective-permute-start | bytes 1572872 | tf_op jit(solution)/shard_map/ppermute | solution.py:90
  58.7 15.9 %collective-permute-start.10 = (bf16[512,256]{1,0:T(8,128)(2,1)S(1)}, bf16[512,256]{1,0:T(8,128)(2,1)S(1)}, u32[]{:S(2)}, u32[]{:S(2)}) collective-permute-start(bf16[512,256]{1,0:T(8,128)(2,1)S(1)} %collective-permute-done.8.refs_1_.refs_5_), channel_id=1, source_target_pairs={{0,8},{4,12},{8,0},{12,4},{16,24},{20,28},{24,16},{28,20},{1,9},{5... | collective-permute-start | bytes 786440 | tf_op jit(solution)/shard_map/ppermute | solution.py:90
  59.2 14.9 %collective-permute-start.13 = (bf16[512,256]{1,0:T(8,128)(2,1)S(1)}, bf16[512,256]{1,0:T(8,128)(2,1)S(1)}, u32[]{:S(2)}, u32[]{:S(2)}) collective-permute-start(bf16[512,256]{1,0:T(8,128)(2,1)S(1)} %collective-permute-done.11.refs_4_.refs_8_), channel_id=1, source_target_pairs={{0,8},{4,12},{8,0},{12,4},{16,24},{20,28},{24,16},{28,20},{1,9},{5... | collective-permute-start | bytes 786440 | tf_op jit(solution)/shard_map/ppermute | solution.py:90
  59.3 26.0 %collective-permute-start.7 = (bf16[2,256,512]{2,1,0:T(8,128)(2,1)}, bf16[2,256,512]{2,1,0:T(8,128)(2,1)S(1)}, u32[]{:S(2)}, u32[]{:S(2)}) collective-permute-start(bf16[2,256,512]{2,1,0:T(8,128)(2,1)} %get-tuple-element.90.here_ref), channel_id=1, source_target_pairs={{0,4},{1,5},{2,6},{3,7},{8,12},{9,13},{10,14},{11,15},{16,20},{17,... | collective-permute-start | bytes 1572872 | tf_op jit(solution)/shard_map/ppermute | solution.py:651
  74.1 22.9 %collective-permute-start.15 = (bf16[4,256,256]{2,1,0:T(8,128)(2,1)}, bf16[4,256,256]{2,1,0:T(8,128)(2,1)S(1)}, u32[]{:S(2)}, u32[]{:S(2)}) collective-permute-start(bf16[4,256,256]{2,1,0:T(8,128)(2,1)} %get-tuple-element.94), channel_id=1, source_target_pairs={{0,8},{4,12},{8,0},{12,4},{16,24},{20,28},{24,16},{28,20},{1,9},{5... | collective-permute-start | bytes 1572872 | tf_op jit(solution)/shard_map/ppermute | solution.py:90
  92.5 14.1 %collective-permute-start.18 = (bf16[8,64,256]{2,1,0:T(8,128)(2,1)}, bf16[8,64,256]{2,1,0:T(8,128)(2,1)S(1)}, u32[]{:S(2)}, u32[]{:S(2)}) collective-permute-start(bf16[8,64,256]{2,1,0:T(8,128)(2,1)} %get-tuple-element.98), channel_id=1, source_target_pairs={{0,1},{1,0},{2,3},{3,2},{4,5},{5,4},{6,7},{7,6},{8,9},{9,8},{10,11... | collective-permute-start | bytes 786440 | tf_op jit(solution)/shard_map/ppermute | solution.py:138
  94.1 21.5 %collective-permute-start.19 = (bf16[8,64,256]{2,1,0:T(8,128)(2,1)}, bf16[8,64,256]{2,1,0:T(8,128)(2,1)S(1)}, u32[]{:S(2)}, u32[]{:S(2)}) collective-permute-start(bf16[8,64,256]{2,1,0:T(8,128)(2,1)} %get-tuple-element.99), channel_id=1, source_target_pairs={{0,2},{1,3},{2,0},{3,1},{4,6},{5,7},{6,4},{7,5},{8,10},{9,11},{10,... | collective-permute-start | bytes 786440 | tf_op jit(solution)/shard_map/ppermute | solution.py:138
  96.7 19.0 %collective-permute-start.20 = (bf16[8,64,256]{2,1,0:T(8,128)(2,1)}, bf16[8,64,256]{2,1,0:T(8,128)(2,1)S(1)}, u32[]{:S(2)}, u32[]{:S(2)}) collective-permute-start(bf16[8,64,256]{2,1,0:T(8,128)(2,1)} %get-tuple-element.100), channel_id=1, source_target_pairs={{0,3},{1,2},{2,1},{3,0},{4,7},{5,6},{6,5},{7,4},{8,11},{9,10},{10,... | collective-permute-start | bytes 786440 | tf_op jit(solution)/shard_map/ppermute | solution.py:138
  118.9 9.0 %collective-permute-start.23 = (bf16[8,64,256]{2,1,0:T(8,128)(2,1)}, bf16[8,64,256]{2,1,0:T(8,128)(2,1)S(1)}, u32[]{:S(2)}, u32[]{:S(2)}) collective-permute-start(bf16[8,64,256]{2,1,0:T(8,128)(2,1)} %get-tuple-element.102.refs_0_), channel_id=1, source_target_pairs={{0,3},{1,2},{2,1},{3,0},{4,7},{5,6},{6,5},{7,4},{8,11},{9,10},{10,... | collective-permute-start | bytes 786440 | tf_op jit(solution)/shard_map/ppermute | solution.py:138
  121.5 23.2 %collective-permute-start.22 = (bf16[8,64,256]{2,1,0:T(8,128)(2,1)}, bf16[8,64,256]{2,1,0:T(8,128)(2,1)S(1)}, u32[]{:S(2)}, u32[]{:S(2)}) collective-permute-start(bf16[8,64,256]{2,1,0:T(8,128)(2,1)} %get-tuple-element.102.refs_0_), channel_id=1, source_target_pairs={{0,2},{1,3},{2,0},{3,1},{4,6},{5,7},{6,4},{7,5},{8,10},{9,11},{10,... | collective-permute-start | bytes 786440 | tf_op jit(solution)/shard_map/ppermute | solution.py:138
  125.8 18.8 %collective-permute-start.21 = (bf16[8,64,256]{2,1,0:T(8,128)(2,1)}, bf16[8,64,256]{2,1,0:T(8,128)(2,1)S(1)}, u32[]{:S(2)}, u32[]{:S(2)}) collective-permute-start(bf16[8,64,256]{2,1,0:T(8,128)(2,1)} %get-tuple-element.102.refs_0_), channel_id=1, source_target_pairs={{0,1},{1,0},{2,3},{3,2},{4,5},{5,4},{6,7},{7,6},{8,9},{9,8},{10,11... | collective-permute-start | bytes 786440 | tf_op jit(solution)/shard_map/ppermute | solution.py:138
  166.7 5.6 %collective-permute-start.25 = (bf16[3,256,1408]{2,1,0:T(8,128)(2,1)}, bf16[3,256,1408]{2,1,0:T(8,128)(2,1)S(1)}, u32[]{:S(2)}, u32[]{:S(2)}) collective-permute-start(bf16[3,256,1408]{2,1,0:T(8,128)(2,1)} %get-tuple-element.116.refs_4_.three_ref), channel_id=1, source_target_pairs={{0,8},{4,12},{8,0},{12,4},{16,24},{20,28},{24,16},{28,20},{1,9},{5... | collective-permute-start | bytes 6488072 | tf_op jit(solution)/shard_map/ppermute | solution.py:90
  167.3 17.8 %collective-permute-start.26 = (bf16[8,64,256]{2,1,0:T(8,128)(2,1)}, bf16[8,64,256]{2,1,0:T(8,128)(2,1)S(1)}, u32[]{:S(2)}, u32[]{:S(2)}) collective-permute-start(bf16[8,64,256]{2,1,0:T(8,128)(2,1)} %get-tuple-element.112), channel_id=1, source_target_pairs={{0,1},{1,0},{2,3},{3,2},{4,5},{5,4},{6,7},{7,6},{8,9},{9,8},{10,11... | collective-permute-start | bytes 786440 | tf_op jit(solution)/shard_map/ppermute | solution.py:138
  168.8 21.5 %collective-permute-start.27 = (bf16[8,64,256]{2,1,0:T(8,128)(2,1)}, bf16[8,64,256]{2,1,0:T(8,128)(2,1)S(1)}, u32[]{:S(2)}, u32[]{:S(2)}) collective-permute-start(bf16[8,64,256]{2,1,0:T(8,128)(2,1)} %get-tuple-element.113), channel_id=1, source_target_pairs={{0,2},{1,3},{2,0},{3,1},{4,6},{5,7},{6,4},{7,5},{8,10},{9,11},{10,... | collective-permute-start | bytes 786440 | tf_op jit(solution)/shard_map/ppermute | solution.py:138
  171.2 19.1 %collective-permute-start.28 = (bf16[8,64,256]{2,1,0:T(8,128)(2,1)}, bf16[8,64,256]{2,1,0:T(8,128)(2,1)S(1)}, u32[]{:S(2)}, u32[]{:S(2)}) collective-permute-start(bf16[8,64,256]{2,1,0:T(8,128)(2,1)} %get-tuple-element.114), channel_id=1, source_target_pairs={{0,3},{1,2},{2,1},{3,0},{4,7},{5,6},{6,5},{7,4},{8,11},{9,10},{10,... | collective-permute-start | bytes 786440 | tf_op jit(solution)/shard_map/ppermute | solution.py:138
  194.2 13.8 %collective-permute-start.31 = (bf16[8,64,256]{2,1,0:T(8,128)(2,1)}, bf16[8,64,256]{2,1,0:T(8,128)(2,1)S(1)}, u32[]{:S(2)}, u32[]{:S(2)}) collective-permute-start(bf16[8,64,256]{2,1,0:T(8,128)(2,1)} %get-tuple-element.115.refs_0_), channel_id=1, source_target_pairs={{0,3},{1,2},{2,1},{3,0},{4,7},{5,6},{6,5},{7,4},{8,11},{9,10},{10,... | collective-permute-start | bytes 786440 | tf_op jit(solution)/shard_map/ppermute | solution.py:138
  196.5 22.8 %collective-permute-start.30 = (bf16[8,64,256]{2,1,0:T(8,128)(2,1)}, bf16[8,64,256]{2,1,0:T(8,128)(2,1)S(1)}, u32[]{:S(2)}, u32[]{:S(2)}) collective-permute-start(bf16[8,64,256]{2,1,0:T(8,128)(2,1)} %get-tuple-element.115.refs_0_), channel_id=1, source_target_pairs={{0,2},{1,3},{2,0},{3,1},{4,6},{5,7},{6,4},{7,5},{8,10},{9,11},{10,... | collective-permute-start | bytes 786440 | tf_op jit(solution)/shard_map/ppermute | solution.py:138
  200.7 18.7 %collective-permute-start.29 = (bf16[8,64,256]{2,1,0:T(8,128)(2,1)}, bf16[8,64,256]{2,1,0:T(8,128)(2,1)S(1)}, u32[]{:S(2)}, u32[]{:S(2)}) collective-permute-start(bf16[8,64,256]{2,1,0:T(8,128)(2,1)} %get-tuple-element.115.refs_0_), channel_id=1, source_target_pairs={{0,1},{1,0},{2,3},{3,2},{4,5},{5,4},{6,7},{7,6},{8,9},{9,8},{10,11... | collective-permute-start | bytes 786440 | tf_op jit(solution)/shard_map/ppermute | solution.py:138
  219.4 16.1 %collective-permute-start.32 = (bf16[8,64,256]{2,1,0:T(8,128)(2,1)}, bf16[8,64,256]{2,1,0:T(8,128)(2,1)}, u32[]{:S(2)}, u32[]{:S(2)}) collective-permute-start(bf16[8,64,256]{2,1,0:T(8,128)(2,1)} %get-tuple-element.121), channel_id=1, source_target_pairs={{0,1},{1,0},{2,3},{3,2},{4,5},{5,4},{6,7},{7,6},{8,9},{9,8},{10,11... | collective-permute-start | bytes 786440 | tf_op jit(solution)/shard_map/ppermute | solution.py:138
  219.5 21.7 %collective-permute-start.33 = (bf16[8,64,256]{2,1,0:T(8,128)(2,1)}, bf16[8,64,256]{2,1,0:T(8,128)(2,1)}, u32[]{:S(2)}, u32[]{:S(2)}) collective-permute-start(bf16[8,64,256]{2,1,0:T(8,128)(2,1)} %get-tuple-element.122), channel_id=1, source_target_pairs={{0,2},{1,3},{2,0},{3,1},{4,6},{5,7},{6,4},{7,5},{8,10},{9,11},{10,... | collective-permute-start | bytes 786440 | tf_op jit(solution)/shard_map/ppermute | solution.py:138
  222.4 18.8 %collective-permute-start.34 = (bf16[8,64,256]{2,1,0:T(8,128)(2,1)}, bf16[8,64,256]{2,1,0:T(8,128)(2,1)}, u32[]{:S(2)}, u32[]{:S(2)}) collective-permute-start(bf16[8,64,256]{2,1,0:T(8,128)(2,1)} %get-tuple-element.123), channel_id=1, source_target_pairs={{0,3},{1,2},{2,1},{3,0},{4,7},{5,6},{6,5},{7,4},{8,11},{9,10},{10,... | collective-permute-start | bytes 786440 | tf_op jit(solution)/shard_map/ppermute | solution.py:138
  233.9 35.2 %collective-permute-start.38 = (bf16[4,256,256]{2,1,0:T(8,128)(2,1)}, bf16[4,256,256]{2,1,0:T(8,128)(2,1)S(1)}, u32[]{:S(2)}, u32[]{:S(2)}) collective-permute-start(bf16[4,256,256]{2,1,0:T(8,128)(2,1)} %get-tuple-element.127), channel_id=1, source_target_pairs={{0,8},{4,12},{8,0},{12,4},{16,24},{20,28},{24,16},{28,20},{1,9},{5... | collective-permute-start | bytes 1572872 | tf_op jit(solution)/shard_map/ppermute | solution.py:90
  233.9 35.1 %collective-permute-start.39 = (bf16[2,256,512]{2,1,0:T(8,128)(2,1)}, bf16[2,256,512]{2,1,0:T(8,128)(2,1)S(1)}, u32[]{:S(2)}, u32[]{:S(2)}) collective-permute-start(bf16[2,256,512]{2,1,0:T(8,128)(2,1)} %get-tuple-element.129), channel_id=1, source_target_pairs={{4,0},{5,1},{6,2},{7,3},{12,8},{13,9},{14,10},{15,11},{20,16},{21,... | collective-permute-start | bytes 1572872 | tf_op jit(solution)/shard_map/ppermute | solution.py:732
  243.7 8.6 %collective-permute-start.37 = (bf16[8,64,256]{2,1,0:T(8,128)(2,1)}, bf16[8,64,256]{2,1,0:T(8,128)(2,1)S(1)}, u32[]{:S(2)}, u32[]{:S(2)}) collective-permute-start(bf16[8,64,256]{2,1,0:T(8,128)(2,1)} %block_out.1.refs_0_), channel_id=1, source_target_pairs={{0,3},{1,2},{2,1},{3,0},{4,7},{5,6},{6,5},{7,4},{8,11},{9,10},{10,... | collective-permute-start | bytes 786440 | tf_op jit(solution)/shard_map/ppermute | solution.py:138
  246.2 22.9 %collective-permute-start.36 = (bf16[8,64,256]{2,1,0:T(8,128)(2,1)}, bf16[8,64,256]{2,1,0:T(8,128)(2,1)S(1)}, u32[]{:S(2)}, u32[]{:S(2)}) collective-permute-start(bf16[8,64,256]{2,1,0:T(8,128)(2,1)} %block_out.1.refs_0_), channel_id=1, source_target_pairs={{0,2},{1,3},{2,0},{3,1},{4,6},{5,7},{6,4},{7,5},{8,10},{9,11},{10,... | collective-permute-start | bytes 786440 | tf_op jit(solution)/shard_map/ppermute | solution.py:138
  250.4 18.6 %collective-permute-start.35 = (bf16[8,64,256]{2,1,0:T(8,128)(2,1)}, bf16[8,64,256]{2,1,0:T(8,128)(2,1)S(1)}, u32[]{:S(2)}, u32[]{:S(2)}) collective-permute-start(bf16[8,64,256]{2,1,0:T(8,128)(2,1)} %block_out.1.refs_0_), channel_id=1, source_target_pairs={{0,1},{1,0},{2,3},{3,2},{4,5},{5,4},{6,7},{7,6},{8,9},{9,8},{10,11... | collective-permute-start | bytes 786440 | tf_op jit(solution)/shard_map/ppermute | solution.py:138
  275.4 10.2 %collective-permute-start.49 = (bf16[3,256,512]{2,1,0:T(8,128)(2,1)S(1)}, bf16[3,256,512]{2,1,0:T(8,128)(2,1)S(1)}, u32[]{:S(2)}, u32[]{:S(2)}) collective-permute-start(bf16[3,256,512]{2,1,0:T(8,128)(2,1)S(1)} %get-tuple-element.147.refs_2_), channel_id=1, source_target_pairs={{0,8},{4,12},{8,0},{12,4},{16,24},{20,28},{24,16},{28,20},{1,9},{5... | collective-permute-start | bytes 2359304 | tf_op jit(solution)/shard_map/ppermute | solution.py:90
  276.3 16.9 %collective-permute-start.42 = (bf16[8,64,256]{2,1,0:T(8,128)(2,1)}, bf16[8,64,256]{2,1,0:T(8,128)(2,1)S(1)}, u32[]{:S(2)}, u32[]{:S(2)}) collective-permute-start(bf16[8,64,256]{2,1,0:T(8,128)(2,1)} %get-tuple-element.135), channel_id=1, source_target_pairs={{0,1},{1,0},{2,3},{3,2},{4,5},{5,4},{6,7},{7,6},{8,9},{9,8},{10,11... | collective-permute-start | bytes 786440 | tf_op jit(solution)/shard_map/ppermute | solution.py:138
  276.3 21.6 %collective-permute-start.43 = (bf16[8,64,256]{2,1,0:T(8,128)(2,1)}, bf16[8,64,256]{2,1,0:T(8,128)(2,1)S(1)}, u32[]{:S(2)}, u32[]{:S(2)}) collective-permute-start(bf16[8,64,256]{2,1,0:T(8,128)(2,1)} %get-tuple-element.136), channel_id=1, source_target_pairs={{0,2},{1,3},{2,0},{3,1},{4,6},{5,7},{6,4},{7,5},{8,10},{9,11},{10,... | collective-permute-start | bytes 786440 | tf_op jit(solution)/shard_map/ppermute | solution.py:138
  279.3 18.6 %collective-permute-start.44 = (bf16[8,64,256]{2,1,0:T(8,128)(2,1)S(1)}, bf16[8,64,256]{2,1,0:T(8,128)(2,1)S(1)}, u32[]{:S(2)}, u32[]{:S(2)}) collective-permute-start(bf16[8,64,256]{2,1,0:T(8,128)(2,1)S(1)} %get-tuple-element.137), channel_id=1, source_target_pairs={{0,3},{1,2},{2,1},{3,0},{4,7},{5,6},{6,5},{7,4},{8,11},{9,10},{10,... | collective-permute-start | bytes 786440 | tf_op jit(solution)/shard_map/ppermute | solution.py:138
  288.2 33.9 %collective-permute-start.50 = (bf16[2,4,256,256]{3,2,1,0:T(8,128)(2,1)S(1)}, bf16[2,4,256,256]{3,2,1,0:T(8,128)(2,1)S(1)}, u32[]{:S(2)}, u32[]{:S(2)}) collective-permute-start(bf16[2,4,256,256]{3,2,1,0:T(8,128)(2,1)S(1)} %get-tuple-element.150), channel_id=1, source_target_pairs={{0,16},{4,20},{8,24},{12,28},{16,0},{20,4},{24,8},{28,12},{1,17},{... | collective-permute-start | bytes 3145736 | tf_op jit(solution)/shard_map/ppermute | solution.py:90
  291.8 32.6 %collective-permute-start.52 = (bf16[2,4,256,256]{3,2,1,0:T(8,128)(2,1)S(1)}, bf16[2,4,256,256]{3,2,1,0:T(8,128)(2,1)S(1)}, u32[]{:S(2)}, u32[]{:S(2)}) collective-permute-start(bf16[2,4,256,256]{3,2,1,0:T(8,128)(2,1)S(1)} %get-tuple-element.152), channel_id=1, source_target_pairs={{0,4},{4,0},{8,12},{12,8},{16,20},{20,16},{24,28},{28,24},{1,5},{5... | collective-permute-start | bytes 3145736 | tf_op jit(solution)/shard_map/ppermute | solution.py:90
  299.4 31.4 %collective-permute-start.47 = (bf16[544,256]{1,0:T(8,128)(2,1)S(1)}, bf16[544,256]{1,0:T(8,128)(2,1)}, u32[]{:S(2)}, u32[]{:S(2)}) collective-permute-start(bf16[544,256]{1,0:T(8,128)(2,1)S(1)} %input_grad.1.refs_0_), channel_id=1, source_target_pairs={{0,3},{1,2},{2,1},{3,0},{4,7},{5,6},{6,5},{7,4},{8,11},{9,10},{10,... | collective-permute-start | bytes 835592 | tf_op jit(solution)/shard_map/ppermute | solution.py:138
  301.9 28.9 %collective-permute-start.46 = (bf16[544,256]{1,0:T(8,128)(2,1)S(1)}, bf16[544,256]{1,0:T(8,128)(2,1)}, u32[]{:S(2)}, u32[]{:S(2)}) collective-permute-start(bf16[544,256]{1,0:T(8,128)(2,1)S(1)} %input_grad.1.refs_0_), channel_id=1, source_target_pairs={{0,2},{1,3},{2,0},{3,1},{4,6},{5,7},{6,4},{7,5},{8,10},{9,11},{10,... | collective-permute-start | bytes 835592 | tf_op jit(solution)/shard_map/ppermute | solution.py:138
  315.4 15.4 %collective-permute-start.45 = (bf16[544,256]{1,0:T(8,128)(2,1)S(1)}, bf16[544,256]{1,0:T(8,128)(2,1)}, u32[]{:S(2)}, u32[]{:S(2)}) collective-permute-start(bf16[544,256]{1,0:T(8,128)(2,1)S(1)} %input_grad.1.refs_0_), channel_id=1, source_target_pairs={{0,1},{1,0},{2,3},{3,2},{4,5},{5,4},{6,7},{7,6},{8,9},{9,8},{10,11... | collective-permute-start | bytes 835592 | tf_op jit(solution)/shard_map/ppermute | solution.py:138
  322.9 13.6 %collective-permute-start.51 = (bf16[1,4,256,256]{3,2,1,0:T(8,128)(2,1)}, bf16[1,4,256,256]{3,2,1,0:T(8,128)(2,1)}, u32[]{:S(2)}, u32[]{:S(2)}) collective-permute-start(bf16[1,4,256,256]{3,2,1,0:T(8,128)(2,1)} %add_convert_fusion.1), channel_id=1, source_target_pairs={{0,4},{4,0},{8,12},{12,8},{16,20},{20,16},{24,28},{28,24},{1,5},{5... | collective-permute-start | bytes 1572872 | tf_op jit(solution)/shard_map/ppermute | solution.py:90
  326.3 13.3 %collective-permute-start.53 = (bf16[1,4,256,256]{3,2,1,0:T(8,128)(2,1)}, bf16[1,4,256,256]{3,2,1,0:T(8,128)(2,1)}, u32[]{:S(2)}, u32[]{:S(2)}) collective-permute-start(bf16[1,4,256,256]{3,2,1,0:T(8,128)(2,1)} %add_convert_fusion), channel_id=1, source_target_pairs={{0,16},{4,20},{8,24},{12,28},{16,0},{20,4},{24,8},{28,12},{1,17},{... | collective-permute-start | bytes 1572872 | tf_op jit(solution)/shard_map/ppermute | solution.py:90
  333.1 6.5 %collective-permute-start.48 = (f32[38,256]{1,0:T(8,128)S(1)}, f32[38,256]{1,0:T(8,128)S(1)}, u32[]{:S(2)}, u32[]{:S(2)}) collective-permute-start(f32[38,256]{1,0:T(8,128)S(1)} %get-tuple-element.144.own_ref), channel_id=1, source_target_pairs={{0,8},{4,12},{8,0},{12,4},{16,24},{20,28},{24,16},{28,20},{1,9},{5... | collective-permute-start | bytes 116744 | tf_op jit(solution)/shard_map/ppermute | solution.py:90
  (71 other events, 861.3 us)
Sparse Core Ops, SparseCore 0:
  46.8 104.3 all-gather.2
  200.9 109.5 reduce-scatter.1

commit v5 on v4

--- a/solution.py
+++ b/solution.py
@@ -716,7 +716,7 @@
         block_out_kernel, "block_out", sends[0], (mid, down_own, *down_got),
         [VM] * (2 + len(down_got)),
     )
-    out_blocks = tensor_gather(out_chunk)
+    out_blocks = [out_chunk] + [tensor_swap(out_chunk, j) for j in range(1, peers - 1)]
 
     low_kept, low_sent, dq, dhere, dearly = call(
         functools.partial(attend_back_kernel, slots, peers), "attend_back",
@@ -737,7 +737,7 @@
             shape((3, tok, feat), bf16), small_shape, own_shape, *sends,
         ),
         (
-            order, at, block_in, tables, dq, tie(dhere, out_blocks, low_got), dback, *qkv_list,
+            order, at, block_in, tables, dq, tie(dhere, tuple(out_blocks), low_got), dback, *qkv_list,
             ffn_gain_grad, ffn_bias_grad,
         ),
         [SM, SM] + [VM] * (7 + count),
@@ -763,13 +763,14 @@
         ffn_out_kernel, "ffn_out", (shape((2, width, hid), f32), shape((hid, width), f32)),
         (ffn_total,), [VM],
     )
+    out_blocks.append(tensor_swap(tie(out_chunk, grad_blocks[1]), peers - 1))
     block_out = call(
         join_kernel, "block_out_rows", shape((tok, model), bf16), (at, *out_blocks),
         [SM] + [VM] * peers,
     )
     input_grad, small = call(
         join_grad_kernel, "input_grad_rows", (shape((tok, model), bf16), small_shape),
-        (at, small, *tie(grad_blocks, block_out, down_grad)), [SM] + [VM] * (1 + peers),
+        (at, small, *tie(grad_blocks, down_grad)), [SM] + [VM] * (1 + peers),
     )
 
     terms = (*terms_a, *terms_b)

time: 350 us -> 349 us (level)
  waiting for transfers between devices: 147 us -> 156 us
  starting transfers between devices: 76.7 us -> 68.8 us
    ppermute x28, waiting for transfers between devices: 47.1 us -> 58.3 us  [swap(): return lax.ppermute(value, ('fsdp', 'context'), pairs)]
    ppermute x24, starting transfers between devices: 54 us -> 45.8 us  [tensor_swap(): return lax.ppermute(value, 'tensor', [(i, i ^ j) for i in range(peers)])]
    unnamed x126 -> x122, local copies, waits for them, and re-layouts: 7.81 us -> 6.4 us
  transfers between devices with their start and end apart: 56 -> 56, of which waited for: 21 -> 24; matrix products, arithmetic and copies ran while one was open for 3% -> 3% of each run, Pallas kernels for 21% -> 20%
where the time goes in v5:
time: 349 us
  waiting for transfers between devices  156 us (45%)
  Pallas kernels  92.4 us (26%)
  starting transfers between devices  68.8 us (20%)
  between operations  14.7 us (4%)
  other arithmetic  9.35 us (3%)
  local copies, waits for them, and re-layouts  7.19 us (2%)
    pallas_call x18, Pallas kernels, call(): pl.pallas_call(kernel, out_shape=outs, in_specs=specs, out_specs=jax.tree...  81.2 us
    ppermute x24, waiting for transfers between devices, tensor_swap(): return lax.ppermute(value, 'tensor', [(i, i ^ j) for i in range(peers)])  80.5 us
    ppermute x28, waiting for transfers between devices, swap(): return lax.ppermute(value, ('fsdp', 'context'), pairs)  58.3 us
    ppermute x24, starting transfers between devices, tensor_swap(): return lax.ppermute(value, 'tensor', [(i, i ^ j) for i in range(peers)])  45.8 us
    ppermute x28, starting transfers between devices, swap(): return lax.ppermute(value, ('fsdp', 'context'), pairs)  18.8 us
    pallas_call x1, Pallas kernels, on_device(): pl.pallas_call(ffn_weights_kernel, grid_spec=pltpu.PrefetchScalarGridSpec...  11.2 us
    ppermute x1, waiting for transfers between devices, on_device(): lax.ppermute(here, 'context', [(i, i + 1) for i in range(plane.context -...  10.7 us
  transfers between devices with their start and end apart: 56, of which 24 were waited for; matrix products, arithmetic and copies ran while one was open for 3% of the time, Pallas kernels for 20%

profile of v5, /device:TPU:0, one launch (start us, length us, event | category | flops | bytes accessed | tf_op | source)
XLA Modules:
  0.0 348.8 jit_solution(5909790658072914765)
XLA Ops:
  7.2 4.0 %collective-permute-start.4 = (bf16[3,256,512]{2,1,0:T(8,128)(2,1)}, bf16[3,256,512]{2,1,0:T(8,128)(2,1)S(1)}, u32[]{:S(2)}, u32[]{:S(2)}) collective-permute-start(bf16[3,256,512]{2,1,0:T(8,128)(2,1)} %refs_0_.4), channel_id=1, source_target_pairs={{0,20},{4,16},{8,28},{12,24},{16,4},{20,0},{24,12},{28,8},{1,21},{... | collective-permute-start | bytes 2359304 | tf_op jit(solution)/shard_map/ppermute | solution.py:90
  18.6 3.2 ffn_shard.1
  22.8 3.4 norm_one.1
  26.2 3.6 %collective-permute-done.4.refs_5_ = bf16[3,256,512]{2,1,0:T(8,128)(2,1)S(1)} collective-permute-done((bf16[3,256,512]{2,1,0:T(8,128)(2,1)}, bf16[3,256,512]{2,1,0:T(8,128)(2,1)S(1)}, u32[]{:S(2)}, u32[]{:S(2)}) %collective-permute-start.4) | collective-permute-done | bytes 786464 | tf_op jit(solution)/shard_map/ppermute | solution.py:90
  29.8 16.3 %collective-permute-done.3.refs_4_ = bf16[3,256,512]{2,1,0:T(8,128)(2,1)S(1)} collective-permute-done((bf16[3,256,512]{2,1,0:T(8,128)(2,1)}, bf16[3,256,512]{2,1,0:T(8,128)(2,1)S(1)}, u32[]{:S(2)}, u32[]{:S(2)}) %collective-permute-start.3) | collective-permute-done | bytes 786464 | tf_op jit(solution)/shard_map/ppermute | solution.py:90
  50.8 5.9 %qkv.1 = (bf16[256,512]{1,0:T(8,128)(2,1)}, bf16[2,256,512]{2,1,0:T(8,128)(2,1)}) custom-call(bf16[256,2048]{1,0:T(8,128)(2,1)} %get-tuple-element.88.x_ref, f32[3,1,512]{2,1,0:T(1,128)} %reshape.289.bias_ref, f32[3,256,128]{2,1,0:T(8,128)} %pad_maximum_fusion.table_ref, bf16[3,256,512]{2,1,0:T(8,128)(2,1)} %refs_0_.4, bf16[3,256,512]{2,1,0:T(8,128)(2,1)} %copy-done.12, ...), custom_call_target="tpu_custom_call" | custom-call | flops 11500000256 | tf_op jit(solution)/shard_map/qkv/pallas_call | solution.py:47
  59.3 2.6 collective-permute-start.7
  61.9 9.3 %collective-permute-done.12.refs_5_.refs_9_ = bf16[512,256]{1,0:T(8,128)(2,1)S(1)} collective-permute-done((bf16[512,256]{1,0:T(8,128)(2,1)S(1)}, bf16[512,256]{1,0:T(8,128)(2,1)S(1)}, u32[]{:S(2)}, u32[]{:S(2)}) %collective-permute-start.12) | collective-permute-done | bytes 262176 | tf_op jit(solution)/shard_map/ppermute | solution.py:90
  71.1 2.9 cotangent_rows.1
  74.6 10.7 %collective-permute-done.7.early_ref = bf16[2,256,512]{2,1,0:T(8,128)(2,1)S(1)} collective-permute-done((bf16[2,256,512]{2,1,0:T(8,128)(2,1)}, bf16[2,256,512]{2,1,0:T(8,128)(2,1)S(1)}, u32[]{:S(2)}, u32[]{:S(2)}) %collective-permute-start.7) | collective-permute-done | bytes 524320 | tf_op jit(solution)/shard_map/ppermute | solution.py:651
  86.1 6.3 %attend.1 = (bf16[256,512]{1,0:T(8,128)(2,1)}, f32[8,256,1]{2,1,0:T(8,128)}, f32[8,64,256]{2,1,0:T(8,128)}, bf16[8,64,256]{2,1,0:T(8,128)(2,1)}, bf16[8,64,256]{...) custom-call(s32[8]{0:T(128)} %iota_xor_fusion.order_ref, s32[4]{0:T(128)} %iota_xor_fusion.1.at_ref, ...), custom_call_target="tpu_custom_call" | custom-call | tf_op jit(solution)/shard_map/attend/pallas_call | solution.py:47
  94.1 2.6 collective-permute-start.19
  97.7 8.9 %collective-permute-done.18.refs_0_ = bf16[8,64,256]{2,1,0:T(8,128)(2,1)S(1)} collective-permute-done((bf16[8,64,256]{2,1,0:T(8,128)(2,1)}, bf16[8,64,256]{2,1,0:T(8,128)(2,1)S(1)}, u32[]{:S(2)}, u32[]{:S(2)}) %collective-permute-start.18) | collective-permute-done | bytes 262176 | tf_op jit(solution)/shard_map/ppermute | solution.py:138
  106.5 9.1 %collective-permute-done.19.refs_1_ = bf16[8,64,256]{2,1,0:T(8,128)(2,1)S(1)} collective-permute-done((bf16[8,64,256]{2,1,0:T(8,128)(2,1)}, bf16[8,64,256]{2,1,0:T(8,128)(2,1)S(1)}, u32[]{:S(2)}, u32[]{:S(2)}) %collective-permute-start.19) | collective-permute-done | bytes 262176 | tf_op jit(solution)/shard_map/ppermute | solution.py:138
  116.4 2.4 mid.1
  118.9 2.5 collective-permute-start.23
  121.4 4.4 %collective-permute-start.22 = (bf16[8,64,256]{2,1,0:T(8,128)(2,1)}, bf16[8,64,256]{2,1,0:T(8,128)(2,1)S(1)}, u32[]{:S(2)}, u32[]{:S(2)}) collective-permute-start(bf16[8,64,256]{2,1,0:T(8,128)(2,1)} %get-tuple-element.103.refs_0_), channel_id=1, source_target_pairs={{0,2},{1,3},{2,0},{3,1},{4,6},{5,7},{6,4},{7,5},{8,10},{9,11},{10,... | collective-permute-start | bytes 786440 | tf_op jit(solution)/shard_map/ppermute | solution.py:138
  125.9 2.0 collective-permute-done.23.refs_3_
  127.9 16.7 %collective-permute-done.22.refs_2_ = bf16[8,64,256]{2,1,0:T(8,128)(2,1)S(1)} collective-permute-done((bf16[8,64,256]{2,1,0:T(8,128)(2,1)}, bf16[8,64,256]{2,1,0:T(8,128)(2,1)S(1)}, u32[]{:S(2)}, u32[]{:S(2)}) %collective-permute-start.22) | collective-permute-done | bytes 262176 | tf_op jit(solution)/shard_map/ppermute | solution.py:138
  144.6 6.6 %all-gather.3.cloned.1.call-done = bf16[6144,1408]{1,0:T(8,128)(2,1)} async-done(((bf16[768,1408]{1,0:T(8,128)(2,1)}), bf16[6144,1408]{1,0:T(8,128)(2,1)}) %all-gather.3.cloned.1.call-update) | async-done | bytes 17301520 | tf_op jit(solution)/shard_map/all_gather | solution.py:645
  151.2 15.4 %ffn.1 = (bf16[4,256,256]{2,1,0:T(8,128)(2,1)}, bf16[4,256,256]{2,1,0:T(8,128)(2,1)}, bf16[3,256,1408]{2,1,0:T(8,128)(2,1)}, f32[8,64,256]{2,1,0:T(8,128)}, bf16...) custom-call(s32[8]{0:T(128)} %iota_xor_fusion.order_ref, ...), custom_call_target="tpu_custom_call" | custom-call | tf_op jit(solution)/shard_map/ffn/pallas_call | solution.py:47
  168.7 2.4 collective-permute-start.27
  173.9 11.2 %ffn_weights.1 = bf16[3072,1408]{1,0:T(8,128)(2,1)} custom-call(s32[4]{0:T(128)} %pad_add_fusion.place_ref, bf16[4,256,256]{2,1,0:T(8,128)(2,1)} %get-tuple-element.109.refs_0_, bf16[4,256,256]{2,1,0:T(8,128)(2,1)} %copy-done.34, bf16[4,256,256]{2,1,0:T(8,128)(2,1)} %get-tuple-element.111.refs_2_, bf16[4,256,256]{2,1,0:T(8,128)(2,1)} %copy-done.33, ...), custom_call_target="tpu_custom_call" | custom-call | tf_op jit(solution)/shard_map/ffn_weights/pallas_call | solution.py:688
  185.0 5.2 %collective-permute-done.27.refs_1_ = bf16[8,64,256]{2,1,0:T(8,128)(2,1)S(1)} collective-permute-done((bf16[8,64,256]{2,1,0:T(8,128)(2,1)}, bf16[8,64,256]{2,1,0:T(8,128)(2,1)S(1)}, u32[]{:S(2)}, u32[]{:S(2)}) %collective-permute-start.27) | collective-permute-done | bytes 262176 | tf_op jit(solution)/shard_map/ppermute | solution.py:138
  191.1 3.1 mid_back.1
  194.1 2.4 collective-permute-start.31
  196.5 4.2 %collective-permute-start.30 = (bf16[8,64,256]{2,1,0:T(8,128)(2,1)}, bf16[8,64,256]{2,1,0:T(8,128)(2,1)S(1)}, u32[]{:S(2)}, u32[]{:S(2)}) collective-permute-start(bf16[8,64,256]{2,1,0:T(8,128)(2,1)} %get-tuple-element.116.refs_0_), channel_id=1, source_target_pairs={{0,2},{1,3},{2,0},{3,1},{4,6},{5,7},{6,4},{7,5},{8,10},{9,11},{10,... | collective-permute-start | bytes 786440 | tf_op jit(solution)/shard_map/ppermute | solution.py:138
  200.8 7.1 %down.1 = (f32[8,64,256]{2,1,0:T(8,128)}, bf16[8,64,256]{2,1,0:T(8,128)(2,1)}, bf16[8,64,256]{2,1,0:T(8,128)(2,1)}, bf16[8,64,256]{2,1,0:T(8,128)(2,1)}) custom-call(bf16[3,256,1408]{2,1,0:T(8,128)(2,1)} %get-tuple-element.117.refs_4_.three_ref, bf16[8,768,1408]{2,1,0:T(8,128)(2,1)} %bitcast.23), custom_call_target="tpu_custom_call" | custom-call | tf_op jit(solution)/shard_map/down/pallas_call | solution.py:47
  207.9 11.4 %collective-permute-done.30.refs_2_ = bf16[8,64,256]{2,1,0:T(8,128)(2,1)S(1)} collective-permute-done((bf16[8,64,256]{2,1,0:T(8,128)(2,1)}, bf16[8,64,256]{2,1,0:T(8,128)(2,1)S(1)}, u32[]{:S(2)}, u32[]{:S(2)}) %collective-permute-start.30) | collective-permute-done | bytes 262176 | tf_op jit(solution)/shard_map/ppermute | solution.py:138
  219.5 3.0 collective-permute-start.33
  223.8 10.0 %attend_back.1 = (bf16[4,256,256]{2,1,0:T(8,128)(2,1)}, bf16[4,256,256]{2,1,0:T(8,128)(2,1)}, bf16[256,512]{1,0:T(8,128)(2,1)}, f32[2,256,512]{2,1,0:T(8,128)}, bf16[2,256,512]{2,1,0:T(8,128)(2,1)}) custom-call(s32[8]{0:T(128)} %iota_xor_fusion.order_ref, s32[4]{0:T(128)} %iota_xor_fusion.1.at_ref, f32[256,512]{1,0:T(8,128)} %and_select_fusion.hide_ref, ...), custom_call_target="tpu_custom_call" | custom-call | flops 230000001024 | tf_op jit(solution)/shard_map/attend_back/pallas_call | solution.py:47
  235.5 5.7 %collective-permute-done.33.refs_1_ = bf16[8,64,256]{2,1,0:T(8,128)(2,1)} collective-permute-done((bf16[8,64,256]{2,1,0:T(8,128)(2,1)}, bf16[8,64,256]{2,1,0:T(8,128)(2,1)}, u32[]{:S(2)}, u32[]{:S(2)}) %collective-permute-start.33) | collective-permute-done | bytes 262176 | tf_op jit(solution)/shard_map/ppermute | solution.py:138
  241.3 2.4 block_out.1.refs_0_
  243.7 6.2 %collective-permute-start.36 = (bf16[8,64,256]{2,1,0:T(8,128)(2,1)}, bf16[8,64,256]{2,1,0:T(8,128)(2,1)S(1)}, u32[]{:S(2)}, u32[]{:S(2)}) collective-permute-start(bf16[8,64,256]{2,1,0:T(8,128)(2,1)} %block_out.1.refs_0_), channel_id=1, source_target_pairs={{0,2},{1,3},{2,0},{3,1},{4,6},{5,7},{6,4},{7,5},{8,10},{9,11},{10,... | collective-permute-start | bytes 786440 | tf_op jit(solution)/shard_map/ppermute | solution.py:138
  249.9 11.6 %collective-permute-done.36.refs_2_ = bf16[8,64,256]{2,1,0:T(8,128)(2,1)S(1)} collective-permute-done((bf16[8,64,256]{2,1,0:T(8,128)(2,1)}, bf16[8,64,256]{2,1,0:T(8,128)(2,1)S(1)}, u32[]{:S(2)}, u32[]{:S(2)}) %collective-permute-start.36) | collective-permute-done | bytes 262176 | tf_op jit(solution)/shard_map/ppermute | solution.py:138
  262.5 4.6 %one_grad.1 = (bf16[3,256,512]{2,1,0:T(8,128)(2,1)S(1)}, f32[38,256]{1,0:T(8,128)S(1)}, f32[8,64,256]{2,1,0:T(8,128)S(1)}, bf16[8,64,256]{2,1,0:T(8,128)(2,1)S(1...) custom-call(s32[8]{0:T(128)S(1)} %copy-done.25, s32[4]{0:T(128)S(1)} %copy-done.24, ...), custom_call_target="tpu_custom_call" | custom-call | tf_op jit(solution)/shard_map/one_grad/pallas_call | solution.py:47
  272.4 3.4 collective-permute-done.39
  277.4 3.4 collective-permute-done.40
  280.9 2.4 attention_weights.1
  286.2 3.9 %collective-permute-done.42.refs_1_ = bf16[8,64,256]{2,1,0:T(8,128)(2,1)S(1)} collective-permute-done((bf16[8,64,256]{2,1,0:T(8,128)(2,1)S(1)}, bf16[8,64,256]{2,1,0:T(8,128)(2,1)S(1)}, u32[]{:S(2)}, u32[]{:S(2)}) %collective-permute-start.42) | collective-permute-done | bytes 262176 | tf_op jit(solution)/shard_map/ppermute | solution.py:138
  290.7 5.5 %collective-permute-start.44 = (bf16[544,256]{1,0:T(8,128)(2,1)S(1)}, bf16[544,256]{1,0:T(8,128)(2,1)S(1)}, u32[]{:S(2)}, u32[]{:S(2)}) collective-permute-start(bf16[544,256]{1,0:T(8,128)(2,1)S(1)} %input_grad.1.refs_0_), channel_id=1, source_target_pairs={{0,1},{1,0},{2,3},{3,2},{4,5},{5,4},{6,7},{7,6},{8,9},{9,8},{10,11... | collective-permute-start | bytes 835592 | tf_op jit(solution)/shard_map/ppermute | solution.py:138
  297.7 5.8 %collective-permute-done.44.refs_1_ = bf16[544,256]{1,0:T(8,128)(2,1)S(1)} collective-permute-done((bf16[544,256]{1,0:T(8,128)(2,1)S(1)}, bf16[544,256]{1,0:T(8,128)(2,1)S(1)}, u32[]{:S(2)}, u32[]{:S(2)}) %collective-permute-start.44) | collective-permute-done | bytes 278560 | tf_op jit(solution)/shard_map/ppermute | solution.py:138
  304.7 17.3 %collective-permute-done.50.refs_1_ = bf16[2,4,256,256]{3,2,1,0:T(8,128)(2,1)S(1)} collective-permute-done((bf16[2,4,256,256]{3,2,1,0:T(8,128)(2,1)S(1)}, bf16[2,4,256,256]{3,2,1,0:T(8,128)(2,1)S(1)}, u32[]{:S(2)}, u32[]{:S(2)}) %collective-permute-start.50) | collective-permute-done | bytes 1048608 | tf_op jit(solution)/shard_map/ppermute | solution.py:90
  326.8 4.0 %ffn_out.1 = (f32[2,256,1408]{2,1,0:T(8,128)}, f32[1408,256]{1,0:T(8,128)}) custom-call(bf16[768,1408]{1,0:T(8,128)(2,1)} %reduce-scatter.2.cloned.1.call-done.total_ref), custom_call_target="tpu_custom_call" | custom-call | tf_op jit(solution)/shard_map/ffn_out/pallas_call | solution.py:47
  330.9 2.1 input_grad_rows.1
  333.0 2.3 block_out_rows.1
  336.2 2.8 collective-permute-done.53.refs_5_
  338.9 3.0 outputs.1
  (231 shorter events, 48.8 us)
Async XLA Ops:
  7.2 144.0 %all-gather.3.cloned.1.call-start = ((), (), s32[]{:S(2)}) async-start(), calls=%async_computation.2 | async-start | bytes 19464192 | tf_op jit(solution)/shard_map/all_gather | solution.py:645
  7.2 22.6 %collective-permute-start.4 = (bf16[3,256,512]{2,1,0:T(8,128)(2,1)}, bf16[3,256,512]{2,1,0:T(8,128)(2,1)S(1)}, u32[]{:S(2)}, u32[]{:S(2)}) collective-permute-start(bf16[3,256,512]{2,1,0:T(8,128)(2,1)} %refs_0_.4), channel_id=1, source_target_pairs={{0,20},{4,16},{8,28},{12,24},{16,4},{20,0},{24,12},{28,8},{1,21},{... | collective-permute-start | bytes 2359304 | tf_op jit(solution)/shard_map/ppermute | solution.py:90
  11.2 34.9 %collective-permute-start.3 = (bf16[3,256,512]{2,1,0:T(8,128)(2,1)}, bf16[3,256,512]{2,1,0:T(8,128)(2,1)S(1)}, u32[]{:S(2)}, u32[]{:S(2)}) collective-permute-start(bf16[3,256,512]{2,1,0:T(8,128)(2,1)} %refs_0_.4), channel_id=1, source_target_pairs={{0,16},{4,20},{8,24},{12,28},{16,0},{20,4},{24,8},{28,12},{1,17},{... | collective-permute-start | bytes 2359304 | tf_op jit(solution)/shard_map/ppermute | solution.py:90
  11.7 36.6 %collective-permute-start.1 = (bf16[3,256,512]{2,1,0:T(8,128)(2,1)}, bf16[3,256,512]{2,1,0:T(8,128)(2,1)S(1)}, u32[]{:S(2)}, u32[]{:S(2)}) collective-permute-start(bf16[3,256,512]{2,1,0:T(8,128)(2,1)} %refs_0_.4), channel_id=1, source_target_pairs={{0,8},{4,12},{8,0},{12,4},{16,24},{20,28},{24,16},{28,20},{1,9},{5... | collective-permute-start | bytes 2359304 | tf_op jit(solution)/shard_map/ppermute | solution.py:90
  11.7 34.4 %collective-permute-start = (bf16[3,256,512]{2,1,0:T(8,128)(2,1)}, bf16[3,256,512]{2,1,0:T(8,128)(2,1)S(1)}, u32[]{:S(2)}, u32[]{:S(2)}) collective-permute-start(bf16[3,256,512]{2,1,0:T(8,128)(2,1)} %refs_0_.4), channel_id=1, source_target_pairs={{0,4},{4,0},{8,12},{12,8},{16,20},{20,16},{24,28},{28,24},{1,5},{5... | collective-permute-start | bytes 2359304 | tf_op jit(solution)/shard_map/ppermute | solution.py:90
  46.7 280.1 %reduce-scatter.2.cloned.1.call-start = ((), (), s32[]{:S(2)}) async-start(), calls=%async_computation.1 | async-start | bytes 10813440 | tf_op jit(solution)/shard_map/reduce_scatter | solution.py:700
  46.8 12.4 %collective-permute-start.11 = (bf16[512,256]{1,0:T(8,128)(2,1)S(1)}, bf16[512,256]{1,0:T(8,128)(2,1)S(1)}, u32[]{:S(2)}, u32[]{:S(2)}) collective-permute-start(bf16[512,256]{1,0:T(8,128)(2,1)S(1)} %copy-done.38), channel_id=1, source_target_pairs={{0,16},{4,20},{8,24},{12,28},{16,0},{20,4},{24,8},{28,12},{1,17},{... | collective-permute-start | bytes 786440 | tf_op jit(solution)/shard_map/ppermute | solution.py:90
  48.3 10.9 %collective-permute-start.9 = (bf16[512,256]{1,0:T(8,128)(2,1)S(1)}, bf16[512,256]{1,0:T(8,128)(2,1)S(1)}, u32[]{:S(2)}, u32[]{:S(2)}) collective-permute-start(bf16[512,256]{1,0:T(8,128)(2,1)S(1)} %copy-done.38), channel_id=1, source_target_pairs={{0,8},{4,12},{8,0},{12,4},{16,24},{20,28},{24,16},{28,20},{1,9},{5... | collective-permute-start | bytes 786440 | tf_op jit(solution)/shard_map/ppermute | solution.py:90
  48.5 8.6 %collective-permute-start.8 = (bf16[512,256]{1,0:T(8,128)(2,1)S(1)}, bf16[512,256]{1,0:T(8,128)(2,1)S(1)}, u32[]{:S(2)}, u32[]{:S(2)}) collective-permute-start(bf16[512,256]{1,0:T(8,128)(2,1)S(1)} %copy-done.38), channel_id=1, source_target_pairs={{0,4},{4,0},{8,12},{12,8},{16,20},{20,16},{24,28},{28,24},{1,5},{5... | collective-permute-start | bytes 786440 | tf_op jit(solution)/shard_map/ppermute | solution.py:90
  57.1 14.1 %collective-permute-start.12 = (bf16[512,256]{1,0:T(8,128)(2,1)S(1)}, bf16[512,256]{1,0:T(8,128)(2,1)S(1)}, u32[]{:S(2)}, u32[]{:S(2)}) collective-permute-start(bf16[512,256]{1,0:T(8,128)(2,1)S(1)} %collective-permute-done.8.refs_1_.refs_5_), channel_id=1, source_target_pairs={{0,16},{4,20},{8,24},{12,28},{16,0},{20,4},{24,8},{28,12},{1,17},{... | collective-permute-start | bytes 786440 | tf_op jit(solution)/shard_map/ppermute | solution.py:90
  58.7 38.0 %collective-permute-start.16 = (bf16[4,256,256]{2,1,0:T(8,128)(2,1)S(1)}, bf16[4,256,256]{2,1,0:T(8,128)(2,1)S(1)}, u32[]{:S(2)}, u32[]{:S(2)}) collective-permute-start(bf16[4,256,256]{2,1,0:T(8,128)(2,1)S(1)} %copy-done.51), channel_id=1, source_target_pairs={{0,8},{4,12},{8,0},{12,4},{16,24},{20,28},{24,16},{28,20},{1,9},{5... | collective-permute-start | bytes 1572872 | tf_op jit(solution)/shard_map/ppermute | solution.py:90
  58.7 15.9 %collective-permute-start.10 = (bf16[512,256]{1,0:T(8,128)(2,1)S(1)}, bf16[512,256]{1,0:T(8,128)(2,1)S(1)}, u32[]{:S(2)}, u32[]{:S(2)}) collective-permute-start(bf16[512,256]{1,0:T(8,128)(2,1)S(1)} %collective-permute-done.8.refs_1_.refs_5_), channel_id=1, source_target_pairs={{0,8},{4,12},{8,0},{12,4},{16,24},{20,28},{24,16},{28,20},{1,9},{5... | collective-permute-start | bytes 786440 | tf_op jit(solution)/shard_map/ppermute | solution.py:90
  59.2 14.9 %collective-permute-start.13 = (bf16[512,256]{1,0:T(8,128)(2,1)S(1)}, bf16[512,256]{1,0:T(8,128)(2,1)S(1)}, u32[]{:S(2)}, u32[]{:S(2)}) collective-permute-start(bf16[512,256]{1,0:T(8,128)(2,1)S(1)} %collective-permute-done.11.refs_4_.refs_8_), channel_id=1, source_target_pairs={{0,8},{4,12},{8,0},{12,4},{16,24},{20,28},{24,16},{28,20},{1,9},{5... | collective-permute-start | bytes 786440 | tf_op jit(solution)/shard_map/ppermute | solution.py:90
  59.3 26.0 %collective-permute-start.7 = (bf16[2,256,512]{2,1,0:T(8,128)(2,1)}, bf16[2,256,512]{2,1,0:T(8,128)(2,1)S(1)}, u32[]{:S(2)}, u32[]{:S(2)}) collective-permute-start(bf16[2,256,512]{2,1,0:T(8,128)(2,1)} %get-tuple-element.91.here_ref), channel_id=1, source_target_pairs={{0,4},{1,5},{2,6},{3,7},{8,12},{9,13},{10,14},{11,15},{16,20},{17,... | collective-permute-start | bytes 1572872 | tf_op jit(solution)/shard_map/ppermute | solution.py:651
  74.1 22.8 %collective-permute-start.15 = (bf16[4,256,256]{2,1,0:T(8,128)(2,1)}, bf16[4,256,256]{2,1,0:T(8,128)(2,1)S(1)}, u32[]{:S(2)}, u32[]{:S(2)}) collective-permute-start(bf16[4,256,256]{2,1,0:T(8,128)(2,1)} %get-tuple-element.95), channel_id=1, source_target_pairs={{0,8},{4,12},{8,0},{12,4},{16,24},{20,28},{24,16},{28,20},{1,9},{5... | collective-permute-start | bytes 1572872 | tf_op jit(solution)/shard_map/ppermute | solution.py:90
  92.5 14.1 %collective-permute-start.18 = (bf16[8,64,256]{2,1,0:T(8,128)(2,1)}, bf16[8,64,256]{2,1,0:T(8,128)(2,1)S(1)}, u32[]{:S(2)}, u32[]{:S(2)}) collective-permute-start(bf16[8,64,256]{2,1,0:T(8,128)(2,1)} %get-tuple-element.99), channel_id=1, source_target_pairs={{0,1},{1,0},{2,3},{3,2},{4,5},{5,4},{6,7},{7,6},{8,9},{9,8},{10,11... | collective-permute-start | bytes 786440 | tf_op jit(solution)/shard_map/ppermute | solution.py:138
  94.1 21.5 %collective-permute-start.19 = (bf16[8,64,256]{2,1,0:T(8,128)(2,1)}, bf16[8,64,256]{2,1,0:T(8,128)(2,1)S(1)}, u32[]{:S(2)}, u32[]{:S(2)}) collective-permute-start(bf16[8,64,256]{2,1,0:T(8,128)(2,1)} %get-tuple-element.100), channel_id=1, source_target_pairs={{0,2},{1,3},{2,0},{3,1},{4,6},{5,7},{6,4},{7,5},{8,10},{9,11},{10,... | collective-permute-start | bytes 786440 | tf_op jit(solution)/shard_map/ppermute | solution.py:138
  96.7 18.9 %collective-permute-start.20 = (bf16[8,64,256]{2,1,0:T(8,128)(2,1)}, bf16[8,64,256]{2,1,0:T(8,128)(2,1)S(1)}, u32[]{:S(2)}, u32[]{:S(2)}) collective-permute-start(bf16[8,64,256]{2,1,0:T(8,128)(2,1)} %get-tuple-element.101), channel_id=1, source_target_pairs={{0,3},{1,2},{2,1},{3,0},{4,7},{5,6},{6,5},{7,4},{8,11},{9,10},{10,... | collective-permute-start | bytes 786440 | tf_op jit(solution)/shard_map/ppermute | solution.py:138
  118.9 9.0 %collective-permute-start.23 = (bf16[8,64,256]{2,1,0:T(8,128)(2,1)}, bf16[8,64,256]{2,1,0:T(8,128)(2,1)S(1)}, u32[]{:S(2)}, u32[]{:S(2)}) collective-permute-start(bf16[8,64,256]{2,1,0:T(8,128)(2,1)} %get-tuple-element.103.refs_0_), channel_id=1, source_target_pairs={{0,3},{1,2},{2,1},{3,0},{4,7},{5,6},{6,5},{7,4},{8,11},{9,10},{10,... | collective-permute-start | bytes 786440 | tf_op jit(solution)/shard_map/ppermute | solution.py:138
  121.4 23.2 %collective-permute-start.22 = (bf16[8,64,256]{2,1,0:T(8,128)(2,1)}, bf16[8,64,256]{2,1,0:T(8,128)(2,1)S(1)}, u32[]{:S(2)}, u32[]{:S(2)}) collective-permute-start(bf16[8,64,256]{2,1,0:T(8,128)(2,1)} %get-tuple-element.103.refs_0_), channel_id=1, source_target_pairs={{0,2},{1,3},{2,0},{3,1},{4,6},{5,7},{6,4},{7,5},{8,10},{9,11},{10,... | collective-permute-start | bytes 786440 | tf_op jit(solution)/shard_map/ppermute | solution.py:138
  125.8 18.8 %collective-permute-start.21 = (bf16[8,64,256]{2,1,0:T(8,128)(2,1)}, bf16[8,64,256]{2,1,0:T(8,128)(2,1)S(1)}, u32[]{:S(2)}, u32[]{:S(2)}) collective-permute-start(bf16[8,64,256]{2,1,0:T(8,128)(2,1)} %get-tuple-element.103.refs_0_), channel_id=1, source_target_pairs={{0,1},{1,0},{2,3},{3,2},{4,5},{5,4},{6,7},{7,6},{8,9},{9,8},{10,11... | collective-permute-start | bytes 786440 | tf_op jit(solution)/shard_map/ppermute | solution.py:138
  166.7 5.6 %collective-permute-start.25 = (bf16[3,256,1408]{2,1,0:T(8,128)(2,1)}, bf16[3,256,1408]{2,1,0:T(8,128)(2,1)S(1)}, u32[]{:S(2)}, u32[]{:S(2)}) collective-permute-start(bf16[3,256,1408]{2,1,0:T(8,128)(2,1)} %get-tuple-element.117.refs_4_.three_ref), channel_id=1, source_target_pairs={{0,8},{4,12},{8,0},{12,4},{16,24},{20,28},{24,16},{28,20},{1,9},{5... | collective-permute-start | bytes 6488072 | tf_op jit(solution)/shard_map/ppermute | solution.py:90
  167.2 17.8 %collective-permute-start.26 = (bf16[8,64,256]{2,1,0:T(8,128)(2,1)}, bf16[8,64,256]{2,1,0:T(8,128)(2,1)S(1)}, u32[]{:S(2)}, u32[]{:S(2)}) collective-permute-start(bf16[8,64,256]{2,1,0:T(8,128)(2,1)} %get-tuple-element.113), channel_id=1, source_target_pairs={{0,1},{1,0},{2,3},{3,2},{4,5},{5,4},{6,7},{7,6},{8,9},{9,8},{10,11... | collective-permute-start | bytes 786440 | tf_op jit(solution)/shard_map/ppermute | solution.py:138
  168.7 21.5 %collective-permute-start.27 = (bf16[8,64,256]{2,1,0:T(8,128)(2,1)}, bf16[8,64,256]{2,1,0:T(8,128)(2,1)S(1)}, u32[]{:S(2)}, u32[]{:S(2)}) collective-permute-start(bf16[8,64,256]{2,1,0:T(8,128)(2,1)} %get-tuple-element.114), channel_id=1, source_target_pairs={{0,2},{1,3},{2,0},{3,1},{4,6},{5,7},{6,4},{7,5},{8,10},{9,11},{10,... | collective-permute-start | bytes 786440 | tf_op jit(solution)/shard_map/ppermute | solution.py:138
  171.1 19.1 %collective-permute-start.28 = (bf16[8,64,256]{2,1,0:T(8,128)(2,1)}, bf16[8,64,256]{2,1,0:T(8,128)(2,1)S(1)}, u32[]{:S(2)}, u32[]{:S(2)}) collective-permute-start(bf16[8,64,256]{2,1,0:T(8,128)(2,1)} %get-tuple-element.115), channel_id=1, source_target_pairs={{0,3},{1,2},{2,1},{3,0},{4,7},{5,6},{6,5},{7,4},{8,11},{9,10},{10,... | collective-permute-start | bytes 786440 | tf_op jit(solution)/shard_map/ppermute | solution.py:138
  194.1 13.8 %collective-permute-start.31 = (bf16[8,64,256]{2,1,0:T(8,128)(2,1)}, bf16[8,64,256]{2,1,0:T(8,128)(2,1)S(1)}, u32[]{:S(2)}, u32[]{:S(2)}) collective-permute-start(bf16[8,64,256]{2,1,0:T(8,128)(2,1)} %get-tuple-element.116.refs_0_), channel_id=1, source_target_pairs={{0,3},{1,2},{2,1},{3,0},{4,7},{5,6},{6,5},{7,4},{8,11},{9,10},{10,... | collective-permute-start | bytes 786440 | tf_op jit(solution)/shard_map/ppermute | solution.py:138
  196.5 22.8 %collective-permute-start.30 = (bf16[8,64,256]{2,1,0:T(8,128)(2,1)}, bf16[8,64,256]{2,1,0:T(8,128)(2,1)S(1)}, u32[]{:S(2)}, u32[]{:S(2)}) collective-permute-start(bf16[8,64,256]{2,1,0:T(8,128)(2,1)} %get-tuple-element.116.refs_0_), channel_id=1, source_target_pairs={{0,2},{1,3},{2,0},{3,1},{4,6},{5,7},{6,4},{7,5},{8,10},{9,11},{10,... | collective-permute-start | bytes 786440 | tf_op jit(solution)/shard_map/ppermute | solution.py:138
  200.7 18.7 %collective-permute-start.29 = (bf16[8,64,256]{2,1,0:T(8,128)(2,1)}, bf16[8,64,256]{2,1,0:T(8,128)(2,1)S(1)}, u32[]{:S(2)}, u32[]{:S(2)}) collective-permute-start(bf16[8,64,256]{2,1,0:T(8,128)(2,1)} %get-tuple-element.116.refs_0_), channel_id=1, source_target_pairs={{0,1},{1,0},{2,3},{3,2},{4,5},{5,4},{6,7},{7,6},{8,9},{9,8},{10,11... | collective-permute-start | bytes 786440 | tf_op jit(solution)/shard_map/ppermute | solution.py:138
  219.4 16.1 %collective-permute-start.32 = (bf16[8,64,256]{2,1,0:T(8,128)(2,1)}, bf16[8,64,256]{2,1,0:T(8,128)(2,1)}, u32[]{:S(2)}, u32[]{:S(2)}) collective-permute-start(bf16[8,64,256]{2,1,0:T(8,128)(2,1)} %get-tuple-element.122), channel_id=1, source_target_pairs={{0,1},{1,0},{2,3},{3,2},{4,5},{5,4},{6,7},{7,6},{8,9},{9,8},{10,11... | collective-permute-start | bytes 786440 | tf_op jit(solution)/shard_map/ppermute | solution.py:138
  219.5 21.7 %collective-permute-start.33 = (bf16[8,64,256]{2,1,0:T(8,128)(2,1)}, bf16[8,64,256]{2,1,0:T(8,128)(2,1)}, u32[]{:S(2)}, u32[]{:S(2)}) collective-permute-start(bf16[8,64,256]{2,1,0:T(8,128)(2,1)} %get-tuple-element.123), channel_id=1, source_target_pairs={{0,2},{1,3},{2,0},{3,1},{4,6},{5,7},{6,4},{7,5},{8,10},{9,11},{10,... | collective-permute-start | bytes 786440 | tf_op jit(solution)/shard_map/ppermute | solution.py:138
  222.4 18.8 %collective-permute-start.34 = (bf16[8,64,256]{2,1,0:T(8,128)(2,1)}, bf16[8,64,256]{2,1,0:T(8,128)(2,1)}, u32[]{:S(2)}, u32[]{:S(2)}) collective-permute-start(bf16[8,64,256]{2,1,0:T(8,128)(2,1)} %get-tuple-element.124), channel_id=1, source_target_pairs={{0,3},{1,2},{2,1},{3,0},{4,7},{5,6},{6,5},{7,4},{8,11},{9,10},{10,... | collective-permute-start | bytes 786440 | tf_op jit(solution)/shard_map/ppermute | solution.py:138
  233.8 27.8 %collective-permute-start.37 = (bf16[4,256,256]{2,1,0:T(8,128)(2,1)}, bf16[4,256,256]{2,1,0:T(8,128)(2,1)S(1)}, u32[]{:S(2)}, u32[]{:S(2)}) collective-permute-start(bf16[4,256,256]{2,1,0:T(8,128)(2,1)} %get-tuple-element.129), channel_id=1, source_target_pairs={{0,8},{4,12},{8,0},{12,4},{16,24},{20,28},{24,16},{28,20},{1,9},{5... | collective-permute-start | bytes 1572872 | tf_op jit(solution)/shard_map/ppermute | solution.py:90
  233.9 27.9 %collective-permute-start.38 = (bf16[2,256,512]{2,1,0:T(8,128)(2,1)}, bf16[2,256,512]{2,1,0:T(8,128)(2,1)S(1)}, u32[]{:S(2)}, u32[]{:S(2)}) collective-permute-start(bf16[2,256,512]{2,1,0:T(8,128)(2,1)} %get-tuple-element.131), channel_id=1, source_target_pairs={{4,0},{5,1},{6,2},{7,3},{12,8},{13,9},{14,10},{15,11},{20,16},{21,... | collective-permute-start | bytes 1572872 | tf_op jit(solution)/shard_map/ppermute | solution.py:732
  243.7 17.8 %collective-permute-start.36 = (bf16[8,64,256]{2,1,0:T(8,128)(2,1)}, bf16[8,64,256]{2,1,0:T(8,128)(2,1)S(1)}, u32[]{:S(2)}, u32[]{:S(2)}) collective-permute-start(bf16[8,64,256]{2,1,0:T(8,128)(2,1)} %block_out.1.refs_0_), channel_id=1, source_target_pairs={{0,2},{1,3},{2,0},{3,1},{4,6},{5,7},{6,4},{7,5},{8,10},{9,11},{10,... | collective-permute-start | bytes 786440 | tf_op jit(solution)/shard_map/ppermute | solution.py:138
  249.9 11.7 %collective-permute-start.35 = (bf16[8,64,256]{2,1,0:T(8,128)(2,1)}, bf16[8,64,256]{2,1,0:T(8,128)(2,1)S(1)}, u32[]{:S(2)}, u32[]{:S(2)}) collective-permute-start(bf16[8,64,256]{2,1,0:T(8,128)(2,1)} %block_out.1.refs_0_), channel_id=1, source_target_pairs={{0,1},{1,0},{2,3},{3,2},{4,5},{5,4},{6,7},{7,6},{8,9},{9,8},{10,11... | collective-permute-start | bytes 786440 | tf_op jit(solution)/shard_map/ppermute | solution.py:138
  267.1 13.7 %collective-permute-start.49 = (bf16[3,256,512]{2,1,0:T(8,128)(2,1)S(1)}, bf16[3,256,512]{2,1,0:T(8,128)(2,1)S(1)}, u32[]{:S(2)}, u32[]{:S(2)}) collective-permute-start(bf16[3,256,512]{2,1,0:T(8,128)(2,1)S(1)} %get-tuple-element.149.refs_2_), channel_id=1, source_target_pairs={{0,8},{4,12},{8,0},{12,4},{16,24},{20,28},{24,16},{28,20},{1,9},{5... | collective-permute-start | bytes 2359304 | tf_op jit(solution)/shard_map/ppermute | solution.py:90
  267.2 19.0 %collective-permute-start.41 = (bf16[8,64,256]{2,1,0:T(8,128)(2,1)S(1)}, bf16[8,64,256]{2,1,0:T(8,128)(2,1)S(1)}, u32[]{:S(2)}, u32[]{:S(2)}) collective-permute-start(bf16[8,64,256]{2,1,0:T(8,128)(2,1)S(1)} %get-tuple-element.136), channel_id=1, source_target_pairs={{0,1},{1,0},{2,3},{3,2},{4,5},{5,4},{6,7},{7,6},{8,9},{9,8},{10,11... | collective-permute-start | bytes 786440 | tf_op jit(solution)/shard_map/ppermute | solution.py:138
  268.8 21.3 %collective-permute-start.42 = (bf16[8,64,256]{2,1,0:T(8,128)(2,1)S(1)}, bf16[8,64,256]{2,1,0:T(8,128)(2,1)S(1)}, u32[]{:S(2)}, u32[]{:S(2)}) collective-permute-start(bf16[8,64,256]{2,1,0:T(8,128)(2,1)S(1)} %get-tuple-element.137), channel_id=1, source_target_pairs={{0,2},{1,3},{2,0},{3,1},{4,6},{5,7},{6,4},{7,5},{8,10},{9,11},{10,... | collective-permute-start | bytes 786440 | tf_op jit(solution)/shard_map/ppermute | solution.py:138
  269.8 20.3 %collective-permute-start.43 = (bf16[8,64,256]{2,1,0:T(8,128)(2,1)S(1)}, bf16[8,64,256]{2,1,0:T(8,128)(2,1)S(1)}, u32[]{:S(2)}, u32[]{:S(2)}) collective-permute-start(bf16[8,64,256]{2,1,0:T(8,128)(2,1)S(1)} %get-tuple-element.138), channel_id=1, source_target_pairs={{0,3},{1,2},{2,1},{3,0},{4,7},{5,6},{6,5},{7,4},{8,11},{9,10},{10,... | collective-permute-start | bytes 786440 | tf_op jit(solution)/shard_map/ppermute | solution.py:138
  283.3 38.7 %collective-permute-start.50 = (bf16[2,4,256,256]{3,2,1,0:T(8,128)(2,1)S(1)}, bf16[2,4,256,256]{3,2,1,0:T(8,128)(2,1)S(1)}, u32[]{:S(2)}, u32[]{:S(2)}) collective-permute-start(bf16[2,4,256,256]{3,2,1,0:T(8,128)(2,1)S(1)} %get-tuple-element.152), channel_id=1, source_target_pairs={{0,16},{4,20},{8,24},{12,28},{16,0},{20,4},{24,8},{28,12},{1,17},{... | collective-permute-start | bytes 3145736 | tf_op jit(solution)/shard_map/ppermute | solution.py:90
  284.8 39.6 %collective-permute-start.52 = (bf16[2,4,256,256]{3,2,1,0:T(8,128)(2,1)S(1)}, bf16[2,4,256,256]{3,2,1,0:T(8,128)(2,1)S(1)}, u32[]{:S(2)}, u32[]{:S(2)}) collective-permute-start(bf16[2,4,256,256]{3,2,1,0:T(8,128)(2,1)S(1)} %get-tuple-element.154), channel_id=1, source_target_pairs={{0,4},{4,0},{8,12},{12,8},{16,20},{20,16},{24,28},{28,24},{1,5},{5... | collective-permute-start | bytes 3145736 | tf_op jit(solution)/shard_map/ppermute | solution.py:90
  290.7 12.8 %collective-permute-start.44 = (bf16[544,256]{1,0:T(8,128)(2,1)S(1)}, bf16[544,256]{1,0:T(8,128)(2,1)S(1)}, u32[]{:S(2)}, u32[]{:S(2)}) collective-permute-start(bf16[544,256]{1,0:T(8,128)(2,1)S(1)} %input_grad.1.refs_0_), channel_id=1, source_target_pairs={{0,1},{1,0},{2,3},{3,2},{4,5},{5,4},{6,7},{7,6},{8,9},{9,8},{10,11... | collective-permute-start | bytes 835592 | tf_op jit(solution)/shard_map/ppermute | solution.py:138
  296.1 34.7 %collective-permute-start.47 = (bf16[544,256]{1,0:T(8,128)(2,1)S(1)}, bf16[544,256]{1,0:T(8,128)(2,1)}, u32[]{:S(2)}, u32[]{:S(2)}) collective-permute-start(bf16[544,256]{1,0:T(8,128)(2,1)S(1)} %input_grad.1.refs_0_), channel_id=1, source_target_pairs={{0,3},{1,2},{2,1},{3,0},{4,7},{5,6},{6,5},{7,4},{8,11},{9,10},{10,... | collective-permute-start | bytes 835592 | tf_op jit(solution)/shard_map/ppermute | solution.py:138
  297.6 33.2 %collective-permute-start.46 = (bf16[544,256]{1,0:T(8,128)(2,1)S(1)}, bf16[544,256]{1,0:T(8,128)(2,1)}, u32[]{:S(2)}, u32[]{:S(2)}) collective-permute-start(bf16[544,256]{1,0:T(8,128)(2,1)S(1)} %input_grad.1.refs_0_), channel_id=1, source_target_pairs={{0,2},{1,3},{2,0},{3,1},{4,6},{5,7},{6,4},{7,5},{8,10},{9,11},{10,... | collective-permute-start | bytes 835592 | tf_op jit(solution)/shard_map/ppermute | solution.py:138
  303.5 29.5 %collective-permute-start.45 = (bf16[8,64,256]{2,1,0:T(8,128)(2,1)}, bf16[8,64,256]{2,1,0:T(8,128)(2,1)}, u32[]{:S(2)}, u32[]{:S(2)}) collective-permute-start(bf16[8,64,256]{2,1,0:T(8,128)(2,1)} %block_out.1.refs_0_), channel_id=1, source_target_pairs={{0,3},{1,2},{2,1},{3,0},{4,7},{5,6},{6,5},{7,4},{8,11},{9,10},{10,... | collective-permute-start | bytes 786440 | tf_op jit(solution)/shard_map/ppermute | solution.py:138
  322.9 13.3 %collective-permute-start.51 = (bf16[1,4,256,256]{3,2,1,0:T(8,128)(2,1)}, bf16[1,4,256,256]{3,2,1,0:T(8,128)(2,1)}, u32[]{:S(2)}, u32[]{:S(2)}) collective-permute-start(bf16[1,4,256,256]{3,2,1,0:T(8,128)(2,1)} %add_convert_fusion.1), channel_id=1, source_target_pairs={{0,4},{4,0},{8,12},{12,8},{16,20},{20,16},{24,28},{28,24},{1,5},{5... | collective-permute-start | bytes 1572872 | tf_op jit(solution)/shard_map/ppermute | solution.py:90
  326.3 12.7 %collective-permute-start.53 = (bf16[1,4,256,256]{3,2,1,0:T(8,128)(2,1)}, bf16[1,4,256,256]{3,2,1,0:T(8,128)(2,1)}, u32[]{:S(2)}, u32[]{:S(2)}) collective-permute-start(bf16[1,4,256,256]{3,2,1,0:T(8,128)(2,1)} %add_convert_fusion), channel_id=1, source_target_pairs={{0,16},{4,20},{8,24},{12,28},{16,0},{20,4},{24,8},{28,12},{1,17},{... | collective-permute-start | bytes 1572872 | tf_op jit(solution)/shard_map/ppermute | solution.py:90
  333.0 6.0 %collective-permute-start.48 = (f32[38,256]{1,0:T(8,128)S(1)}, f32[38,256]{1,0:T(8,128)S(1)}, u32[]{:S(2)}, u32[]{:S(2)}) collective-permute-start(f32[38,256]{1,0:T(8,128)S(1)} %get-tuple-element.146.own_ref), channel_id=1, source_target_pairs={{0,8},{4,12},{8,0},{12,4},{16,24},{20,28},{24,16},{28,20},{1,9},{5... | collective-permute-start | bytes 116744 | tf_op jit(solution)/shard_map/ppermute | solution.py:90
  (69 other events, 766.7 us)
Sparse Core Ops, SparseCore 0:
  46.8 104.3 all-gather.2
  200.9 115.0 reduce-scatter.1
